TPU v7x, 256 devices: a whole 4x4x8 slice. The times are simulated.
256 devices in a mesh: batch: 256 (over y, z, x, core).
Axes of the slice: x: 4, y: 4, z: 8, core: 2. Of those that a mesh axis runs over, the one named last changes fastest.
Arguments:
- image: bfloat16 [32768, 1024], P('batch'), may hold values from -6 to 6
- text: bfloat16 [32768, 1024], P('batch'), may hold values from -6 to 6
- image_bank: bfloat16 [2048, 1024], P('batch'), may hold values from -6 to 6
- text_bank: bfloat16 [2048, 1024], P('batch'), may hold values from -6 to 6
Outputs:
- losses: float32 [6], replicated
- grad_image: float32 [32768, 1024], P('batch')
- grad_text: float32 [32768, 1024], P('batch')
- grad_image_bank: float32 [2048, 1024], P('batch')
- grad_text_bank: float32 [2048, 1024], P('batch')
All inputs are finite; a program needn't handle non-finite values.
Results may differ from a plain program's by a relative error of at most 0.0033.
Values may be sent and summed in bfloat16 or wider, within the bound.
No kernel may reach another device: no remote copies, remote signals or barrier semaphores. Data moves between devices by JAX's collectives and lax.ppermute only.
A program may use at most 192 MiB of HBM per device.

v0:
```python
import jax
import jax.numpy as jnp
from jax import lax
from jax.sharding import PartitionSpec as P

SCALE = 20.0
EPS = 1e-06


def contract(left, right):
    return lax.dot_general(
        left, right, (((1,), (1,)), ((), ())), preferred_element_type=jnp.float32
    )


def across_rows(left, right):
    return lax.dot_general(
        left, right, (((0,), (0,)), ((), ())), preferred_element_type=jnp.float32
    )


def inverse_norm(values, width):
    part = values[:, :width].astype(jnp.float32)
    return lax.rsqrt(jnp.sum(part * part, axis=1) + EPS)


def products(query, keys, widths):
    found = []
    for width in widths:
        found.append(contract(query[:, :width], keys[:, :width]))
    return found


def bank_terms(count, lower, upper, widths, sources):
    parts = []
    for weights, queries, columns, rbank, bank in sources:
        total_term = jnp.zeros((count, upper - lower), jnp.float32)
        for level in range(6):
            width = widths[level]
            limit = min(width, upper)
            piece = weights[level]
            summed = across_rows(piece, queries[:, lower:limit])
            rsel = rbank[level]
            csel = columns[level]
            bsel = bank[:, lower:limit].astype(jnp.float32)
            term = summed - (csel * rsel * rsel)[:, None] * bsel
            total_term = total_term.at[:, : limit - lower].add(term)
        parts.append(total_term)
    return jnp.concatenate(parts, axis=1)


def on_device(image, text, image_bank, text_bank):
    rows, depth = image.shape
    bank_rows = image_bank.shape[0]
    widths = [depth // 2 ** (5 - level) for level in range(6)]
    all_image_bank, all_text_bank = (
        lax.all_gather(image_bank, "batch", axis=0, tiled=True),
        lax.all_gather(text_bank, "batch", axis=0, tiled=True),
    )
    dots_a = products(image, all_text_bank, widths)
    dots_b = products(text, all_image_bank, widths)
    grad_image = jnp.zeros((rows, depth), jnp.float32)
    grad_text = jnp.zeros((rows, depth), jnp.float32)
    weights_alist = []
    weights_blist = []
    column_alist = []
    column_blist = []
    rimage_banks = []
    rtext_banks = []
    loss_list = []
    for level in range(6):
        width = widths[level]
        rimage = inverse_norm(image, width)
        rtext = inverse_norm(text, width)
        rimage_bank = inverse_norm(all_image_bank, width)
        rtext_bank = inverse_norm(all_text_bank, width)
        img_wide = image[:, :width].astype(jnp.float32)
        txt_wide = text[:, :width].astype(jnp.float32)
        matched = SCALE * jnp.sum(img_wide * txt_wide, axis=1) * rimage * rtext
        scores_a = SCALE * dots_a[level] * rimage[:, None] * rtext_bank[None, :]
        scores_b = SCALE * dots_b[level] * rtext[:, None] * rimage_bank[None, :]
        lse_a = jnp.log(jnp.exp(matched) + jnp.sum(jnp.exp(scores_a), axis=1))
        lse_b = jnp.log(jnp.exp(matched) + jnp.sum(jnp.exp(scores_b), axis=1))
        probs_a = jnp.exp(scores_a - lse_a[:, None])
        probs_b = jnp.exp(scores_b - lse_b[:, None])
        match_grad = jnp.exp(matched - lse_a) + jnp.exp(matched - lse_b) - 2.0
        across_a = jnp.sum(probs_a * scores_a, axis=1) + match_grad * matched
        across_b = jnp.sum(probs_b * scores_b, axis=1) + match_grad * matched
        weights_a = (SCALE * rimage[:, None] * rtext_bank[None, :] * probs_a).astype(jnp.bfloat16)
        weights_b = (SCALE * rtext[:, None] * rimage_bank[None, :] * probs_b).astype(jnp.bfloat16)
        cross = SCALE * match_grad * rimage * rtext
        term_image = (
            jnp.dot(weights_a, all_text_bank[:, :width], preferred_element_type=jnp.float32)
            + cross[:, None] * txt_wide
            - (across_a * rimage * rimage)[:, None] * img_wide
        )
        term_text = (
            jnp.dot(weights_b, all_image_bank[:, :width], preferred_element_type=jnp.float32)
            + cross[:, None] * img_wide
            - (across_b * rtext * rtext)[:, None] * txt_wide
        )
        grad_image = grad_image.at[:, :width].add(term_image)
        grad_text = grad_text.at[:, :width].add(term_text)
        weights_alist.append(weights_a)
        weights_blist.append(weights_b)
        column_alist.append(jnp.sum(probs_a * scores_a, axis=0))
        column_blist.append(jnp.sum(probs_b * scores_b, axis=0))
        rimage_banks.append(rimage_bank)
        rtext_banks.append(rtext_bank)
        loss_list.append(jnp.sum(lse_a + lse_b - 2.0 * matched))
    total = rows * lax.axis_size("batch")
    losses = lax.psum(jnp.stack(loss_list), "batch") / (2.0 * total)
    sources = (
        (weights_blist, text, column_blist, rimage_banks, all_image_bank),
        (weights_alist, image, column_alist, rtext_banks, all_text_bank),
    )
    summed = lax.psum_scatter(
        bank_terms(bank_rows * lax.axis_size("batch"), 0, depth, widths, sources),
        "batch",
        scatter_dimension=0,
        tiled=True,
    )
    grad_image_bank = summed[:, :depth]
    grad_text_bank = summed[:, depth:]
    return (losses, grad_image, grad_text, grad_image_bank, grad_text_bank)


def solution(mesh):
    placed = (P("batch", None), P("batch", None), P("batch", None), P("batch", None))
    return jax.shard_map(
        on_device,
        mesh=mesh,
        in_specs=placed,
        out_specs=(P(), P("batch", None), P("batch", None), P("batch", None), P("batch", None)),
        check_vma=False,
    )
```

profile of v0, /device:TPU:1, one launch (start us, length us, event | category | flops | bytes accessed | tf_op | source)
XLA Modules:
  0.0 1632.2 jit_solution(15435062964933498818)
XLA Ops:
  8.7 1.1 copy.35
  9.8 1.2 copy.36
  13.8 117.2 %all-gather.3.cloned.1.call-done = bf16[2048,1024]{1,0:T(8,128)(2,1)} async-done(((bf16[8,1024]{1,0:T(8,128)(2,1)}), bf16[2048,1024]{1,0:T(8,128)(2,1)}) %all-gather.3.cloned.1.call-update) | async-done | bytes 4194320 | tf_op jit(solution)/shard_map/all_gather | solution.py:58
  131.0 6.5 copy.37
  137.5 0.9 fusion.161
  138.4 1.0 fusion.152
  139.5 1.2 fusion.110
  140.6 1.5 fusion.40
  142.1 2.0 fusion.6
  144.1 3.1 fusion
  147.2 99.7 %all-gather.5.cloned.1.call-done = bf16[2048,1024]{1,0:T(8,128)(2,1)} async-done(((bf16[8,1024]{1,0:T(8,128)(2,1)}), bf16[2048,1024]{1,0:T(8,128)(2,1)}) %all-gather.5.cloned.1.call-update) | async-done | bytes 4194320 | tf_op jit(solution)/shard_map/all_gather | solution.py:57
  246.9 6.7 copy.38
  253.6 0.9 fusion.162
  254.6 1.2 fusion.153
  255.7 1.4 fusion.111
  257.1 1.5 fusion.41
  258.6 2.0 fusion.8
  260.6 3.1 fusion.3
  263.9 1.6 exponential_reduce_fusion
  266.0 1.6 exponential_reduce_fusion.1
  267.6 1.3 multiply_multiply_fusion.12
  268.9 0.9 fusion.134
  271.4 1.4 multiply_multiply_fusion.13
  275.0 1.3 multiply_multiply_fusion.14
  276.4 0.9 fusion.130
  278.6 1.3 multiply_multiply_fusion.15
  279.9 0.9 fusion.128
  282.8 1.2 multiply_multiply_fusion.16
  284.0 0.9 fusion.126
  286.3 1.1 multiply_multiply_fusion.17
  287.5 1.0 fusion.124
  288.5 0.8 fusion.39
  290.4 1.0 scatter-add.91
  291.5 1.0 scatter-add.84
  292.6 1.1 fusion.34
  293.7 1.3 fusion.16
  295.0 1.6 fusion.12
  296.7 2.6 fusion.11
  299.3 2.9 fusion.2
  302.3 2.5 fusion.37
  304.8 2.7 fusion.19
  307.5 1.6 fusion.13
  309.2 2.7 fusion.10
  311.9 1.6 fusion.5
  313.6 6.4 pad_maximum_fusion
  320.0 17.6 %copy.79 = f32[2048,2048]{1,0:T(8,128)} copy(f32[2048,2048]{0,1:T(8,128)} %pad_maximum_fusion) | data formatting | bytes 33554432
  338.0 4.1 stack.27
  342.1 75.3 %psum.7 = f32[6]{0:T(128)S(1)} all-reduce(f32[6]{0:T(128)S(1)} %stack.27), channel_id=1, replica_groups=mesh['batch'=256] {'batch'}, use_global_device_ids=true, to_apply=%region_48.0 | all-reduce | flops 6 | bytes 48 | tf_op jit(solution)/shard_map/psum | solution.py:112
  417.4 2.2 fusion.109
  420.0 2.3 fusion.105
  422.3 2.2 fusion.97
  424.5 1.3 fusion.89
  425.9 1.8 fusion.79
  427.8 2.4 fusion.49
  430.2 2.1 copy.67
  432.3 2.3 fusion.107
  434.7 2.3 fusion.101
  437.1 2.2 fusion.93
  439.4 1.3 fusion.85
  440.7 1.7 fusion.70
  442.5 1.6 fusion.51
  444.1 1.0 copy.68
  445.6 1178.2 %reduce-scatter.4.cloned.1.call-done = f32[8,2048]{1,0:T(8,128)} async-done(((f32[2048,2048]{1,0:T(8,128)}), f32[8,2048]{1,0:T(8,128)}) %reduce-scatter.4.cloned.1.call-update) | async-done | bytes 65552
  1623.8 1.4 fusion.206
  (324 shorter events, 14.6 us)
Async XLA Ops:
  7.2 123.8 %all-gather.3.cloned.1.call-start = ((), (), s32[]{:S(2)}) async-start(), calls=%async_computation.1 | async-start | bytes 4210688 | tf_op jit(solution)/shard_map/all_gather | solution.py:58
  7.9 239.0 %all-gather.5.cloned.1.call-start = ((), (), s32[]{:S(2)}) async-start(), calls=%async_computation.2 | async-start | bytes 4210688 | tf_op jit(solution)/shard_map/all_gather | solution.py:57
  8.6 1615.2 %reduce-scatter.4.cloned.1.call-start = ((), (), s32[]{:S(2)}) async-start(), calls=%async_computation.3 | async-start | bytes 16842752
  9.8 286.8 %copy-start.13 = (bf16[128,1024]{0,1:T(8,128)(2,1)}, bf16[128,1024]{0,1:T(8,128)(2,1)S(1)}, u32[]{:S(2)}) copy-start(bf16[128,1024]{0,1:T(8,128)(2,1)S(1)} %copy.35) | copy-start | bytes 786436
  11.1 277.4 %copy-start.15 = (bf16[128,1024]{0,1:T(8,128)(2,1)}, bf16[128,1024]{0,1:T(8,128)(2,1)S(1)}, u32[]{:S(2)}) copy-start(bf16[128,1024]{0,1:T(8,128)(2,1)S(1)} %copy.36) | copy-start | bytes 786436
  13.2 272.1 %copy-start.71 = (f32[128]{0:T(128)}, f32[128]{0:T(128)S(1)}, u32[]{:S(2)}) copy-start(f32[128]{0:T(128)S(1)} %get-tuple-element.376) | copy-start | bytes 1540
  13.2 273.1 %copy-start.42 = (f32[128]{0:T(128)}, f32[128]{0:T(128)S(1)}, u32[]{:S(2)}) copy-start(f32[128]{0:T(128)S(1)} %get-tuple-element.374) | copy-start | bytes 1540
  13.3 268.1 %copy-start.61 = (f32[128]{0:T(128)}, f32[128]{0:T(128)S(1)}, u32[]{:S(2)}) copy-start(f32[128]{0:T(128)S(1)} %get-tuple-element.373) | copy-start | bytes 1540
  13.3 264.4 %copy-start.63 = (f32[128]{0:T(128)}, f32[128]{0:T(128)S(1)}, u32[]{:S(2)}) copy-start(f32[128]{0:T(128)S(1)} %get-tuple-element.370) | copy-start | bytes 1540
  13.4 260.8 %copy-start.65 = (f32[128]{0:T(128)}, f32[128]{0:T(128)S(1)}, u32[]{:S(2)}) copy-start(f32[128]{0:T(128)S(1)} %get-tuple-element.367) | copy-start | bytes 1540
  13.5 256.9 %copy-start.67 = (f32[128]{0:T(128)}, f32[128]{0:T(128)S(1)}, u32[]{:S(2)}) copy-start(f32[128]{0:T(128)S(1)} %get-tuple-element.364) | copy-start | bytes 1540
  13.6 251.9 %copy-start.69 = (f32[128]{0:T(128)}, f32[128]{0:T(128)S(1)}, u32[]{:S(2)}) copy-start(f32[128]{0:T(128)S(1)} %get-tuple-element.361) | copy-start | bytes 1540
  13.7 267.2 %copy-start.117 = (f32[128]{0:T(128)}, f32[128]{0:T(128)S(1)}, u32[]{:S(2)}) copy-start(f32[128]{0:T(128)S(1)} %broadcast_multiply_fusion.9) | copy-start | bytes 1540
  13.7 263.6 %copy-start.97 = (f32[128]{0:T(128)}, f32[128]{0:T(128)S(1)}, u32[]{:S(2)}) copy-start(f32[128]{0:T(128)S(1)} %broadcast_multiply_fusion.7) | copy-start | bytes 1540
  13.7 260.0 %copy-start.111 = (f32[128]{0:T(128)}, f32[128]{0:T(128)S(1)}, u32[]{:S(2)}) copy-start(f32[128]{0:T(128)S(1)} %broadcast_multiply_fusion.5) | copy-start | bytes 1540
  13.7 256.1 %copy-start.114 = (f32[128]{0:T(128)}, f32[128]{0:T(128)S(1)}, u32[]{:S(2)}) copy-start(f32[128]{0:T(128)S(1)} %broadcast_multiply_fusion.3) | copy-start | bytes 1540
  13.7 250.1 %copy-start.44 = (f32[128]{0:T(128)}, f32[128]{0:T(128)S(1)}, u32[]{:S(2)}) copy-start(f32[128]{0:T(128)S(1)} %broadcast_multiply_fusion.1) | copy-start | bytes 1540
  270.5 26.2 %copy-start.100 = (f32[128]{0:T(128)}, f32[128]{0:T(128)S(1)}, u32[]{:S(2)}) copy-start(f32[128]{0:T(128)S(1)} %get-tuple-element.430) | copy-start | bytes 1540
  271.4 25.3 %copy-start.34 = (f32[128,2048]{1,0:T(8,128)}, f32[128,2048]{1,0:T(8,128)S(1)}, u32[]{:S(2)}) copy-start(f32[128,2048]{1,0:T(8,128)S(1)} %get-tuple-element.454) | copy-start | bytes 3145732
  272.8 23.9 %copy-start.51 = (f32[128]{0:T(128)}, f32[128]{0:T(128)S(1)}, u32[]{:S(2)}) copy-start(f32[128]{0:T(128)S(1)} %get-tuple-element.416) | copy-start | bytes 1540
  274.2 20.8 %copy-start.85 = (f32[128]{0:T(128)}, f32[128]{0:T(128)S(1)}, u32[]{:S(2)}) copy-start(f32[128]{0:T(128)S(1)} %get-tuple-element.431) | copy-start | bytes 1540
  275.0 20.0 %copy-start.25 = (f32[128,2048]{1,0:T(8,128)}, f32[128,2048]{1,0:T(8,128)S(1)}, u32[]{:S(2)}) copy-start(f32[128,2048]{1,0:T(8,128)S(1)} %get-tuple-element.450) | copy-start | bytes 3145732
  276.4 18.6 %copy-start.55 = (f32[128]{0:T(128)}, f32[128]{0:T(128)S(1)}, u32[]{:S(2)}) copy-start(f32[128]{0:T(128)S(1)} %get-tuple-element.419) | copy-start | bytes 1540
  277.8 15.9 copy-start.59
  278.6 15.0 copy-start.20
  279.9 13.7 copy-start.57
  337.6 79.8 %copy-start.43 = (f32[128]{0:T(128)S(1)}, f32[128]{0:T(128)}, u32[]{:S(2)}) copy-start(f32[128]{0:T(128)} %copy-done.42) | copy-start | bytes 1540
  337.6 79.8 %copy-start.72 = (f32[128]{0:T(128)S(1)}, f32[128]{0:T(128)}, u32[]{:S(2)}) copy-start(f32[128]{0:T(128)} %copy-done.71) | copy-start | bytes 1540
  337.6 79.8 %copy-start.84 = (f32[128]{0:T(128)S(1)}, f32[128]{0:T(128)}, u32[]{:S(2)}) copy-start(f32[128]{0:T(128)} %copy-done.83) | copy-start | bytes 1540
  337.6 79.8 %copy-start.96 = (f32[128]{0:T(128)S(1)}, f32[128]{0:T(128)}, u32[]{:S(2)}) copy-start(f32[128]{0:T(128)} %get-tuple-element.358) | copy-start | bytes 1540
  337.6 79.8 %copy-start.110 = (f32[128]{0:T(128)S(1)}, f32[128]{0:T(128)}, u32[]{:S(2)}) copy-start(f32[128]{0:T(128)} %get-tuple-element.398) | copy-start | bytes 1540
  337.6 79.8 %copy-start.14 = (bf16[128,1024]{0,1:T(8,128)(2,1)S(1)}, bf16[128,1024]{0,1:T(8,128)(2,1)}, u32[]{:S(2)}) copy-start(bf16[128,1024]{0,1:T(8,128)(2,1)} %copy-done.13) | copy-start | bytes 786436
  337.6 79.8 %copy-start.17 = (bf16[128,1024]{0,1:T(8,128)(2,1)S(1)}, bf16[128,1024]{0,1:T(8,128)(2,1)}, u32[]{:S(2)}) copy-start(bf16[128,1024]{0,1:T(8,128)(2,1)} %copy-done.15) | copy-start | bytes 786436
  337.6 79.8 %copy-start.30 = (bf16[128,2048]{1,0:T(8,128)(2,1)S(1)}, bf16[128,2048]{1,0:T(8,128)(2,1)}, u32[]{:S(2)}) copy-start(bf16[128,2048]{1,0:T(8,128)(2,1)} %copy-done.29) | copy-start | bytes 1572868
  337.7 82.0 %copy-start.70 = (f32[128]{0:T(128)S(1)}, f32[128]{0:T(128)}, u32[]{:S(2)}) copy-start(f32[128]{0:T(128)} %copy-done.69) | copy-start | bytes 1540
  337.7 82.0 %copy-start.74 = (f32[128]{0:T(128)S(1)}, f32[128]{0:T(128)}, u32[]{:S(2)}) copy-start(f32[128]{0:T(128)} %copy-done.73) | copy-start | bytes 1540
  337.7 82.0 %copy-start.87 = (f32[128]{0:T(128)S(1)}, f32[128]{0:T(128)}, u32[]{:S(2)}) copy-start(f32[128]{0:T(128)} %get-tuple-element.348) | copy-start | bytes 1540
  337.7 82.0 %copy-start.105 = (f32[128]{0:T(128)S(1)}, f32[128]{0:T(128)}, u32[]{:S(2)}) copy-start(f32[128]{0:T(128)} %get-tuple-element.378) | copy-start | bytes 1540
  337.7 82.0 %copy-start.68 = (f32[128]{0:T(128)S(1)}, f32[128]{0:T(128)}, u32[]{:S(2)}) copy-start(f32[128]{0:T(128)} %copy-done.67) | copy-start | bytes 1540
  337.7 82.0 %copy-start.76 = (f32[128]{0:T(128)S(1)}, f32[128]{0:T(128)}, u32[]{:S(2)}) copy-start(f32[128]{0:T(128)} %copy-done.75) | copy-start | bytes 1540
  337.7 82.0 %copy-start.90 = (f32[128]{0:T(128)S(1)}, f32[128]{0:T(128)}, u32[]{:S(2)}) copy-start(f32[128]{0:T(128)} %get-tuple-element.350) | copy-start | bytes 1540
  337.7 82.0 %copy-start.106 = (f32[128]{0:T(128)S(1)}, f32[128]{0:T(128)}, u32[]{:S(2)}) copy-start(f32[128]{0:T(128)} %get-tuple-element.382) | copy-start | bytes 1540
  337.7 82.0 %copy-start.66 = (f32[128]{0:T(128)S(1)}, f32[128]{0:T(128)}, u32[]{:S(2)}) copy-start(f32[128]{0:T(128)} %copy-done.65) | copy-start | bytes 1540
  337.7 82.0 %copy-start.78 = (f32[128]{0:T(128)S(1)}, f32[128]{0:T(128)}, u32[]{:S(2)}) copy-start(f32[128]{0:T(128)} %copy-done.77) | copy-start | bytes 1540
  337.8 82.0 %copy-start.91 = (f32[128]{0:T(128)S(1)}, f32[128]{0:T(128)}, u32[]{:S(2)}) copy-start(f32[128]{0:T(128)} %get-tuple-element.352) | copy-start | bytes 1540
  337.8 82.0 %copy-start.107 = (f32[128]{0:T(128)S(1)}, f32[128]{0:T(128)}, u32[]{:S(2)}) copy-start(f32[128]{0:T(128)} %get-tuple-element.386) | copy-start | bytes 1540
  337.8 82.1 %copy-start.64 = (f32[128]{0:T(128)S(1)}, f32[128]{0:T(128)}, u32[]{:S(2)}) copy-start(f32[128]{0:T(128)} %copy-done.63) | copy-start | bytes 1540
  337.8 82.1 %copy-start.80 = (f32[128]{0:T(128)S(1)}, f32[128]{0:T(128)}, u32[]{:S(2)}) copy-start(f32[128]{0:T(128)} %copy-done.79) | copy-start | bytes 1540
  337.8 82.1 %copy-start.92 = (f32[128]{0:T(128)S(1)}, f32[128]{0:T(128)}, u32[]{:S(2)}) copy-start(f32[128]{0:T(128)} %get-tuple-element.354) | copy-start | bytes 1540
  337.8 82.1 %copy-start.108 = (f32[128]{0:T(128)S(1)}, f32[128]{0:T(128)}, u32[]{:S(2)}) copy-start(f32[128]{0:T(128)} %get-tuple-element.390) | copy-start | bytes 1540
  337.8 82.1 %copy-start.62 = (f32[128]{0:T(128)S(1)}, f32[128]{0:T(128)}, u32[]{:S(2)}) copy-start(f32[128]{0:T(128)} %copy-done.61) | copy-start | bytes 1540
  337.8 82.1 %copy-start.82 = (f32[128]{0:T(128)S(1)}, f32[128]{0:T(128)}, u32[]{:S(2)}) copy-start(f32[128]{0:T(128)} %copy-done.81) | copy-start | bytes 1540
  337.8 82.1 %copy-start.95 = (f32[128]{0:T(128)S(1)}, f32[128]{0:T(128)}, u32[]{:S(2)}) copy-start(f32[128]{0:T(128)} %get-tuple-element.356) | copy-start | bytes 1540
  337.8 82.1 %copy-start.109 = (f32[128]{0:T(128)S(1)}, f32[128]{0:T(128)}, u32[]{:S(2)}) copy-start(f32[128]{0:T(128)} %get-tuple-element.394) | copy-start | bytes 1540
  337.9 82.1 %copy-start.94 = (f32[128]{0:T(128)S(1)}, f32[128]{0:T(128)}, u32[]{:S(2)}) copy-start(f32[128]{0:T(128)} %copy-done.93) | copy-start | bytes 1540
  337.9 82.1 %copy-start.103 = (f32[128]{0:T(128)S(1)}, f32[128]{0:T(128)}, u32[]{:S(2)}) copy-start(f32[128]{0:T(128)} %copy-done.102) | copy-start | bytes 1540
  337.9 84.4 %copy-start.21 = (f32[128,2048]{1,0:T(8,128)S(1)}, f32[128,2048]{1,0:T(8,128)}, u32[]{:S(2)}) copy-start(f32[128,2048]{1,0:T(8,128)} %copy-done.20) | copy-start | bytes 3145732
  337.9 84.4 %copy-start.58 = (f32[128]{0:T(128)S(1)}, f32[128]{0:T(128)}, u32[]{:S(2)}) copy-start(f32[128]{0:T(128)} %copy-done.57) | copy-start | bytes 1540
  337.9 84.4 %copy-start.60 = (f32[128]{0:T(128)S(1)}, f32[128]{0:T(128)}, u32[]{:S(2)}) copy-start(f32[128]{0:T(128)} %copy-done.59) | copy-start | bytes 1540
  337.9 86.6 %copy-start.26 = (f32[128,2048]{1,0:T(8,128)S(1)}, f32[128,2048]{1,0:T(8,128)}, u32[]{:S(2)}) copy-start(f32[128,2048]{1,0:T(8,128)} %copy-done.25) | copy-start | bytes 3145732
  337.9 86.6 %copy-start.56 = (f32[128]{0:T(128)S(1)}, f32[128]{0:T(128)}, u32[]{:S(2)}) copy-start(f32[128]{0:T(128)} %copy-done.55) | copy-start | bytes 1540
  337.9 86.6 %copy-start.86 = (f32[128]{0:T(128)S(1)}, f32[128]{0:T(128)}, u32[]{:S(2)}) copy-start(f32[128]{0:T(128)} %copy-done.85) | copy-start | bytes 1540
  338.0 87.9 %copy-start.52 = (f32[128]{0:T(128)S(1)}, f32[128]{0:T(128)}, u32[]{:S(2)}) copy-start(f32[128]{0:T(128)} %copy-done.51) | copy-start | bytes 1540
  338.0 87.9 %copy-start.101 = (f32[128]{0:T(128)S(1)}, f32[128]{0:T(128)}, u32[]{:S(2)}) copy-start(f32[128]{0:T(128)} %copy-done.100) | copy-start | bytes 1540
  (62 other events, 356.4 us)
Sparse Core Ops, SparseCore 0:
  11.6 119.3 all-gather.2
  134.5 112.3 all-gather.4
  338.1 1285.7 reduce-scatter.3
where the time goes:
time: 1640 us; the launch traced here: 1630 us
  waiting for transfers between devices  1400 us (85%)
  blocking collectives  75.3 us (5%)
  matrix products  53.9 us (3%)
  other arithmetic  45.3 us (3%)
  local copies, waits for them, and re-layouts  44.4 us (3%)
  between operations  16.6 us (1%)
    unnamed x4, waiting for transfers between devices  1180 us
    all_gather x1, waiting for transfers between devices, on_device(): lax.all_gather(text_bank, 'batch', axis=0, tiled=True)  117 us
    all_gather x1, waiting for transfers between devices, on_device(): lax.all_gather(image_bank, 'batch', axis=0, tiled=True)  99.7 us
    psum x1, blocking collectives, on_device(): losses = lax.psum(jnp.stack(loss_list), 'batch') / (2.0 * total)  75.3 us
  transfers between devices with their start and end apart: 3, of which 3 were waited for; matrix products, arithmetic and copies ran while one was open for 3% of the time, Pallas kernels for 0%

commit v1 on v0

v1 whole, which is shorter than its diff:
```python
import jax
import jax.numpy as jnp
from jax import lax
from jax.experimental import pallas as pl
from jax.experimental.pallas import tpu as pltpu
from jax.sharding import Mesh, PartitionSpec as P

SCALE = 20.0
EPS = 1e-06
LOG2E = 1.4426950408889634
LEVELS = 6
EDGES = (0, 32, 64, 128, 256, 512, 1024)
D = 1024
ROWS = 128
RING = 4
CHUNK = ROWS * RING
QUERIES = 2 * CHUNK
KEYS = 256
LANES = 128
PAIRS = 32
STEP_F = 32
STEP_B = 32
VMEM_LIMIT = 56 * 1024 * 1024
BF = jnp.bfloat16
F32 = jnp.float32


def dot_nt(left, right):
    return lax.dot_general(left, right, (((1,), (1,)), ((), ())), preferred_element_type=F32)


def dot_nn(left, right):
    return lax.dot_general(left, right, (((1,), (0,)), ((), ())), preferred_element_type=F32)


def dot_tn(left, right):
    return lax.dot_general(left, right, (((0,), (0,)), ((), ())), preferred_element_type=F32)


def iota(shape, axis):
    return lax.broadcasted_iota(jnp.int32, shape, axis)


def level_mask(shape, level_axis):
    width = jnp.left_shift(32, jnp.minimum(iota(shape, level_axis), LEVELS - 1))
    return jnp.where(iota(shape, 1 - level_axis) < width, 1.0, 0.0).astype(BF)


def halves(values):
    high = values.astype(BF)
    return high, (values - high.astype(F32)).astype(BF)


def sums_across(values, mask):
    high, low = halves(values)
    return dot_nt(mask, high) + dot_nt(mask, low)


def sums_down(values, mask):
    high, low = halves(values)
    return dot_nn(high, mask) + dot_nn(low, mask)


def pick_lanes(values, level):
    lane = iota(values.shape, 1)
    keep = (lane >= EDGES[level]) & (lane < EDGES[level + 1])
    return jnp.where(keep, values.astype(F32), 0.0).astype(BF)


def keys_of(keys, side):
    return slice((1 - side) * D, (2 - side) * D)


def raw_scores(keys, queries, dots, side):
    base = (1 - side) * D
    for level in range(3):
        dots[level] = dot_nt(keys[:, base : base + LANES], pick_lanes(queries[side, :, :LANES], level))
    for level in range(3, LEVELS):
        lower, upper = EDGES[level], EDGES[level + 1]
        dots[level] = dot_nt(keys[:, base + lower : base + upper], queries[side, :, lower:upper])


def fold(values):
    return jnp.sum(values.reshape(values.shape[0] // 8, 8, values.shape[1]), axis=0)


def widen(values, n):
    return jnp.concatenate([values] * n, axis=1)


def spread(cols, level):
    return jnp.broadcast_to(cols[:, level : level + 1], (cols.shape[0], LANES))


def prepare(q0, q1, q2, q3, late, xs, rq, matched):
    across = level_mask((16, D), 0)
    for side in range(2):
        for s, q in enumerate((q0, q1, q2, q3)):
            xs[side, s * ROWS : (s + 1) * ROWS, :] = q[side * ROWS : (side + 1) * ROWS, :]
        wide = xs[side].astype(F32)
        rq[side] = lax.rsqrt(sums_across(wide * wide, across) + EPS)[:8]
    product = q0[:ROWS, :].astype(F32) * q0[ROWS:, :].astype(F32)
    matched[...] = SCALE * sums_across(product, across)[:8] * rq[0, :, :ROWS] * rq[1, :, :ROWS]


def forward(xs, xo, rq, ro, matched, keys, sums, kn, dots, wide):
    down = level_mask((D, LANES), 1)
    grown = jnp.exp(matched[...])
    for side in range(2):
        y = keys[:, keys_of(keys, side)].astype(F32)
        norms = lax.rsqrt(sums_down(y * y, down) + EPS)
        kn[side] = norms
        for level in range(LEVELS):
            wide[level] = spread(norms, level)
        for part, (queries, scale) in enumerate(((xs, rq), (xo, ro))):
            raw_scores(keys, queries, dots, side)
            row = (SCALE * LOG2E) * scale[side]

            def body(t, acc):
                at = pl.ds(pl.multiple_of(t * STEP_F, STEP_F), STEP_F)
                dot = jnp.zeros((STEP_F, CHUNK), F32)
                out = []
                for level in range(LEVELS):
                    dot = dot + dots[level, at, :]
                    key = widen(wide[level, at, :], CHUNK // LANES)
                    grow = jnp.exp2(dot * key * row[level : level + 1, :])
                    out.append(acc[level] + fold(grow))
                return tuple(out)

            start = tuple(jnp.zeros((8, CHUNK), F32) for _ in range(LEVELS))
            acc = lax.fori_loop(0, KEYS // STEP_F, body, start)
            rows = [jnp.sum(a, axis=0, keepdims=True) for a in acc]
            found = jnp.concatenate(rows + [jnp.ones((2, CHUNK), F32)], axis=0)
            sums[8 * side : 8 * side + 8, part * CHUNK : (part + 1) * CHUNK] = found
        sums[8 * side : 8 * side + 8, :ROWS] = sums[8 * side : 8 * side + 8, :ROWS] + grown
    total = jnp.sum(matched[...], axis=1, keepdims=True)
    sums[16:24, :] = jnp.broadcast_to(total, (8, QUERIES))


def suffix(rows):
    out = [rows[LEVELS - 1 : LEVELS]]
    for level in range(LEVELS - 2, -1, -1):
        out.append(out[-1] + rows[level : level + 1])
    return jnp.concatenate(out[::-1] + [jnp.zeros((2, rows.shape[1]), F32)], axis=0)


def columns_of(rows):
    n = rows.shape[1]
    return jnp.transpose(jnp.concatenate([rows, jnp.zeros((LANES - 8, n), F32)], axis=0))


def by_lane(parts):
    lane = iota(parts[0].shape, 1)
    return jnp.where(lane < EDGES[1], parts[0], jnp.where(lane < EDGES[2], parts[1], parts[2]))


def pick(parts, block):
    if block == 0:
        return by_lane(parts[:3])
    return parts[3 if block == 1 else (4 if block < 4 else 5)]


def loss_tail(loss):
    high = loss.astype(BF).astype(F32)
    mid = (loss - high).astype(BF).astype(F32)
    low = (loss - high) - mid
    lane = iota(loss.shape, 1)
    return jnp.where(lane == 0, high, jnp.where(lane == 1, mid, jnp.where(lane == 2, low, 0.0)))


def backward(xs, xo, rq, ro, matched, keys, kn, s0, s1, s2, s3,
             send, gq0, gown, gother, dots, wide, ws, ea, acc_q):
    parts = (s0, s1, s2, s3)
    total = []
    for block in range(2 * RING):
        flip, s = divmod(block, RING)
        found = None
        for t in range(RING):
            at = flip * CHUNK + ((s - t) % RING) * ROWS
            more = parts[t][:16, at : at + ROWS]
            found = more if found is None else found + more
        total.append(found)
    total = jnp.concatenate(total, axis=1)
    inverse = 1.0 / total
    logs = jnp.log(total)
    all_matched = sum(p[16:24, :LANES] for p in parts)
    each = jnp.sum(logs[:8] + logs[8:], axis=1, keepdims=True)
    tail = loss_tail(jnp.broadcast_to(each, (8, LANES)) - 2.0 * all_matched)
    send[:, 2 * D :] = jnp.concatenate([tail] * (KEYS // 8), axis=0).astype(BF)

    own = matched[...]
    grown = jnp.exp(own)
    m = grown * inverse[:8, :ROWS] + grown * inverse[8:, :ROWS] - 2.0
    cross = columns_of(suffix(SCALE * m * rq[0, :, :ROWS] * rq[1, :, :ROWS]))
    crosses = [spread(cross, level) for level in range(LEVELS)]
    ones = jnp.ones((LANES, LANES), BF)

    for side in range(2):
        base = (1 - side) * D
        norms = kn[side]
        for level in range(LEVELS):
            wide[level] = spread(norms, level)
        for part, (queries, scale) in enumerate(((xs, rq), (xo, ro))):
            raw_scores(keys, queries, dots, side)
            cols = slice(part * CHUNK, (part + 1) * CHUNK)
            row = (SCALE * LOG2E) * scale[side]
            gain = SCALE * scale[side] * inverse[8 * side : 8 * side + 8, cols]

            def body(t, acc):
                at = pl.ds(pl.multiple_of(t * STEP_B, STEP_B), STEP_B)
                dot = jnp.zeros((STEP_B, CHUNK), F32)
                out = []
                for level in range(LEVELS):
                    dot = dot + dots[level, at, :]
                    key = widen(wide[level, at, :], CHUNK // LANES)
                    scaled = dot * key
                    grow = jnp.exp2(scaled * row[level : level + 1, :])
                    weight = grow * gain[level : level + 1, :]
                    ws[level, at, cols] = (weight * key).astype(BF)
                    pa = weight * scaled
                    out.append(acc[level] + fold(pa))
                    summed = pa[:, :LANES]
                    for b in range(1, CHUNK // LANES):
                        summed = summed + pa[:, b * LANES : (b + 1) * LANES]
                    if part == 0:
                        ea[level, at, :] = summed
                    else:
                        ea[level, at, :] = ea[level, at, :] + summed
                return tuple(out)

            start = tuple(jnp.zeros((8, CHUNK), F32) for _ in range(LEVELS))
            acc = lax.fori_loop(0, KEYS // STEP_B, body, start)
            rows = [jnp.sum(a, axis=0, keepdims=True) for a in acc]
            ca = jnp.concatenate(rows + [jnp.zeros((2, CHUNK), F32)], axis=0)
            if part == 0:
                ca = jnp.concatenate([ca[:, :ROWS] + m * own, ca[:, ROWS:]], axis=1)
            ca = columns_of(suffix(ca * scale[side] * scale[side]))
            cas = [spread(ca, level) for level in range(LEVELS)]

            for level in range(LEVELS - 1, -1, -1):
                width = max(EDGES[level + 1], LANES)
                more = dot_tn(ws[level, :, cols], keys[:, base : base + width])
                if level < 2:
                    more = jnp.where(iota((CHUNK, LANES), 1) < EDGES[level + 1], more, 0.0)
                acc_q[:, :width] = more if level == LEVELS - 1 else acc_q[:, :width] + more
            for block in range(D // LANES):
                at = slice(block * LANES, (block + 1) * LANES)
                value = acc_q[:, at] - pick(cas, block) * queries[side, :, at].astype(F32)
                if part == 0:
                    partner = xs[1 - side, :ROWS, at].astype(F32)
                    gq0[side, :, at] = value[:ROWS] + pick(crosses, block) * partner
                    gown[side, :, at] = value[ROWS:].astype(BF)
                else:
                    gother[side, :, at] = value.astype(BF)

        ebs = [None] * LEVELS
        held = None
        for level in range(LEVELS - 1, -1, -1):
            term = sums_down(ea[level], ones) * wide[level] * wide[level]
            held = term if held is None else held + term
            ebs[level] = held
        for lower, upper in ((0, 128), (128, 256), (256, 512), (512, 1024)):
            grad = None
            for level in range(2 if lower == 0 else EDGES.index(lower), LEVELS):
                more = dot_nn(ws[level, :, :CHUNK], xs[side, :, lower:upper])
                more = more + dot_nn(ws[level, :, CHUNK:], xo[side, :, lower:upper])
                grad = more if grad is None else grad + more
            if lower == 0:
                for level in (1, 0):
                    more = dot_nn(ws[level, :, :CHUNK], xs[side, :, lower:upper])
                    more = more + dot_nn(ws[level, :, CHUNK:], xo[side, :, lower:upper])
                    grad = grad + jnp.where(iota((KEYS, LANES), 1) < EDGES[level + 1], more, 0.0)
            for block in range(lower // LANES, upper // LANES):
                rel = slice(block * LANES - lower, (block + 1) * LANES - lower)
                home = slice(base + block * LANES, base + (block + 1) * LANES)
                value = grad[:, rel] - pick(ebs, block) * keys[:, home].astype(F32)
                send[:, home] = value.astype(BF)


def after_core(g0, own, other, kept, x1, x2, x3):
    for side in range(2):
        place = slice(side * ROWS, (side + 1) * ROWS)
        kept[place, :] = g0[side] + other[side, :ROWS, :].astype(F32)
        for s, ref in ((1, x1), (2, x2), (3, x3)):
            mine = own[side, (s - 1) * ROWS : s * ROWS, :].astype(F32)
            theirs = other[side, s * ROWS : (s + 1) * ROWS, :].astype(F32)
            ref[place, :] = (mine + theirs).astype(BF)


def at_end(got, after, image_bank, text_bank, losses):
    for at in range(0, 2 * D, 2 * LANES):
        value = fold(got[:, at : at + 2 * LANES].astype(F32))
        if at < D:
            image_bank[:, at : at + 2 * LANES] = value
        else:
            text_bank[:, at - D : at - D + 2 * LANES] = value
    tail = fold(got[:, 2 * D :].astype(F32)) * (1.0 / 65536.0)
    for level in range(LEVELS):
        losses[level] = jnp.sum(tail[level : level + 1, :])


def query_end(own, r1, r2, r3, grad_image, grad_text):
    for kind, ref in ((0, grad_image), (1, grad_text)):
        rows = slice(kind * ROWS, (kind + 1) * ROWS)
        value = own[rows, :] + r1[rows, :].astype(F32)
        ref[...] = value + (r2[rows, :].astype(F32) + r3[rows, :].astype(F32))


def shaped(shape, dtype=F32):
    return jax.ShapeDtypeStruct(shape, dtype)


def call(kernel, outs, scratch=()):
    return pl.pallas_call(
        kernel,
        out_shape=tuple(outs),
        scratch_shapes=tuple(scratch),
        compiler_params=pltpu.CompilerParams(vmem_limit_bytes=VMEM_LIMIT),
    )


def move(value, step, flip=0):
    pairs = []
    for i in range(2 * RING):
        x, c = divmod(i, 2)
        pairs.append((i, 2 * ((x + step) % RING) + (c ^ flip)))
    return lax.ppermute(value, ("x", "c"), pairs)


def exchange(value):
    return lax.all_to_all(value, ("y", "z"), 0, 0, tiled=True)


def prepare_call(queries, late):
    return pl.pallas_call(
        prepare,
        out_shape=(shaped((2, CHUNK, D), BF), shaped((2, 8, CHUNK)), shaped((8, ROWS))),
        in_specs=[pl.BlockSpec(memory_space=pltpu.VMEM)] * 4 + [pl.BlockSpec(memory_space=pl.ANY)],
        compiler_params=pltpu.CompilerParams(vmem_limit_bytes=VMEM_LIMIT),
    )(*queries, late)


def forward_call(*values):
    return call(
        forward,
        [shaped((24, QUERIES)), shaped((2, KEYS, LANES))],
        [pltpu.VMEM((LEVELS, KEYS, CHUNK), F32), pltpu.VMEM((LEVELS, KEYS, LANES), F32)],
    )(*values)


def backward_call(*values):
    return call(
        backward,
        [
            shaped((KEYS, 2 * D + LANES), BF),
            shaped((2, ROWS, D)),
            shaped((2, CHUNK - ROWS, D), BF),
            shaped((2, CHUNK, D), BF),
        ],
        [
            pltpu.VMEM((LEVELS, KEYS, CHUNK), F32),
            pltpu.VMEM((LEVELS, KEYS, LANES), F32),
            pltpu.VMEM((LEVELS, KEYS, QUERIES), BF),
            pltpu.VMEM((LEVELS, KEYS, LANES), F32),
            pltpu.VMEM((CHUNK, D), F32),
        ],
    )(*values)


def on_device(image, text, image_bank, text_bank):
    query = jnp.concatenate([image, text], axis=0)
    queries = [query] + [move(query, s) for s in (1, 2, 3)]
    bank = jnp.concatenate([image_bank, text_bank], axis=1)
    keys = exchange(jnp.tile(bank, (PAIRS, 1)))
    xs, rq, matched = prepare_call(queries, keys)
    xo, ro = move(xs, 0, 1), move(rq, 0, 1)

    sums, kn = forward_call(xs, xo, rq, ro, matched, keys)
    theirs = move(sums, 0, 1)
    sums = sums + jnp.concatenate([theirs[:, CHUNK:], theirs[:, :CHUNK]], axis=1)
    found = [sums] + [move(sums, s) for s in (1, 2, 3)]
    send, gq0, gown, gother = backward_call(xs, xo, rq, ro, matched, keys, kn, *found)

    got = exchange(send)
    kept, x1, x2, x3 = call(after_core, [shaped((2 * ROWS, D))] + [shaped((2 * ROWS, D), BF)] * 3)(
        gq0, gown, move(gother, 0, 1)
    )
    back = [move(g, -s) for s, g in ((1, x1), (2, x2), (3, x3))]
    grad_image, grad_text = call(query_end, [shaped((ROWS, D))] * 2)(kept, *back)
    grad_image_bank, grad_text_bank, losses = pl.pallas_call(
        at_end,
        out_shape=(shaped((8, D)), shaped((8, D)), shaped((LEVELS,))),
        in_specs=[pl.BlockSpec(memory_space=pltpu.VMEM), pl.BlockSpec(memory_space=pl.ANY)],
        out_specs=(pl.BlockSpec(memory_space=pltpu.VMEM),) * 2 + (pl.BlockSpec(memory_space=pltpu.SMEM),),
        compiler_params=pltpu.CompilerParams(vmem_limit_bytes=VMEM_LIMIT),
    )(got, grad_image)
    return losses, grad_image, grad_text, grad_image_bank, grad_text_bank


def solution(mesh):
    torus = Mesh(mesh.devices.reshape(4, 8, 4, 2), ("y", "z", "x", "c"))
    rows = P(("y", "z", "x", "c"), None)
    return jax.shard_map(
        on_device,
        mesh=torus,
        in_specs=(rows,) * 4,
        out_specs=(P(),) + (rows,) * 4,
        check_vma=False,
    )
```

time: 1640 us -> 145 us (0.09)
  waiting for transfers between devices: 1400 us -> 63.6 us
  blocking collectives: 75.3 us -> 0 us
  matrix products: 53.9 us -> 0 us
  other arithmetic: 45.3 us -> 1.7 us
  Pallas kernels: 0 us -> 41 us
  local copies, waits for them, and re-layouts: 44.4 us -> 7.42 us
  starting transfers between devices: 0.11 us -> 29.5 us
    unnamed x4 -> x0, waiting for transfers between devices: 1180 us -> none
    all_gather x2 -> x0, waiting for transfers between devices: 217 us -> none  [the longest x1 117 us: on_device(): lax.all_gather(text_bank, 'batch', axis=0, tiled=True)]
    psum x1 -> x0, blocking collectives: 75.3 us -> none  [on_device(): losses = lax.psum(jnp.stack(loss_list), 'batch') / (2.0 * total)]
    ppermute x0 -> x13, waiting for transfers between devices: none -> 63.6 us  [move(): return lax.ppermute(value, ('x', 'c'), pairs)]
    dot_general x36 -> x0, matrix products: 53.9 us -> none  [the longest x12 22.3 us: across_rows(): lax.dot_general(left, right, (((0,), (0,)), ((), ())), preferred_element_...]
    pallas_call x0 -> x6, Pallas kernels: none -> 41 us  [the longest x1 19.2 us: backward_call(): call(backward, [shaped((KEYS, 2 * D + LANES), BF), shaped((2, ROWS, D)),...]
    reduce_sum x30 -> x0, other arithmetic: 27.7 us -> none  [the longest x18 20.2 us: inverse_norm(): return lax.rsqrt(jnp.sum(part * part, axis=1) + EPS)]
    all_to_all x0 -> x2, starting transfers between devices: none -> 19.4 us  [exchange(): return lax.all_to_all(value, ('y', 'z'), 0, 0, tiled=True)]
  transfers between devices with their start and end apart: 3 -> 15, of which waited for: 3 -> 11; matrix products, arithmetic and copies ran while one was open for 3% -> 0% of each run, Pallas kernels for 0% -> 5%
where the time goes in v1:
time: 145 us; the launch traced here: 144 us
  waiting for transfers between devices  63.6 us (44%)
  Pallas kernels  41 us (28%)
  starting transfers between devices  29.5 us (20%)
  local copies, waits for them, and re-layouts  7.42 us (5%)
  other arithmetic  1.7 us (1%)
    ppermute x13, waiting for transfers between devices, move(): return lax.ppermute(value, ('x', 'c'), pairs)  63.6 us
    all_to_all x2, starting transfers between devices, exchange(): return lax.all_to_all(value, ('y', 'z'), 0, 0, tiled=True)  19.4 us
    pallas_call x1, Pallas kernels, backward_call(): call(backward, [shaped((KEYS, 2 * D + LANES), BF), shaped((2, ROWS, D)),...  19.2 us
    ppermute x13, starting transfers between devices, move(): return lax.ppermute(value, ('x', 'c'), pairs)  10.1 us
    pallas_call x1, Pallas kernels, forward_call(): call(forward, [shaped((24, QUERIES)), shaped((2, KEYS, LANES))], [pltpu.V...  9.12 us
    unnamed x37, local copies, waits for them, and re-layouts  6.29 us
    pallas_call x1, Pallas kernels, on_device(): call(after_core, [shaped((2 * ROWS, D))] + [shaped((2 * ROWS, D), BF)] * 3)  4.01 us
    pallas_call x1, Pallas kernels, prepare_call(): pl.pallas_call(prepare, out_shape=(shaped((2, CHUNK, D), BF), shaped((2,...  3.8 us
  transfers between devices with their start and end apart: 15, of which 11 were waited for; matrix products, arithmetic and copies ran while one was open for 0% of the time, Pallas kernels for 5%

profile of v1, /device:TPU:1, one launch (start us, length us, event | category | flops | bytes accessed | tf_op | source)
XLA Modules:
  0.0 144.2 jit_solution(7620588025515283879)
XLA Ops:
  0.6 0.0 copy-start.12
  0.6 0.0 copy-start.13
  0.7 0.8 pad_maximum_fusion
  1.4 1.1 tile.2
  2.6 12.0 %all-to-all-start = ((bf16[32,8,2048]{2,1,0:T(8,128)(2,1)}), bf16[32,8,2048]{2,1,0:T(8,128)(2,1)S(1)}, u32[]{:S(2)}, u32[]{:S(2)}) async-start(bf16[32,8,2048]{2,1,0:T(8,128)(2,1)} %tile.2), calls=%async_computation | async-start | bytes 2097152 | tf_op jit(solution)/shard_map/all_to_all | solution.py:331
  14.6 0.0 copy-done.12
  14.6 0.0 copy-done.13
  14.7 0.0 copy-start.4
  14.7 2.6 %collective-permute-start.2 = (bf16[256,1024]{1,0:T(8,128)(2,1)S(1)}, bf16[256,1024]{1,0:T(8,128)(2,1)S(1)}, u32[]{:S(2)}, u32[]{:S(2)}) collective-permute-start(bf16[256,1024]{1,0:T(8,128)(2,1)S(1)} %constant_dynamic-update-slice_fusion.q0), channel_id=1, source_target_pairs={{0,6},{1,7},{2,0},{3,1},{4,2},{5,3},{6,4},{7,5},{8,14},{9,15},{10,... | collective-permute-start | bytes 1572872 | tf_op jit(solution)/shard_map/ppermute | solution.py:327
  17.2 0.5 collective-permute-start.1
  17.8 0.6 collective-permute-start
  18.4 9.9 %collective-permute-done.2.q3 = bf16[256,1024]{1,0:T(8,128)(2,1)S(1)} collective-permute-done((bf16[256,1024]{1,0:T(8,128)(2,1)S(1)}, bf16[256,1024]{1,0:T(8,128)(2,1)S(1)}, u32[]{:S(2)}, u32[]{:S(2)}) %collective-permute-start.2) | collective-permute-done | bytes 524320 | tf_op jit(solution)/shard_map/ppermute | solution.py:327
  28.3 2.7 %collective-permute-done.1.q2 = bf16[256,1024]{1,0:T(8,128)(2,1)S(1)} collective-permute-done((bf16[256,1024]{1,0:T(8,128)(2,1)S(1)}, bf16[256,1024]{1,0:T(8,128)(2,1)S(1)}, u32[]{:S(2)}, u32[]{:S(2)}) %collective-permute-start.1) | collective-permute-done | bytes 524320 | tf_op jit(solution)/shard_map/ppermute | solution.py:327
  31.0 0.0 copy-start.9
  31.0 12.9 %collective-permute-done.q1 = bf16[256,1024]{1,0:T(8,128)(2,1)S(1)} collective-permute-done((bf16[256,1024]{1,0:T(8,128)(2,1)S(1)}, bf16[256,1024]{1,0:T(8,128)(2,1)S(1)}, u32[]{:S(2)}, u32[]{:S(2)}) %collective-permute-start) | collective-permute-done | bytes 524320 | tf_op jit(solution)/shard_map/ppermute | solution.py:327
  43.8 0.0 copy-start.10
  43.8 0.0 all-to-all-done
  43.8 0.0 copy-done.4
  43.8 0.0 copy-done.8
  43.8 0.0 copy-done.9
  43.9 0.8 copy-done.10
  44.6 0.4 copy-done
  45.0 3.8 %shard_map.83 = (bf16[2,512,1024]{2,1,0:T(8,128)(2,1)}, f32[2,8,512]{2,1,0:T(8,128)}, f32[8,128]{1,0:T(8,128)}) custom-call(bf16[256,1024]{1,0:T(8,128)(2,1)} %copy-done.4, bf16[256,1024]{1,0:T(8,128)(2,1)} %copy-done.10, bf16[256,1024]{1,0:T(8,128)(2,1)} %copy-done.9, bf16[256,1024]{1,0:T(8,128)(2,1)} %copy-done.8, bf16[256,2048]{1,0:T(8,128)(2,1)} %bitcast.3), custom_call_target="tpu_custom_call" | custom-call | tf_op jit(solution)/shard_map/pallas_call | solution.py:335
  48.8 0.5 collective-permute-start.3
  49.3 0.0 collective-permute-start.4
  49.3 4.0 %collective-permute-done.4.ro = f32[2,8,512]{2,1,0:T(8,128)S(1)} collective-permute-done((f32[2,8,512]{2,1,0:T(8,128)}, f32[2,8,512]{2,1,0:T(8,128)S(1)}, u32[]{:S(2)}, u32[]{:S(2)}) %collective-permute-start.4) | collective-permute-done | bytes 32800 | tf_op jit(solution)/shard_map/ppermute | solution.py:327
  53.3 0.0 collective-permute-done.3.xo
  53.3 0.6 copy-done.14
  53.9 0.7 copy-done.1
  54.7 9.1 %shard_map.84 = (f32[24,1024]{1,0:T(8,128)}, f32[2,256,128]{2,1,0:T(8,128)}) custom-call(bf16[2,512,1024]{2,1,0:T(8,128)(2,1)} %get-tuple-element.23.xs, bf16[2,512,1024]{2,1,0:T(8,128)(2,1)} %copy-done.1, f32[2,8,512]{2,1,0:T(8,128)} %get-tuple-element.24.rq, f32[2,8,512]{2,1,0:T(8,128)} %copy-done.14, f32[8,128]{1,0:T(8,128)} %get-tuple-element.25.matched, ...), custom_call_target="tpu_custom_call" | custom-call | tf_op jit(solution)/shard_map/pallas_call | solution.py:344
  63.8 0.4 collective-permute-start.5
  64.2 1.2 collective-permute-done.5
  65.3 0.9 maximum_add_fusion.s0
  66.2 0.0 copy-start.11
  66.3 2.3 %collective-permute-start.8 = (f32[24,1024]{1,0:T(8,128)S(1)}, f32[24,1024]{1,0:T(8,128)S(1)}, u32[]{:S(2)}, u32[]{:S(2)}) collective-permute-start(f32[24,1024]{1,0:T(8,128)S(1)} %maximum_add_fusion.s0), channel_id=1, source_target_pairs={{0,6},{1,7},{2,0},{3,1},{4,2},{5,3},{6,4},{7,5},{8,14},{9,15},{10,... | collective-permute-start | bytes 294920 | tf_op jit(solution)/shard_map/ppermute | solution.py:327
  68.5 0.5 collective-permute-start.7
  69.0 0.6 collective-permute-start.6
  69.6 0.7 collective-permute-done.8.s3
  70.4 3.2 %collective-permute-done.7.s2 = f32[24,1024]{1,0:T(8,128)S(1)} collective-permute-done((f32[24,1024]{1,0:T(8,128)S(1)}, f32[24,1024]{1,0:T(8,128)S(1)}, u32[]{:S(2)}, u32[]{:S(2)}) %collective-permute-start.7) | collective-permute-done | bytes 98336 | tf_op jit(solution)/shard_map/ppermute | solution.py:327
  73.6 3.1 %collective-permute-done.6.s1 = f32[24,1024]{1,0:T(8,128)S(1)} collective-permute-done((f32[24,1024]{1,0:T(8,128)S(1)}, f32[24,1024]{1,0:T(8,128)S(1)}, u32[]{:S(2)}, u32[]{:S(2)}) %collective-permute-start.6) | collective-permute-done | bytes 98336 | tf_op jit(solution)/shard_map/ppermute | solution.py:327
  76.6 0.0 copy-done.11
  76.6 0.0 copy-done.15
  76.6 0.0 copy-done.16
  76.6 0.6 copy-done.17
  77.2 19.2 %shard_map.85 = (bf16[256,2176]{1,0:T(8,128)(2,1)}, f32[2,128,1024]{2,1,0:T(8,128)}, bf16[2,384,1024]{2,1,0:T(8,128)(2,1)}, bf16[2,512,1024]{2,1,0:T(8,128)(2,1)}) custom-call(bf16[2,512,1024]{2,1,0:T(8,128)(2,1)} %get-tuple-element.23.xs, bf16[2,512,1024]{2,1,0:T(8,128)(2,1)} %copy-done.1, f32[2,8,512]{2,1,0:T(8,128)} %get-tuple-element.24.rq, ...), custom_call_target="tpu_custom_call" | custom-call | tf_op jit(solution)/shard_map/pallas_call | solution.py:352
  96.5 0.7 collective-permute-start.9
  97.2 7.4 %all-to-all-start.1 = ((bf16[32,8,2176]{2,1,0:T(8,128)(2,1)}), bf16[32,8,2176]{2,1,0:T(8,128)(2,1)S(1)}, u32[]{:S(2)}, u32[]{:S(2)}) async-start(bf16[32,8,2176]{2,1,0:T(8,128)(2,1)} %bitcast.7), calls=%async_computation.1 | async-start | bytes 2228224 | tf_op jit(solution)/shard_map/all_to_all | solution.py:331
  104.6 0.0 collective-permute-done.9.other
  104.6 0.0 copy-start.3
  104.6 1.3 copy-done.3
  105.9 4.0 %shard_map.86 = (f32[256,1024]{1,0:T(8,128)}, bf16[256,1024]{1,0:T(8,128)(2,1)}, bf16[256,1024]{1,0:T(8,128)(2,1)}, bf16[256,1024]{1,0:T(8,128)(2,1)}) custom-call(f32[2,128,1024]{2,1,0:T(8,128)} %get-tuple-element.29.g0, bf16[2,384,1024]{2,1,0:T(8,128)(2,1)} %get-tuple-element.30.own, bf16[2,512,1024]{2,1,0:T(8,128)(2,1)} %copy-done.3), custom_call_target="tpu_custom_call" | custom-call | tf_op jit(solution)/shard_map/pallas_call | solution.py:385
  109.9 0.6 collective-permute-start.10
  110.6 0.3 collective-permute-start.11
  110.9 0.5 collective-permute-start.12
  111.4 12.0 %collective-permute-done.10.r1 = bf16[256,1024]{1,0:T(8,128)(2,1)S(1)} collective-permute-done((bf16[256,1024]{1,0:T(8,128)(2,1)}, bf16[256,1024]{1,0:T(8,128)(2,1)S(1)}, u32[]{:S(2)}, u32[]{:S(2)}) %collective-permute-start.10) | collective-permute-done | bytes 524320 | tf_op jit(solution)/shard_map/ppermute | solution.py:327
  123.4 1.8 %collective-permute-done.11.r2 = bf16[256,1024]{1,0:T(8,128)(2,1)S(1)} collective-permute-done((bf16[256,1024]{1,0:T(8,128)(2,1)}, bf16[256,1024]{1,0:T(8,128)(2,1)S(1)}, u32[]{:S(2)}, u32[]{:S(2)}) %collective-permute-start.11) | collective-permute-done | bytes 524320 | tf_op jit(solution)/shard_map/ppermute | solution.py:327
  125.2 12.1 %collective-permute-done.12.r3 = bf16[256,1024]{1,0:T(8,128)(2,1)S(1)} collective-permute-done((bf16[256,1024]{1,0:T(8,128)(2,1)}, bf16[256,1024]{1,0:T(8,128)(2,1)S(1)}, u32[]{:S(2)}, u32[]{:S(2)}) %collective-permute-start.12) | collective-permute-done | bytes 524320 | tf_op jit(solution)/shard_map/ppermute | solution.py:327
  137.4 0.0 copy-done.5
  137.4 0.0 copy-done.6
  137.4 0.8 copy-done.7
  138.1 2.7 %shard_map.87 = (f32[128,1024]{1,0:T(8,128)}, f32[128,1024]{1,0:T(8,128)}) custom-call(f32[256,1024]{1,0:T(8,128)} %get-tuple-element.32.own, bf16[256,1024]{1,0:T(8,128)(2,1)} %copy-done.5, bf16[256,1024]{1,0:T(8,128)(2,1)} %copy-done.6, bf16[256,1024]{1,0:T(8,128)(2,1)} %copy-done.7), custom_call_target="tpu_custom_call" | custom-call | tf_op jit(solution)/shard_map/pallas_call | solution.py:389
  140.9 0.0 all-to-all-done.1
  140.9 1.0 copy-done.2
  141.9 2.1 %shard_map.88 = (f32[8,1024]{1,0:T(8,128)}, f32[8,1024]{1,0:T(8,128)}, f32[6]{0:T(128)}) custom-call(bf16[256,2176]{1,0:T(8,128)(2,1)} %bitcast.6, f32[128,1024]{1,0:T(8,128)} %get-tuple-element.19.after), custom_call_target="tpu_custom_call" | custom-call | tf_op jit(solution)/shard_map/pallas_call | solution.py:390
  (14 shorter events, 0.1 us)
Async XLA Ops:
  0.6 14.0 %copy-start.12 = (bf16[128,1024]{1,0:T(8,128)(2,1)S(1)}, bf16[128,1024]{1,0:T(8,128)(2,1)}, u32[]{:S(2)}) copy-start(bf16[128,1024]{1,0:T(8,128)(2,1)} %param.4) | copy-start | bytes 786436
  0.6 14.0 %copy-start.13 = (bf16[128,1024]{1,0:T(8,128)(2,1)S(1)}, bf16[128,1024]{1,0:T(8,128)(2,1)}, u32[]{:S(2)}) copy-start(bf16[128,1024]{1,0:T(8,128)(2,1)} %param.5) | copy-start | bytes 786436
  2.6 41.3 %all-to-all-start = ((bf16[32,8,2048]{2,1,0:T(8,128)(2,1)}), bf16[32,8,2048]{2,1,0:T(8,128)(2,1)S(1)}, u32[]{:S(2)}, u32[]{:S(2)}) async-start(bf16[32,8,2048]{2,1,0:T(8,128)(2,1)} %tile.2), calls=%async_computation | async-start | bytes 2097152 | tf_op jit(solution)/shard_map/all_to_all | solution.py:331
  14.7 29.2 %copy-start.4 = (bf16[256,1024]{1,0:T(8,128)(2,1)}, bf16[256,1024]{1,0:T(8,128)(2,1)S(1)}, u32[]{:S(2)}) copy-start(bf16[256,1024]{1,0:T(8,128)(2,1)S(1)} %constant_dynamic-update-slice_fusion.q0) | copy-start | bytes 1572868
  14.7 13.6 %collective-permute-start.2 = (bf16[256,1024]{1,0:T(8,128)(2,1)S(1)}, bf16[256,1024]{1,0:T(8,128)(2,1)S(1)}, u32[]{:S(2)}, u32[]{:S(2)}) collective-permute-start(bf16[256,1024]{1,0:T(8,128)(2,1)S(1)} %constant_dynamic-update-slice_fusion.q0), channel_id=1, source_target_pairs={{0,6},{1,7},{2,0},{3,1},{4,2},{5,3},{6,4},{7,5},{8,14},{9,15},{10,... | collective-permute-start | bytes 1572872 | tf_op jit(solution)/shard_map/ppermute | solution.py:327
  17.2 13.7 %collective-permute-start.1 = (bf16[256,1024]{1,0:T(8,128)(2,1)S(1)}, bf16[256,1024]{1,0:T(8,128)(2,1)S(1)}, u32[]{:S(2)}, u32[]{:S(2)}) collective-permute-start(bf16[256,1024]{1,0:T(8,128)(2,1)S(1)} %constant_dynamic-update-slice_fusion.q0), channel_id=1, source_target_pairs={{0,4},{1,5},{2,6},{3,7},{4,0},{5,1},{6,2},{7,3},{8,12},{9,13},{10,... | collective-permute-start | bytes 1572872 | tf_op jit(solution)/shard_map/ppermute | solution.py:327
  17.8 26.1 %collective-permute-start = (bf16[256,1024]{1,0:T(8,128)(2,1)S(1)}, bf16[256,1024]{1,0:T(8,128)(2,1)S(1)}, u32[]{:S(2)}, u32[]{:S(2)}) collective-permute-start(bf16[256,1024]{1,0:T(8,128)(2,1)S(1)} %constant_dynamic-update-slice_fusion.q0), channel_id=1, source_target_pairs={{0,2},{1,3},{2,4},{3,5},{4,6},{5,7},{6,0},{7,1},{8,10},{9,11},{10,... | collective-permute-start | bytes 1572872 | tf_op jit(solution)/shard_map/ppermute | solution.py:327
  28.3 15.5 %copy-start.8 = (bf16[256,1024]{1,0:T(8,128)(2,1)}, bf16[256,1024]{1,0:T(8,128)(2,1)S(1)}, u32[]{:S(2)}) copy-start(bf16[256,1024]{1,0:T(8,128)(2,1)S(1)} %collective-permute-done.2.q3) | copy-start | bytes 1572868
  31.0 12.9 %copy-start.9 = (bf16[256,1024]{1,0:T(8,128)(2,1)}, bf16[256,1024]{1,0:T(8,128)(2,1)S(1)}, u32[]{:S(2)}) copy-start(bf16[256,1024]{1,0:T(8,128)(2,1)S(1)} %collective-permute-done.1.q2) | copy-start | bytes 1572868
  43.8 0.8 copy-start.10
  43.8 1.2 copy-start
  48.8 4.5 %collective-permute-start.3 = (bf16[2,512,1024]{2,1,0:T(8,128)(2,1)}, bf16[2,512,1024]{2,1,0:T(8,128)(2,1)S(1)}, u32[]{:S(2)}, u32[]{:S(2)}) collective-permute-start(bf16[2,512,1024]{2,1,0:T(8,128)(2,1)} %get-tuple-element.23.xs), channel_id=1, source_target_pairs={{0,1},{1,0},{2,3},{3,2},{4,5},{5,4},{6,7},{7,6},{8,9},{9,8},{10,11... | collective-permute-start | bytes 6291464 | tf_op jit(solution)/shard_map/ppermute | solution.py:327
  49.3 4.0 %collective-permute-start.4 = (f32[2,8,512]{2,1,0:T(8,128)}, f32[2,8,512]{2,1,0:T(8,128)S(1)}, u32[]{:S(2)}, u32[]{:S(2)}) collective-permute-start(f32[2,8,512]{2,1,0:T(8,128)} %get-tuple-element.24.rq), channel_id=1, source_target_pairs={{0,1},{1,0},{2,3},{3,2},{4,5},{5,4},{6,7},{7,6},{8,9},{9,8},{10,11... | collective-permute-start | bytes 98312 | tf_op jit(solution)/shard_map/ppermute | solution.py:327
  53.3 0.6 copy-start.14
  53.3 1.3 copy-start.1
  63.8 1.5 %collective-permute-start.5 = (f32[24,1024]{1,0:T(8,128)}, f32[24,1024]{1,0:T(8,128)S(1)}, u32[]{:S(2)}, u32[]{:S(2)}) collective-permute-start(f32[24,1024]{1,0:T(8,128)} %get-tuple-element.27), channel_id=1, source_target_pairs={{0,1},{1,0},{2,3},{3,2},{4,5},{5,4},{6,7},{7,6},{8,9},{9,8},{10,11... | collective-permute-start | bytes 294920 | tf_op jit(solution)/shard_map/ppermute | solution.py:327
  66.2 10.4 %copy-start.11 = (f32[24,1024]{1,0:T(8,128)}, f32[24,1024]{1,0:T(8,128)S(1)}, u32[]{:S(2)}) copy-start(f32[24,1024]{1,0:T(8,128)S(1)} %maximum_add_fusion.s0) | copy-start | bytes 294916
  66.3 4.1 %collective-permute-start.8 = (f32[24,1024]{1,0:T(8,128)S(1)}, f32[24,1024]{1,0:T(8,128)S(1)}, u32[]{:S(2)}, u32[]{:S(2)}) collective-permute-start(f32[24,1024]{1,0:T(8,128)S(1)} %maximum_add_fusion.s0), channel_id=1, source_target_pairs={{0,6},{1,7},{2,0},{3,1},{4,2},{5,3},{6,4},{7,5},{8,14},{9,15},{10,... | collective-permute-start | bytes 294920 | tf_op jit(solution)/shard_map/ppermute | solution.py:327
  68.5 5.1 %collective-permute-start.7 = (f32[24,1024]{1,0:T(8,128)S(1)}, f32[24,1024]{1,0:T(8,128)S(1)}, u32[]{:S(2)}, u32[]{:S(2)}) collective-permute-start(f32[24,1024]{1,0:T(8,128)S(1)} %maximum_add_fusion.s0), channel_id=1, source_target_pairs={{0,4},{1,5},{2,6},{3,7},{4,0},{5,1},{6,2},{7,3},{8,12},{9,13},{10,... | collective-permute-start | bytes 294920 | tf_op jit(solution)/shard_map/ppermute | solution.py:327
  69.0 7.6 %collective-permute-start.6 = (f32[24,1024]{1,0:T(8,128)S(1)}, f32[24,1024]{1,0:T(8,128)S(1)}, u32[]{:S(2)}, u32[]{:S(2)}) collective-permute-start(f32[24,1024]{1,0:T(8,128)S(1)} %maximum_add_fusion.s0), channel_id=1, source_target_pairs={{0,2},{1,3},{2,4},{3,5},{4,6},{5,7},{6,0},{7,1},{8,10},{9,11},{10,... | collective-permute-start | bytes 294920 | tf_op jit(solution)/shard_map/ppermute | solution.py:327
  70.4 6.3 %copy-start.15 = (f32[24,1024]{1,0:T(8,128)}, f32[24,1024]{1,0:T(8,128)S(1)}, u32[]{:S(2)}) copy-start(f32[24,1024]{1,0:T(8,128)S(1)} %collective-permute-done.8.s3) | copy-start | bytes 294916
  73.6 3.1 %copy-start.16 = (f32[24,1024]{1,0:T(8,128)}, f32[24,1024]{1,0:T(8,128)S(1)}, u32[]{:S(2)}) copy-start(f32[24,1024]{1,0:T(8,128)S(1)} %collective-permute-done.7.s2) | copy-start | bytes 294916
  76.6 0.6 copy-start.17
  96.5 8.1 %collective-permute-start.9 = (bf16[2,512,1024]{2,1,0:T(8,128)(2,1)}, bf16[2,512,1024]{2,1,0:T(8,128)(2,1)S(1)}, u32[]{:S(2)}, u32[]{:S(2)}) collective-permute-start(bf16[2,512,1024]{2,1,0:T(8,128)(2,1)} %get-tuple-element.31), channel_id=1, source_target_pairs={{0,1},{1,0},{2,3},{3,2},{4,5},{5,4},{6,7},{7,6},{8,9},{9,8},{10,11... | collective-permute-start | bytes 6291464 | tf_op jit(solution)/shard_map/ppermute | solution.py:327
  97.2 43.7 %all-to-all-start.1 = ((bf16[32,8,2176]{2,1,0:T(8,128)(2,1)}), bf16[32,8,2176]{2,1,0:T(8,128)(2,1)S(1)}, u32[]{:S(2)}, u32[]{:S(2)}) async-start(bf16[32,8,2176]{2,1,0:T(8,128)(2,1)} %bitcast.7), calls=%async_computation.1 | async-start | bytes 2228224 | tf_op jit(solution)/shard_map/all_to_all | solution.py:331
  104.6 1.4 copy-start.3
  109.9 13.4 %collective-permute-start.10 = (bf16[256,1024]{1,0:T(8,128)(2,1)}, bf16[256,1024]{1,0:T(8,128)(2,1)S(1)}, u32[]{:S(2)}, u32[]{:S(2)}) collective-permute-start(bf16[256,1024]{1,0:T(8,128)(2,1)} %get-tuple-element.33), channel_id=1, source_target_pairs={{0,6},{1,7},{2,0},{3,1},{4,2},{5,3},{6,4},{7,5},{8,14},{9,15},{10,... | collective-permute-start | bytes 1572872 | tf_op jit(solution)/shard_map/ppermute | solution.py:327
  110.6 14.7 %collective-permute-start.11 = (bf16[256,1024]{1,0:T(8,128)(2,1)}, bf16[256,1024]{1,0:T(8,128)(2,1)S(1)}, u32[]{:S(2)}, u32[]{:S(2)}) collective-permute-start(bf16[256,1024]{1,0:T(8,128)(2,1)} %get-tuple-element.34), channel_id=1, source_target_pairs={{0,4},{1,5},{2,6},{3,7},{4,0},{5,1},{6,2},{7,3},{8,12},{9,13},{10,... | collective-permute-start | bytes 1572872 | tf_op jit(solution)/shard_map/ppermute | solution.py:327
  110.9 26.5 %collective-permute-start.12 = (bf16[256,1024]{1,0:T(8,128)(2,1)}, bf16[256,1024]{1,0:T(8,128)(2,1)S(1)}, u32[]{:S(2)}, u32[]{:S(2)}) collective-permute-start(bf16[256,1024]{1,0:T(8,128)(2,1)} %get-tuple-element.35), channel_id=1, source_target_pairs={{0,2},{1,3},{2,4},{3,5},{4,6},{5,7},{6,0},{7,1},{8,10},{9,11},{10,... | collective-permute-start | bytes 1572872 | tf_op jit(solution)/shard_map/ppermute | solution.py:327
  123.4 14.0 %copy-start.5 = (bf16[256,1024]{1,0:T(8,128)(2,1)}, bf16[256,1024]{1,0:T(8,128)(2,1)S(1)}, u32[]{:S(2)}) copy-start(bf16[256,1024]{1,0:T(8,128)(2,1)S(1)} %collective-permute-done.10.r1) | copy-start | bytes 1572868
  125.2 12.1 %copy-start.6 = (bf16[256,1024]{1,0:T(8,128)(2,1)}, bf16[256,1024]{1,0:T(8,128)(2,1)S(1)}, u32[]{:S(2)}) copy-start(bf16[256,1024]{1,0:T(8,128)(2,1)S(1)} %collective-permute-done.11.r2) | copy-start | bytes 1572868
  137.4 0.8 copy-start.7
  140.9 1.0 copy-start.2

commit v2 on v1

v2 whole, which is shorter than its diff:
```python
import jax
import jax.numpy as jnp
from jax import lax
from jax.experimental import pallas as pl
from jax.experimental.pallas import tpu as pltpu
from jax.sharding import Mesh, PartitionSpec as P

SCALE = 20.0
EPS = 1e-06
LOG2E = 1.4426950408889634
LEVELS = 6
EDGES = (0, 32, 64, 128, 256, 512, 1024)
D = 1024
ROWS = 128
RING = 4
CHUNK = ROWS * RING
KEYS = 256
BANK = 2 * KEYS
LANES = 128
PAIRS = 8
NEAR = 64
STEP_F = 32
STEP_B = 32
VMEM_LIMIT = 56 * 1024 * 1024
BF = jnp.bfloat16
F32 = jnp.float32


def dot_nt(left, right):
    return lax.dot_general(left, right, (((1,), (1,)), ((), ())), preferred_element_type=F32)


def dot_nn(left, right):
    return lax.dot_general(left, right, (((1,), (0,)), ((), ())), preferred_element_type=F32)


def dot_tn(left, right):
    return lax.dot_general(left, right, (((0,), (0,)), ((), ())), preferred_element_type=F32)


def iota(shape, axis):
    return lax.broadcasted_iota(jnp.int32, shape, axis)


def level_mask(shape, level_axis):
    width = jnp.left_shift(32, jnp.minimum(iota(shape, level_axis), LEVELS - 1))
    return jnp.where(iota(shape, 1 - level_axis) < width, 1.0, 0.0).astype(BF)


def halves(values):
    high = values.astype(BF)
    return high, (values - high.astype(F32)).astype(BF)


def sums_across(values, mask):
    high, low = halves(values)
    return dot_nt(mask, high) + dot_nt(mask, low)


def sums_down(values, mask):
    high, low = halves(values)
    return dot_nn(high, mask) + dot_nn(low, mask)


def pick_lanes(values, level):
    lane = iota(values.shape, 1)
    keep = (lane >= EDGES[level]) & (lane < EDGES[level + 1])
    return jnp.where(keep, values.astype(F32), 0.0).astype(BF)


def keys_of(keys, side):
    return slice((1 - side) * D, (2 - side) * D)


def raw_scores(keys, queries, dots, side):
    base = (1 - side) * D
    for level in range(3):
        dots[level] = dot_nt(keys[:, base : base + LANES], pick_lanes(queries[side, :, :LANES], level))
    for level in range(3, LEVELS):
        lower, upper = EDGES[level], EDGES[level + 1]
        dots[level] = dot_nt(keys[:, base + lower : base + upper], queries[side, :, lower:upper])


def fold(values):
    return jnp.sum(values.reshape(values.shape[0] // 8, 8, values.shape[1]), axis=0)


def widen(values, n):
    return jnp.concatenate([values] * n, axis=1)


def spread(cols, level):
    return jnp.broadcast_to(cols[:, level : level + 1], (cols.shape[0], LANES))


def prepare(q0, q1, q2, q3, rq, matched):
    across = level_mask((16, D), 0)
    for side in range(2):
        rows = slice(side * ROWS, (side + 1) * ROWS)
        for s, block in enumerate((q0[rows, :], q1[rows, :], q2[rows, :], q3[rows, :])):
            wide = block.astype(F32)
            found = lax.rsqrt(sums_across(wide * wide, across) + EPS)
            rq[side, :, s * ROWS : (s + 1) * ROWS] = found[:8]
    product = q0[:ROWS, :].astype(F32) * q0[ROWS:, :].astype(F32)
    matched[...] = SCALE * sums_across(product, across)[:8] * rq[0, :, :ROWS] * rq[1, :, :ROWS]


def prepare_keys(b0, b1, b2, b3, after, kn):
    down = level_mask((D, LANES), 1)
    for s, block in enumerate((b0, b1, b2, b3)):
        for side in range(2):
            y = block[:, keys_of(block, side)].astype(F32)
            kn[side, s * NEAR : (s + 1) * NEAR, :] = lax.rsqrt(sums_down(y * y, down) + EPS)


def fetch(blocks, xs, ks, sems):
    q0, q1, q2, q3 = blocks[:4]
    count = 0

    def start(source, target):
        nonlocal count
        copy = pltpu.make_async_copy(source, target, sems.at[count])
        copy.start()
        count += 1
        return copy

    def queries(side):
        rows = slice(side * ROWS, (side + 1) * ROWS)
        parts = (q0.at[rows, :], q1.at[rows, :], q2.at[rows, :], q3.at[rows, :])
        return [start(p, xs.at[side, s * ROWS : (s + 1) * ROWS, :]) for s, p in enumerate(parts)]

    def keys(part):
        found = blocks[4 + 4 * part : 8 + 4 * part]
        return [start(b, ks.at[part * KEYS + s * NEAR : part * KEYS + (s + 1) * NEAR, :]) for s, b in enumerate(found)]

    first = queries(0)
    return [first, keys(0), keys(1), queries(1)]


def arrive(copies):
    for copy in copies:
        copy.wait()


def forward(*refs):
    rq, matched, n0, n1 = refs[12:16]
    sums, xs, ks, dots, wide, sems = refs[16:]
    near_queries, near_keys, far_keys, other_queries = fetch(refs[:12], xs, ks, sems)
    grown = jnp.exp(matched[...])
    total = jnp.broadcast_to(jnp.sum(matched[...], axis=1, keepdims=True), (8, ROWS))
    spare = [jnp.concatenate([total[r : r + 1] for r in rows], axis=1) for rows in ((0, 1, 2, 3), (4, 5, 5, 5))]
    for side in range(2):
        row = (SCALE * LOG2E) * rq[side]
        arrive(near_queries if side == 0 else other_queries)
        acc = tuple(jnp.zeros((8, CHUNK), F32) for _ in range(LEVELS))
        for part, norms in enumerate((n0, n1)):
            if side == 0:
                arrive((near_keys, far_keys)[part])
            rows = slice(part * KEYS, (part + 1) * KEYS)
            for level in range(LEVELS):
                wide[level, rows, :] = spread(norms[side], level)
            raw_scores(ks.at[rows, :], xs, dots.at[part], side)

            def body(t, acc):
                at = pl.ds(pl.multiple_of(t * STEP_F, STEP_F), STEP_F)
                to = pl.ds(pl.multiple_of(part * KEYS + t * STEP_F, STEP_F), STEP_F)
                dot = jnp.zeros((STEP_F, CHUNK), F32)
                out = []
                for level in range(LEVELS):
                    dot = dot + dots[part, level, at, :]
                    key = widen(wide[level, to, :], CHUNK // LANES)
                    grow = jnp.exp2(dot * key * row[level : level + 1, :])
                    out.append(acc[level] + fold(grow))
                return tuple(out)

            acc = lax.fori_loop(0, KEYS // STEP_F, body, acc, unroll=True)
        rows = [jnp.sum(a, axis=0, keepdims=True) for a in acc]
        sums[8 * side : 8 * side + 8, :] = jnp.concatenate(rows + spare, axis=0)
        sums[8 * side : 8 * side + LEVELS, :ROWS] = sums[8 * side : 8 * side + LEVELS, :ROWS] + grown[:LEVELS]


def suffix(rows):
    out = [rows[LEVELS - 1 : LEVELS]]
    for level in range(LEVELS - 2, -1, -1):
        out.append(out[-1] + rows[level : level + 1])
    return jnp.concatenate(out[::-1] + [jnp.zeros((2, rows.shape[1]), F32)], axis=0)


def columns_of(rows):
    n = rows.shape[1]
    return jnp.transpose(jnp.concatenate([rows, jnp.zeros((LANES - 8, n), F32)], axis=0))


def by_lane(parts):
    lane = iota(parts[0].shape, 1)
    return jnp.where(lane < EDGES[1], parts[0], jnp.where(lane < EDGES[2], parts[1], parts[2]))


def pick(parts, block):
    if block == 0:
        return by_lane(parts[:3])
    return parts[3 if block == 1 else (4 if block < 4 else 5)]


def put_loss(ref, loss):
    ref[:, 2 * D :] = jnp.concatenate([loss_tail(loss)] * (NEAR // 8), axis=0).astype(ref.dtype)


def loss_of(ref):
    tail = ref[:, 2 * D :].astype(F32)[:8]
    return jnp.broadcast_to(jnp.sum(tail, axis=1, keepdims=True), (8, LANES))


def loss_tail(loss):
    high = loss.astype(BF).astype(F32)
    mid = (loss - high).astype(BF).astype(F32)
    low = (loss - high) - mid
    lane = iota(loss.shape, 1)
    return jnp.where(lane == 0, high, jnp.where(lane == 1, mid, jnp.where(lane == 2, low, 0.0)))


def backward(*refs):
    rq, matched, n0, n1, s0, s1, s2, s3 = refs[12:20]
    outs, loss = refs[20:26], refs[26]
    xs, ks, gq0, gq1, gq2, gq3, gown, gother, dots, wide, ws, ea, acc_q, sems, out_sems = refs[27:]
    near_queries, near_keys, far_keys, other_queries = fetch(refs[:12], xs, ks, sems)
    leaving = []

    def leave(n, rows, cols):
        source = (gq0, gq1, gq2, gq3, gown, gother)[n]
        copy = pltpu.make_async_copy(source.at[rows, cols], outs[n].at[rows, cols], out_sems.at[len(leaving)])
        copy.start()
        leaving.append(copy)

    parts = (s0, s1, s2, s3)
    total = []
    for s in range(RING):
        found = None
        for t in range(RING):
            at = ((s - t) % RING) * ROWS
            more = parts[t][:, at : at + ROWS]
            found = more if found is None else found + more
        total.append(found)
    total = jnp.concatenate(total, axis=1)
    inverse = 1.0 / total
    logs = jnp.log(total)
    spare = (s0[6:8, :] + s1[6:8, :]) + (s2[6:8, :] + s3[6:8, :])
    all_matched = [spare[r // 4 : r // 4 + 1, (r % 4) * ROWS : (r % 4 + 1) * ROWS] for r in range(LEVELS)]
    all_matched = jnp.concatenate(all_matched + [jnp.zeros((2, ROWS), F32)], axis=0)
    each = jnp.sum(logs[:8] + logs[8:], axis=1, keepdims=True)
    mine = jnp.broadcast_to(each, (8, LANES)) - 2.0 * all_matched
    loss[...] = mine
    gother[KEYS:, :LANES] = jnp.concatenate([loss_tail(mine)] * 2, axis=0).astype(BF)
    gother[KEYS:, LANES:] = jnp.zeros((16, 2 * D - LANES), BF)

    own = matched[...]
    grown = jnp.exp(own)
    m = grown * inverse[:8, :ROWS] + grown * inverse[8:, :ROWS] - 2.0
    cross = columns_of(suffix(SCALE * m * rq[0, :, :ROWS] * rq[1, :, :ROWS]))
    crosses = [spread(cross, level) for level in range(LEVELS)]
    ones = jnp.ones((LANES, LANES), BF)

    for side in range(2):
        base = (1 - side) * D
        if side == 0:
            arrive(near_queries)
        row = (SCALE * LOG2E) * rq[side]
        gain = SCALE * rq[side] * inverse[8 * side : 8 * side + 8, :]
        acc = tuple(jnp.zeros((8, CHUNK), F32) for _ in range(LEVELS))
        for part, norms in enumerate((n0, n1)):
            if side == 0:
                arrive((near_keys, far_keys)[part])
            rows = slice(part * KEYS, (part + 1) * KEYS)
            for level in range(LEVELS):
                wide[level, rows, :] = spread(norms[side], level)
            raw_scores(ks.at[rows, :], xs, dots.at[part], side)

            def body(t, acc):
                at = pl.ds(pl.multiple_of(t * STEP_B, STEP_B), STEP_B)
                to = pl.ds(pl.multiple_of(part * KEYS + t * STEP_B, STEP_B), STEP_B)
                dot = jnp.zeros((STEP_B, CHUNK), F32)
                sums = []
                for level in range(LEVELS):
                    dot = dot + dots[part, level, at, :]
                    key = widen(wide[level, to, :], CHUNK // LANES)
                    scaled = dot * key
                    grow = jnp.exp2(scaled * row[level : level + 1, :])
                    weight = grow * gain[level : level + 1, :]
                    ws[level, to, :] = (weight * key).astype(BF)
                    pa = weight * scaled
                    sums.append(acc[level] + fold(pa))
                    summed = pa[:, :LANES]
                    for b in range(1, CHUNK // LANES):
                        summed = summed + pa[:, b * LANES : (b + 1) * LANES]
                    ea[level, to, :] = summed
                return tuple(sums)

            acc = lax.fori_loop(0, KEYS // STEP_B, body, acc, unroll=True)

        ebs = [None] * LEVELS
        held = None
        for level in range(LEVELS - 1, -1, -1):
            term = sums_down(ea[level], ones) * wide[level] * wide[level]
            held = term if held is None else held + term
            ebs[level] = held
        for lower, upper in ((0, 128), (128, 256), (256, 512), (512, 1024)):
            grad = None
            for level in range(2 if lower == 0 else EDGES.index(lower), LEVELS):
                more = dot_nn(ws[level], xs[side, :, lower:upper])
                grad = more if grad is None else grad + more
            if lower == 0:
                for level in (1, 0):
                    more = dot_nn(ws[level], xs[side, :, lower:upper])
                    grad = grad + jnp.where(iota((BANK, LANES), 1) < EDGES[level + 1], more, 0.0)
            for block in range(lower // LANES, upper // LANES):
                rel = slice(block * LANES - lower, (block + 1) * LANES - lower)
                home = slice(base + block * LANES, base + (block + 1) * LANES)
                value = grad[:, rel] - pick(ebs, block) * ks[:, home].astype(F32)
                gown[:, home] = value[:KEYS]
                gother[:KEYS, home] = value[KEYS:].astype(BF)
        leave(4, slice(0, KEYS), slice(base, base + D))
        leave(5, slice(0, KEYS + 16), slice(base, base + D))

        rows = [jnp.sum(a, axis=0, keepdims=True) for a in acc]
        if side == 0:
            arrive(other_queries)
        ca = jnp.concatenate(rows + [jnp.zeros((2, CHUNK), F32)], axis=0)
        ca = jnp.concatenate([ca[:, :ROWS] + m * own, ca[:, ROWS:]], axis=1)
        ca = columns_of(suffix(ca * rq[side] * rq[side]))
        cas = [spread(ca, level) for level in range(LEVELS)]
        for level in range(LEVELS - 1, -1, -1):
            width = max(EDGES[level + 1], LANES)
            more = dot_tn(ws[level], ks[:, base : base + width])
            if level < 2:
                more = jnp.where(iota((CHUNK, LANES), 1) < EDGES[level + 1], more, 0.0)
            acc_q[:, :width] = more if level == LEVELS - 1 else acc_q[:, :width] + more
        place = slice(side * ROWS, (side + 1) * ROWS)
        for block in range(D // LANES):
            at = slice(block * LANES, (block + 1) * LANES)
            value = acc_q[:, at] - pick(cas, block) * xs[side, :, at].astype(F32)
            partner = xs[1 - side, :ROWS, at].astype(F32)
            gq0[place, at] = value[:ROWS] + pick(crosses, block) * partner
            for s, ref in ((1, gq1), (2, gq2), (3, gq3)):
                ref[place, at] = value[s * ROWS : (s + 1) * ROWS].astype(BF)
        for n in range(RING):
            leave(n, place, slice(0, D))
    arrive(leaving)


def after_core(own, other, loss, kept, y1, y2, y3):
    tail = other[KEYS:, :LANES].astype(F32)[:8]
    total = loss[...] + jnp.broadcast_to(jnp.sum(tail, axis=1, keepdims=True), (8, LANES))
    for s, ref in enumerate((kept, y1, y2, y3)):
        rows = slice(s * NEAR, (s + 1) * NEAR)
        ref[:, : 2 * D] = (own[rows, :] + other[rows, :].astype(F32)).astype(ref.dtype)
        put_loss(ref, total)


def after_y(own, r1, r2, r3, *rest):
    send = rest[-1]
    for at in range(0, 2 * D, LANES):
        cols = slice(at, at + LANES)
        value = own[:, cols] + r1[:, cols].astype(F32)
        send[:, cols] = (value + (r2[:, cols].astype(F32) + r3[:, cols].astype(F32))).astype(BF)
    put_loss(send, (loss_of(own) + loss_of(r1)) + (loss_of(r2) + loss_of(r3)))


def at_end(got, after, image_bank, text_bank, losses):
    for at in range(0, 2 * D, 2 * LANES):
        value = fold(got[:, at : at + 2 * LANES].astype(F32))
        if at < D:
            image_bank[:, at : at + 2 * LANES] = value
        else:
            text_bank[:, at - D : at - D + 2 * LANES] = value
    tail = fold(got[:, 2 * D :].astype(F32)) * (1.0 / 65536.0)
    for level in range(LEVELS):
        losses[level] = jnp.sum(tail[level : level + 1, :])


def query_end(own, r1, r2, r3, grad_image, grad_text):
    for kind, ref in ((0, grad_image), (1, grad_text)):
        rows = slice(kind * ROWS, (kind + 1) * ROWS)
        value = own[rows, :] + r1[rows, :].astype(F32)
        ref[...] = value + (r2[rows, :].astype(F32) + r3[rows, :].astype(F32))


def shaped(shape, dtype=F32):
    return jax.ShapeDtypeStruct(shape, dtype)


def call(kernel, outs, scratch=()):
    return pl.pallas_call(
        kernel,
        out_shape=tuple(outs),
        scratch_shapes=tuple(scratch),
        compiler_params=pltpu.CompilerParams(vmem_limit_bytes=VMEM_LIMIT),
    )


def move(value, step, flip=0):
    pairs = []
    for i in range(2 * RING):
        x, c = divmod(i, 2)
        pairs.append((i, 2 * ((x + step) % RING) + (c ^ flip)))
    return lax.ppermute(value, ("x", "c"), pairs)


def along_y(value, step):
    n = lax.axis_size("y")
    return lax.ppermute(value, "y", [(i, (i + step) % n) for i in range(n)])


def exchange(value):
    return lax.all_to_all(value, "z", 0, 0, tiled=True)


ANYWHERE = pl.BlockSpec(memory_space=pl.ANY)
INSIDE = pl.BlockSpec(memory_space=pltpu.VMEM)


def placed(kernel, ins, outs, shapes, scratch=()):
    return pl.pallas_call(
        kernel,
        out_shape=tuple(shapes),
        in_specs=list(ins),
        out_specs=tuple(outs),
        scratch_shapes=tuple(scratch),
        compiler_params=pltpu.CompilerParams(vmem_limit_bytes=VMEM_LIMIT),
    )


def on_device(image, text, image_bank, text_bank):
    query = jnp.concatenate([image, text], axis=0)
    queries = [query] + [move(query, s) for s in (1, 2, 3)]
    bank = jnp.concatenate([image_bank, text_bank], axis=1)
    near = exchange(jnp.tile(bank, (PAIRS, 1)))
    around = [near] + [along_y(near, s) for s in (1, 2, 3)]
    rq, matched = call(prepare, [shaped((2, 8, CHUNK)), shaped((8, ROWS))])(*queries)
    (n0,) = placed(prepare_keys, [INSIDE] * 4 + [ANYWHERE], [INSIDE], [shaped((2, KEYS, LANES))])(*around, matched)
    n1 = move(n0, 0, 1)
    far = [move(b, 0, 1) for b in around]
    blocks = queries + around + far
    held = [
        pltpu.VMEM((2, CHUNK, D), BF),
        pltpu.VMEM((BANK, 2 * D), BF),
    ]
    scores = [pltpu.VMEM((2, LEVELS, KEYS, CHUNK), F32), pltpu.VMEM((LEVELS, BANK, LANES), F32)]

    (sums,) = placed(
        forward,
        [ANYWHERE] * 12 + [INSIDE] * 4,
        [INSIDE],
        [shaped((16, CHUNK))],
        held + scores + [pltpu.SemaphoreType.DMA((16,))],
    )(*blocks, rq, matched, n0, n1)
    found = [sums] + [move(sums, s) for s in (1, 2, 3)]
    grads = [
        shaped((2 * ROWS, D)),
        shaped((2 * ROWS, D), BF),
        shaped((2 * ROWS, D), BF),
        shaped((2 * ROWS, D), BF),
        shaped((KEYS, 2 * D)),
        shaped((KEYS + 16, 2 * D), BF),
    ]
    gq0, gq1, gq2, gq3, gown, gother, loss = placed(
        backward,
        [ANYWHERE] * 12 + [INSIDE] * 8,
        [ANYWHERE] * 6 + [INSIDE],
        grads + [shaped((8, LANES))],
        held
        + [pltpu.VMEM(g.shape, g.dtype) for g in grads]
        + scores
        + [
            pltpu.VMEM((LEVELS, BANK, CHUNK), BF),
            pltpu.VMEM((LEVELS, BANK, LANES), F32),
            pltpu.VMEM((CHUNK, D), F32),
            pltpu.SemaphoreType.DMA((16,)),
            pltpu.SemaphoreType.DMA((12,)),
        ],
    )(*blocks, rq, matched, n0, n1, *found)

    back = [move(g, -s) for s, g in ((1, gq1), (2, gq2), (3, gq3))]
    kept, y1, y2, y3 = call(
        after_core,
        [shaped((NEAR, 2 * D + LANES))] + [shaped((NEAR, 2 * D + LANES), BF)] * 3,
    )(gown, move(gother, 0, 1), loss)
    summed = [along_y(g, -s) for s, g in ((1, y1), (2, y2), (3, y3))]
    (send,) = placed(
        after_y, [INSIDE] * 4 + [ANYWHERE] * 1, [INSIDE], [shaped((NEAR, 2 * D + LANES), BF)]
    )(kept, *summed, back[0])
    got = exchange(send)
    grad_image, grad_text = call(query_end, [shaped((ROWS, D))] * 2)(gq0, *back)
    grad_image_bank, grad_text_bank, losses = placed(
        at_end,
        [INSIDE, ANYWHERE],
        [INSIDE, INSIDE, pl.BlockSpec(memory_space=pltpu.SMEM)],
        [shaped((8, D)), shaped((8, D)), shaped((LEVELS,))],
    )(got, grad_image)
    return losses, grad_image, grad_text, grad_image_bank, grad_text_bank


def solution(mesh):
    torus = Mesh(mesh.devices.reshape(4, 8, 4, 2), ("y", "z", "x", "c"))
    rows = P(("y", "z", "x", "c"), None)
    return jax.shard_map(
        on_device,
        mesh=torus,
        in_specs=(rows,) * 4,
        out_specs=(P(),) + (rows,) * 4,
        check_vma=False,
    )
```

time: 145 us -> 135 us (0.931)
  waiting for transfers between devices: 63.6 us -> 44.3 us
  starting transfers between devices: 29.5 us -> 39.6 us
    ppermute x13 -> x15, waiting for transfers between devices: 63.6 us -> 17 us  [move(): return lax.ppermute(value, ('x', 'c'), pairs)]
    all_to_all x2, waiting for transfers between devices: 0.01 us -> 16.3 us  [exchange(): return lax.all_to_all(value, 'z', 0, 0, tiled=True)]
    ppermute x0 -> x6, waiting for transfers between devices: none -> 10.9 us  [along_y(): return lax.ppermute(value, 'y', [(i, (i + step) % n) for i in range(n)])]
    ppermute x0 -> x6, starting transfers between devices: none -> 7.55 us  [along_y(): return lax.ppermute(value, 'y', [(i, (i + step) % n) for i in range(n)])]
    ppermute x13 -> x15, starting transfers between devices: 10.1 us -> 17.2 us  [move(): return lax.ppermute(value, ('x', 'c'), pairs)]
    all_to_all x2, starting transfers between devices: 19.4 us -> 14.8 us  [exchange(): return lax.all_to_all(value, 'z', 0, 0, tiled=True)]
    pallas_call x6 -> x8, Pallas kernels: 41 us -> 39.8 us  [the longest x1 17.4 us: on_device(): placed(backward, [ANYWHERE] * 12 + [INSIDE] * 8, [ANYWHERE] * 6 + [INSIDE...]
    unnamed x37 -> x53, local copies, waits for them, and re-layouts: 6.29 us -> 6.75 us
  transfers between devices with their start and end apart: 15 -> 23, of which waited for: 11 -> 11; matrix products, arithmetic and copies ran while one was open for 0% -> 1% of each run, Pallas kernels for 5% -> 11%
where the time goes in v2:
time: 135 us; the launch traced here: 134 us
  waiting for transfers between devices  44.3 us (33%)
  Pallas kernels  39.8 us (29%)
  starting transfers between devices  39.6 us (29%)
  local copies, waits for them, and re-layouts  8.44 us (6%)
    pallas_call x1, Pallas kernels, on_device(): placed(backward, [ANYWHERE] * 12 + [INSIDE] * 8, [ANYWHERE] * 6 + [INSIDE...  17.4 us
    ppermute x15, starting transfers between devices, move(): return lax.ppermute(value, ('x', 'c'), pairs)  17.2 us
    ppermute x15, waiting for transfers between devices, move(): return lax.ppermute(value, ('x', 'c'), pairs)  17 us
    all_to_all x2, waiting for transfers between devices, exchange(): return lax.all_to_all(value, 'z', 0, 0, tiled=True)  16.3 us
    all_to_all x2, starting transfers between devices, exchange(): return lax.all_to_all(value, 'z', 0, 0, tiled=True)  14.8 us
    ppermute x6, waiting for transfers between devices, along_y(): return lax.ppermute(value, 'y', [(i, (i + step) % n) for i in range(n)])  10.9 us
    ppermute x6, starting transfers between devices, along_y(): return lax.ppermute(value, 'y', [(i, (i + step) % n) for i in range(n)])  7.55 us
    unnamed x53, local copies, waits for them, and re-layouts  6.75 us
  transfers between devices with their start and end apart: 23, of which 11 were waited for; matrix products, arithmetic and copies ran while one was open for 1% of the time, Pallas kernels for 11%

profile of v2, /device:TPU:1, one launch (start us, length us, event | category | flops | bytes accessed | tf_op | source)
XLA Modules:
  0.0 133.8 jit_solution(11951556728291954235)
XLA Ops:
  0.6 1.0 constant_dynamic-update-slice_fusion.1
  1.6 1.0 constant_dynamic-update-slice_fusion.q0.refs_0_
  2.6 0.0 copy-start
  2.6 3.4 %collective-permute-start.2 = (bf16[256,1024]{1,0:T(8,128)(2,1)S(1)}, bf16[256,1024]{1,0:T(8,128)(2,1)S(1)}, u32[]{:S(2)}, u32[]{:S(2)}) collective-permute-start(bf16[256,1024]{1,0:T(8,128)(2,1)S(1)} %constant_dynamic-update-slice_fusion.q0.refs_0_), channel_id=1, source_target_pairs={{0,6},{1,7},{2,0},{3,1},{4,2},{5,3},{6,4},{7,5},{8,14},{9,15},{10,... | collective-permute-start | bytes 1572872 | tf_op jit(solution)/shard_map/ppermute | solution.py:405
  6.0 0.7 pad_maximum_fusion
  6.7 0.7 tile.2
  7.4 8.2 %all-to-all-start = ((bf16[8,8,2048]{2,1,0:T(8,128)(2,1)}), bf16[8,8,2048]{2,1,0:T(8,128)(2,1)S(1)}, u32[]{:S(2)}, u32[]{:S(2)}) async-start(bf16[8,8,2048]{2,1,0:T(8,128)(2,1)} %tile.2), calls=%async_computation | async-start | bytes 524288 | tf_op jit(solution)/shard_map/all_to_all | solution.py:414
  15.6 0.5 collective-permute-start.1
  16.1 0.6 collective-permute-start
  16.7 9.0 %all-to-all-done = bf16[8,8,2048]{2,1,0:T(8,128)(2,1)S(1)} async-done(((bf16[8,8,2048]{2,1,0:T(8,128)(2,1)}), bf16[8,8,2048]{2,1,0:T(8,128)(2,1)S(1)}, u32[]{:S(2)}, u32[]{:S(2)}) %all-to-all-start) | async-done | bytes 262176 | tf_op jit(solution)/shard_map/all_to_all | solution.py:414
  25.7 2.7 %collective-permute-start.5 = (bf16[64,2048]{1,0:T(8,128)(2,1)S(1)}, bf16[64,2048]{1,0:T(8,128)(2,1)S(1)}, u32[]{:S(2)}, u32[]{:S(2)}) collective-permute-start(bf16[64,2048]{1,0:T(8,128)(2,1)S(1)} %bitcast.3), channel_id=1, source_target_pairs={{0,192},{64,0},{128,64},{192,128},{1,193},{65,1},{129,65},{193,129... | collective-permute-start | bytes 786440 | tf_op jit(solution)/shard_map/ppermute | solution.py:410
  28.4 0.3 collective-permute-start.4
  28.8 0.0 collective-permute-done.2.q3.refs_3_
  28.8 0.7 collective-permute-start.3
  29.5 0.0 collective-permute-done.1.q2.refs_2_
  29.5 3.8 %collective-permute-start.6 = (bf16[64,2048]{1,0:T(8,128)(2,1)S(1)}, bf16[64,2048]{1,0:T(8,128)(2,1)S(1)}, u32[]{:S(2)}, u32[]{:S(2)}) collective-permute-start(bf16[64,2048]{1,0:T(8,128)(2,1)S(1)} %bitcast.6), channel_id=1, source_target_pairs={{0,1},{1,0},{2,3},{3,2},{4,5},{5,4},{6,7},{7,6},{8,9},{9,8},{10,11... | collective-permute-start | bytes 786440 | tf_op jit(solution)/shard_map/ppermute | solution.py:405
  33.3 8.9 %collective-permute-done.q1.refs_1_ = bf16[256,1024]{1,0:T(8,128)(2,1)S(1)} collective-permute-done((bf16[256,1024]{1,0:T(8,128)(2,1)S(1)}, bf16[256,1024]{1,0:T(8,128)(2,1)S(1)}, u32[]{:S(2)}, u32[]{:S(2)}) %collective-permute-start) | collective-permute-done | bytes 524320 | tf_op jit(solution)/shard_map/ppermute | solution.py:405
  42.2 0.0 copy-start.3
  42.2 0.8 copy-done.3
  43.0 3.5 %shard_map.83 = (f32[2,8,512]{2,1,0:T(8,128)}, f32[8,128]{1,0:T(8,128)}) custom-call(bf16[256,1024]{1,0:T(8,128)(2,1)} %copy-done, bf16[256,1024]{1,0:T(8,128)(2,1)} %copy-done.3, bf16[256,1024]{1,0:T(8,128)(2,1)} %copy-done.2, bf16[256,1024]{1,0:T(8,128)(2,1)} %copy-done.1), custom_call_target="tpu_custom_call" | custom-call | tf_op jit(solution)/shard_map/pallas_call | solution.py:438
  46.5 0.6 collective-permute-start.9
  47.1 0.0 collective-permute-done.4.b2.refs_6_
  47.1 0.1 collective-permute-start.8
  47.2 0.4 collective-permute-start.7
  47.6 0.2 copy-done.6
  47.8 0.1 copy-done.7
  48.0 2.7 %shard_map.84.refs_14_ = f32[2,256,128]{2,1,0:T(8,128)} custom-call(bf16[64,2048]{1,0:T(8,128)(2,1)} %bitcast.7, bf16[64,2048]{1,0:T(8,128)(2,1)} %copy-done.7, bf16[64,2048]{1,0:T(8,128)(2,1)} %copy-done.6, bf16[64,2048]{1,0:T(8,128)(2,1)} %copy-done.5, f32[8,128]{1,0:T(8,128)} %get-tuple-element.24.after.refs_13_), custom_call_target="tpu_custom_call" | custom-call | tf_op jit(solution)/shard_map/pallas_call | solution.py:439
  50.6 0.4 collective-permute-start.10
  51.0 0.0 collective-permute-done.6.refs_8_
  51.0 0.0 collective-permute-done.9.refs_11_
  51.1 1.3 collective-permute-done.10.refs_15_
  52.4 0.7 copy-done.15
  53.1 6.5 %shard_map.85.refs_16_ = f32[16,512]{1,0:T(8,128)} custom-call(bf16[256,1024]{1,0:T(8,128)(2,1)} %copy-done, bf16[256,1024]{1,0:T(8,128)(2,1)} %copy-done.3, bf16[256,1024]{1,0:T(8,128)(2,1)} %copy-done.2, bf16[256,1024]{1,0:T(8,128)(2,1)} %copy-done.1, bf16[64,2048]{1,0:T(8,128)(2,1)} %bitcast.8, bf16[64,2048]{1,0:T(8,128)(2,1)} %copy-done.7, ...), custom_call_target="tpu_custom_call" | custom-call | tf_op jit(solution)/shard_map/pallas_call | solution.py:449
  59.6 0.4 collective-permute-start.13
  60.0 0.5 collective-permute-start.12
  60.5 0.6 collective-permute-start.11
  61.2 1.5 %collective-permute-done.13.refs_19_ = f32[16,512]{1,0:T(8,128)S(1)} collective-permute-done((f32[16,512]{1,0:T(8,128)}, f32[16,512]{1,0:T(8,128)S(1)}, u32[]{:S(2)}, u32[]{:S(2)}) %collective-permute-start.13) | collective-permute-done | bytes 32800 | tf_op jit(solution)/shard_map/ppermute | solution.py:405
  62.7 1.8 %collective-permute-done.12.refs_18_ = f32[16,512]{1,0:T(8,128)S(1)} collective-permute-done((f32[16,512]{1,0:T(8,128)}, f32[16,512]{1,0:T(8,128)S(1)}, u32[]{:S(2)}, u32[]{:S(2)}) %collective-permute-start.12) | collective-permute-done | bytes 32800 | tf_op jit(solution)/shard_map/ppermute | solution.py:405
  64.5 0.6 collective-permute-done.11.refs_17_
  65.1 0.6 copy-done.23
  65.7 17.4 %shard_map.86 = (f32[256,1024]{1,0:T(8,128)}, bf16[256,1024]{1,0:T(8,128)(2,1)}, bf16[256,1024]{1,0:T(8,128)(2,1)}, bf16[256,1024]{1,0:T(8,128)(2,1)}, f32[256,2...) custom-call(bf16[256,1024]{1,0:T(8,128)(2,1)} %copy-done, bf16[256,1024]{1,0:T(8,128)(2,1)} %copy-done.3, ...), custom_call_target="tpu_custom_call" | custom-call | tf_op jit(solution)/shard_map/pallas_call | solution.py:465
  83.1 1.9 %collective-permute-start.14 = (bf16[272,2048]{1,0:T(8,128)(2,1)}, bf16[272,2048]{1,0:T(8,128)(2,1)S(1)}, u32[]{:S(2)}, u32[]{:S(2)}) collective-permute-start(bf16[272,2048]{1,0:T(8,128)(2,1)} %get-tuple-element.26), channel_id=1, source_target_pairs={{0,1},{1,0},{2,3},{3,2},{4,5},{5,4},{6,7},{7,6},{8,9},{9,8},{10,11... | collective-permute-start | bytes 3342344 | tf_op jit(solution)/shard_map/ppermute | solution.py:405
  85.0 1.7 %collective-permute-start.18 = (bf16[256,1024]{1,0:T(8,128)(2,1)}, bf16[256,1024]{1,0:T(8,128)(2,1)S(1)}, u32[]{:S(2)}, u32[]{:S(2)}) collective-permute-start(bf16[256,1024]{1,0:T(8,128)(2,1)} %get-tuple-element.32), channel_id=1, source_target_pairs={{0,6},{1,7},{2,0},{3,1},{4,2},{5,3},{6,4},{7,5},{8,14},{9,15},{10,... | collective-permute-start | bytes 1572872 | tf_op jit(solution)/shard_map/ppermute | solution.py:405
  86.7 0.9 collective-permute-done.14.other
  87.6 1.0 copy-done.9
  88.6 3.2 %shard_map.87 = (f32[64,2176]{1,0:T(8,128)}, bf16[64,2176]{1,0:T(8,128)(2,1)}, bf16[64,2176]{1,0:T(8,128)(2,1)}, bf16[64,2176]{1,0:T(8,128)(2,1)}) custom-call(f32[256,2048]{1,0:T(8,128)} %get-tuple-element.25.own, bf16[272,2048]{1,0:T(8,128)(2,1)} %copy-done.9, f32[8,128]{1,0:T(8,128)} %get-tuple-element.27.loss), custom_call_target="tpu_custom_call" | custom-call | tf_op jit(solution)/shard_map/pallas_call | solution.py:483
  91.8 2.7 %collective-permute-start.15 = (bf16[64,2176]{1,0:T(8,128)(2,1)}, bf16[64,2176]{1,0:T(8,128)(2,1)S(1)}, u32[]{:S(2)}, u32[]{:S(2)}) collective-permute-start(bf16[64,2176]{1,0:T(8,128)(2,1)} %get-tuple-element.29), channel_id=1, source_target_pairs={{0,192},{64,0},{128,64},{192,128},{1,193},{65,1},{129,65},{193,129... | collective-permute-start | bytes 835592 | tf_op jit(solution)/shard_map/ppermute | solution.py:410
  94.5 0.3 collective-permute-start.16
  94.9 0.7 collective-permute-start.17
  95.6 1.1 collective-permute-start.19
  96.7 2.0 %collective-permute-done.18.rest_0_.r1 = bf16[256,1024]{1,0:T(8,128)(2,1)S(1)} collective-permute-done((bf16[256,1024]{1,0:T(8,128)(2,1)}, bf16[256,1024]{1,0:T(8,128)(2,1)S(1)}, u32[]{:S(2)}, u32[]{:S(2)}) %collective-permute-start.18) | collective-permute-done | bytes 524320 | tf_op jit(solution)/shard_map/ppermute | solution.py:405
  98.7 1.1 collective-permute-start.20
  99.8 6.5 %collective-permute-done.15.r1 = bf16[64,2176]{1,0:T(8,128)(2,1)S(1)} collective-permute-done((bf16[64,2176]{1,0:T(8,128)(2,1)}, bf16[64,2176]{1,0:T(8,128)(2,1)S(1)}, u32[]{:S(2)}, u32[]{:S(2)}) %collective-permute-start.15) | collective-permute-done | bytes 278560 | tf_op jit(solution)/shard_map/ppermute | solution.py:410
  106.3 0.0 collective-permute-done.16.r2
  106.3 4.4 %collective-permute-done.17.r3 = bf16[64,2176]{1,0:T(8,128)(2,1)S(1)} collective-permute-done((bf16[64,2176]{1,0:T(8,128)(2,1)}, bf16[64,2176]{1,0:T(8,128)(2,1)S(1)}, u32[]{:S(2)}, u32[]{:S(2)}) %collective-permute-start.17) | collective-permute-done | bytes 278560 | tf_op jit(solution)/shard_map/ppermute | solution.py:410
  110.8 0.7 copy-done.20
  111.5 2.1 %shard_map.88 = bf16[64,2176]{1,0:T(8,128)(2,1)} custom-call(f32[64,2176]{1,0:T(8,128)} %get-tuple-element.28.own, bf16[64,2176]{1,0:T(8,128)(2,1)} %copy-done.18, bf16[64,2176]{1,0:T(8,128)(2,1)} %copy-done.19, bf16[64,2176]{1,0:T(8,128)(2,1)} %copy-done.20, bf16[256,1024]{1,0:T(8,128)(2,1)} %copy-done.8), custom_call_target="tpu_custom_call" | custom-call | tf_op jit(solution)/shard_map/pallas_call | solution.py:488
  113.6 6.7 %all-to-all-start.1 = ((bf16[8,8,2176]{2,1,0:T(8,128)(2,1)}), bf16[8,8,2176]{2,1,0:T(8,128)(2,1)S(1)}, u32[]{:S(2)}, u32[]{:S(2)}) async-start(bf16[8,8,2176]{2,1,0:T(8,128)(2,1)} %bitcast.10), calls=%async_computation.1 | async-start | bytes 557056 | tf_op jit(solution)/shard_map/all_to_all | solution.py:414
  120.3 0.8 copy-done.16
  121.1 0.2 copy-done.17
  121.2 2.7 %shard_map.89 = (f32[128,1024]{1,0:T(8,128)}, f32[128,1024]{1,0:T(8,128)}) custom-call(f32[256,1024]{1,0:T(8,128)} %get-tuple-element.33.own, bf16[256,1024]{1,0:T(8,128)(2,1)} %copy-done.8, bf16[256,1024]{1,0:T(8,128)(2,1)} %copy-done.16, bf16[256,1024]{1,0:T(8,128)(2,1)} %copy-done.17), custom_call_target="tpu_custom_call" | custom-call | tf_op jit(solution)/shard_map/pallas_call | solution.py:492
  124.0 7.4 %all-to-all-done.1 = bf16[8,8,2176]{2,1,0:T(8,128)(2,1)S(1)} async-done(((bf16[8,8,2176]{2,1,0:T(8,128)(2,1)}), bf16[8,8,2176]{2,1,0:T(8,128)(2,1)S(1)}, u32[]{:S(2)}, u32[]{:S(2)}) %all-to-all-start.1) | async-done | bytes 278560 | tf_op jit(solution)/shard_map/all_to_all | solution.py:414
  131.3 0.7 copy-done.10
  132.1 1.6 %shard_map.90 = (f32[8,1024]{1,0:T(8,128)}, f32[8,1024]{1,0:T(8,128)}, f32[6]{0:T(128)}) custom-call(bf16[64,2176]{1,0:T(8,128)(2,1)} %bitcast.11, f32[128,1024]{1,0:T(8,128)} %get-tuple-element.19.after), custom_call_target="tpu_custom_call" | custom-call | tf_op jit(solution)/shard_map/pallas_call | solution.py:493
  (46 shorter events, 0.1 us)
Async XLA Ops:
  2.6 39.6 %copy-start = (bf16[256,1024]{1,0:T(8,128)(2,1)}, bf16[256,1024]{1,0:T(8,128)(2,1)S(1)}, u32[]{:S(2)}) copy-start(bf16[256,1024]{1,0:T(8,128)(2,1)S(1)} %constant_dynamic-update-slice_fusion.q0.refs_0_) | copy-start | bytes 1572868
  2.6 26.2 %collective-permute-start.2 = (bf16[256,1024]{1,0:T(8,128)(2,1)S(1)}, bf16[256,1024]{1,0:T(8,128)(2,1)S(1)}, u32[]{:S(2)}, u32[]{:S(2)}) collective-permute-start(bf16[256,1024]{1,0:T(8,128)(2,1)S(1)} %constant_dynamic-update-slice_fusion.q0.refs_0_), channel_id=1, source_target_pairs={{0,6},{1,7},{2,0},{3,1},{4,2},{5,3},{6,4},{7,5},{8,14},{9,15},{10,... | collective-permute-start | bytes 1572872 | tf_op jit(solution)/shard_map/ppermute | solution.py:405
  7.4 18.3 %all-to-all-start = ((bf16[8,8,2048]{2,1,0:T(8,128)(2,1)}), bf16[8,8,2048]{2,1,0:T(8,128)(2,1)S(1)}, u32[]{:S(2)}, u32[]{:S(2)}) async-start(bf16[8,8,2048]{2,1,0:T(8,128)(2,1)} %tile.2), calls=%async_computation | async-start | bytes 524288 | tf_op jit(solution)/shard_map/all_to_all | solution.py:414
  15.6 13.9 %collective-permute-start.1 = (bf16[256,1024]{1,0:T(8,128)(2,1)S(1)}, bf16[256,1024]{1,0:T(8,128)(2,1)S(1)}, u32[]{:S(2)}, u32[]{:S(2)}) collective-permute-start(bf16[256,1024]{1,0:T(8,128)(2,1)S(1)} %constant_dynamic-update-slice_fusion.q0.refs_0_), channel_id=1, source_target_pairs={{0,4},{1,5},{2,6},{3,7},{4,0},{5,1},{6,2},{7,3},{8,12},{9,13},{10,... | collective-permute-start | bytes 1572872 | tf_op jit(solution)/shard_map/ppermute | solution.py:405
  16.1 26.1 %collective-permute-start = (bf16[256,1024]{1,0:T(8,128)(2,1)S(1)}, bf16[256,1024]{1,0:T(8,128)(2,1)S(1)}, u32[]{:S(2)}, u32[]{:S(2)}) collective-permute-start(bf16[256,1024]{1,0:T(8,128)(2,1)S(1)} %constant_dynamic-update-slice_fusion.q0.refs_0_), channel_id=1, source_target_pairs={{0,2},{1,3},{2,4},{3,5},{4,6},{5,7},{6,0},{7,1},{8,10},{9,11},{10,... | collective-permute-start | bytes 1572872 | tf_op jit(solution)/shard_map/ppermute | solution.py:405
  25.7 21.9 %copy-start.4 = (bf16[8,8,2048]{2,1,0:T(8,128)(2,1)}, bf16[8,8,2048]{2,1,0:T(8,128)(2,1)S(1)}, u32[]{:S(2)}) copy-start(bf16[8,8,2048]{2,1,0:T(8,128)(2,1)S(1)} %all-to-all-done) | copy-start | bytes 786436
  25.7 20.8 %collective-permute-start.5 = (bf16[64,2048]{1,0:T(8,128)(2,1)S(1)}, bf16[64,2048]{1,0:T(8,128)(2,1)S(1)}, u32[]{:S(2)}, u32[]{:S(2)}) collective-permute-start(bf16[64,2048]{1,0:T(8,128)(2,1)S(1)} %bitcast.3), channel_id=1, source_target_pairs={{0,192},{64,0},{128,64},{192,128},{1,193},{65,1},{129,65},{193,129... | collective-permute-start | bytes 786440 | tf_op jit(solution)/shard_map/ppermute | solution.py:410
  28.4 18.7 %collective-permute-start.4 = (bf16[64,2048]{1,0:T(8,128)(2,1)S(1)}, bf16[64,2048]{1,0:T(8,128)(2,1)S(1)}, u32[]{:S(2)}, u32[]{:S(2)}) collective-permute-start(bf16[64,2048]{1,0:T(8,128)(2,1)S(1)} %bitcast.4), channel_id=1, source_target_pairs={{0,128},{64,192},{128,0},{192,64},{1,129},{65,193},{129,1},{193,65... | collective-permute-start | bytes 786440 | tf_op jit(solution)/shard_map/ppermute | solution.py:410
  28.8 13.4 %copy-start.1 = (bf16[256,1024]{1,0:T(8,128)(2,1)}, bf16[256,1024]{1,0:T(8,128)(2,1)S(1)}, u32[]{:S(2)}) copy-start(bf16[256,1024]{1,0:T(8,128)(2,1)S(1)} %collective-permute-done.2.q3.refs_3_) | copy-start | bytes 1572868
  28.8 18.4 %collective-permute-start.3 = (bf16[64,2048]{1,0:T(8,128)(2,1)S(1)}, bf16[64,2048]{1,0:T(8,128)(2,1)S(1)}, u32[]{:S(2)}, u32[]{:S(2)}) collective-permute-start(bf16[64,2048]{1,0:T(8,128)(2,1)S(1)} %bitcast.5), channel_id=1, source_target_pairs={{0,64},{64,128},{128,192},{192,0},{1,65},{65,129},{129,193},{193,1... | collective-permute-start | bytes 786440 | tf_op jit(solution)/shard_map/ppermute | solution.py:410
  29.5 12.7 %copy-start.2 = (bf16[256,1024]{1,0:T(8,128)(2,1)}, bf16[256,1024]{1,0:T(8,128)(2,1)S(1)}, u32[]{:S(2)}) copy-start(bf16[256,1024]{1,0:T(8,128)(2,1)S(1)} %collective-permute-done.1.q2.refs_2_) | copy-start | bytes 1572868
  29.5 21.5 %collective-permute-start.6 = (bf16[64,2048]{1,0:T(8,128)(2,1)S(1)}, bf16[64,2048]{1,0:T(8,128)(2,1)S(1)}, u32[]{:S(2)}, u32[]{:S(2)}) collective-permute-start(bf16[64,2048]{1,0:T(8,128)(2,1)S(1)} %bitcast.6), channel_id=1, source_target_pairs={{0,1},{1,0},{2,3},{3,2},{4,5},{5,4},{6,7},{7,6},{8,9},{9,8},{10,11... | collective-permute-start | bytes 786440 | tf_op jit(solution)/shard_map/ppermute | solution.py:405
  42.2 0.8 copy-start.3
  46.5 1.1 copy-start.5
  46.5 4.5 %collective-permute-start.9 = (bf16[64,2048]{1,0:T(8,128)(2,1)S(1)}, bf16[64,2048]{1,0:T(8,128)(2,1)S(1)}, u32[]{:S(2)}, u32[]{:S(2)}) collective-permute-start(bf16[64,2048]{1,0:T(8,128)(2,1)S(1)} %collective-permute-done.5.b3.refs_7_), channel_id=1, source_target_pairs={{0,1},{1,0},{2,3},{3,2},{4,5},{5,4},{6,7},{7,6},{8,9},{9,8},{10,11... | collective-permute-start | bytes 786440 | tf_op jit(solution)/shard_map/ppermute | solution.py:405
  47.1 0.7 copy-start.6
  47.1 3.9 %collective-permute-start.8 = (bf16[64,2048]{1,0:T(8,128)(2,1)S(1)}, bf16[64,2048]{1,0:T(8,128)(2,1)S(1)}, u32[]{:S(2)}, u32[]{:S(2)}) collective-permute-start(bf16[64,2048]{1,0:T(8,128)(2,1)S(1)} %collective-permute-done.4.b2.refs_6_), channel_id=1, source_target_pairs={{0,1},{1,0},{2,3},{3,2},{4,5},{5,4},{6,7},{7,6},{8,9},{9,8},{10,11... | collective-permute-start | bytes 786440 | tf_op jit(solution)/shard_map/ppermute | solution.py:405
  47.2 0.7 copy-start.7
  47.2 3.8 %collective-permute-start.7 = (bf16[64,2048]{1,0:T(8,128)(2,1)S(1)}, bf16[64,2048]{1,0:T(8,128)(2,1)S(1)}, u32[]{:S(2)}, u32[]{:S(2)}) collective-permute-start(bf16[64,2048]{1,0:T(8,128)(2,1)S(1)} %collective-permute-done.3.b1.refs_5_), channel_id=1, source_target_pairs={{0,1},{1,0},{2,3},{3,2},{4,5},{5,4},{6,7},{7,6},{8,9},{9,8},{10,11... | collective-permute-start | bytes 786440 | tf_op jit(solution)/shard_map/ppermute | solution.py:405
  50.6 1.8 %collective-permute-start.10 = (f32[2,256,128]{2,1,0:T(8,128)}, f32[2,256,128]{2,1,0:T(8,128)S(1)}, u32[]{:S(2)}, u32[]{:S(2)}) collective-permute-start(f32[2,256,128]{2,1,0:T(8,128)} %shard_map.84.refs_14_), channel_id=1, source_target_pairs={{0,1},{1,0},{2,3},{3,2},{4,5},{5,4},{6,7},{7,6},{8,9},{9,8},{10,11... | collective-permute-start | bytes 786440 | tf_op jit(solution)/shard_map/ppermute | solution.py:405
  51.0 1.4 %copy-start.11 = (bf16[64,2048]{1,0:T(8,128)(2,1)}, bf16[64,2048]{1,0:T(8,128)(2,1)S(1)}, u32[]{:S(2)}) copy-start(bf16[64,2048]{1,0:T(8,128)(2,1)S(1)} %collective-permute-done.6.refs_8_) | copy-start | bytes 786436
  51.0 1.4 %copy-start.12 = (bf16[64,2048]{1,0:T(8,128)(2,1)}, bf16[64,2048]{1,0:T(8,128)(2,1)S(1)}, u32[]{:S(2)}) copy-start(bf16[64,2048]{1,0:T(8,128)(2,1)S(1)} %collective-permute-done.9.refs_11_) | copy-start | bytes 786436
  51.0 1.4 %copy-start.13 = (bf16[64,2048]{1,0:T(8,128)(2,1)}, bf16[64,2048]{1,0:T(8,128)(2,1)S(1)}, u32[]{:S(2)}) copy-start(bf16[64,2048]{1,0:T(8,128)(2,1)S(1)} %collective-permute-done.8.refs_10_) | copy-start | bytes 786436
  51.1 1.3 copy-start.14
  52.4 0.7 copy-start.15
  59.6 3.1 %collective-permute-start.13 = (f32[16,512]{1,0:T(8,128)}, f32[16,512]{1,0:T(8,128)S(1)}, u32[]{:S(2)}, u32[]{:S(2)}) collective-permute-start(f32[16,512]{1,0:T(8,128)} %shard_map.85.refs_16_), channel_id=1, source_target_pairs={{0,6},{1,7},{2,0},{3,1},{4,2},{5,3},{6,4},{7,5},{8,14},{9,15},{10,... | collective-permute-start | bytes 98312 | tf_op jit(solution)/shard_map/ppermute | solution.py:405
  60.0 4.5 %collective-permute-start.12 = (f32[16,512]{1,0:T(8,128)}, f32[16,512]{1,0:T(8,128)S(1)}, u32[]{:S(2)}, u32[]{:S(2)}) collective-permute-start(f32[16,512]{1,0:T(8,128)} %shard_map.85.refs_16_), channel_id=1, source_target_pairs={{0,4},{1,5},{2,6},{3,7},{4,0},{5,1},{6,2},{7,3},{8,12},{9,13},{10,... | collective-permute-start | bytes 98312 | tf_op jit(solution)/shard_map/ppermute | solution.py:405
  60.5 4.6 %collective-permute-start.11 = (f32[16,512]{1,0:T(8,128)}, f32[16,512]{1,0:T(8,128)S(1)}, u32[]{:S(2)}, u32[]{:S(2)}) collective-permute-start(f32[16,512]{1,0:T(8,128)} %shard_map.85.refs_16_), channel_id=1, source_target_pairs={{0,2},{1,3},{2,4},{3,5},{4,6},{5,7},{6,0},{7,1},{8,10},{9,11},{10,... | collective-permute-start | bytes 98312 | tf_op jit(solution)/shard_map/ppermute | solution.py:405
  62.7 2.4 %copy-start.21 = (f32[16,512]{1,0:T(8,128)}, f32[16,512]{1,0:T(8,128)S(1)}, u32[]{:S(2)}) copy-start(f32[16,512]{1,0:T(8,128)S(1)} %collective-permute-done.13.refs_19_) | copy-start | bytes 98308
  64.5 0.6 copy-start.22
  65.1 0.6 copy-start.23
  83.1 4.5 %collective-permute-start.14 = (bf16[272,2048]{1,0:T(8,128)(2,1)}, bf16[272,2048]{1,0:T(8,128)(2,1)S(1)}, u32[]{:S(2)}, u32[]{:S(2)}) collective-permute-start(bf16[272,2048]{1,0:T(8,128)(2,1)} %get-tuple-element.26), channel_id=1, source_target_pairs={{0,1},{1,0},{2,3},{3,2},{4,5},{5,4},{6,7},{7,6},{8,9},{9,8},{10,11... | collective-permute-start | bytes 3342344 | tf_op jit(solution)/shard_map/ppermute | solution.py:405
  85.0 13.7 %collective-permute-start.18 = (bf16[256,1024]{1,0:T(8,128)(2,1)}, bf16[256,1024]{1,0:T(8,128)(2,1)S(1)}, u32[]{:S(2)}, u32[]{:S(2)}) collective-permute-start(bf16[256,1024]{1,0:T(8,128)(2,1)} %get-tuple-element.32), channel_id=1, source_target_pairs={{0,6},{1,7},{2,0},{3,1},{4,2},{5,3},{6,4},{7,5},{8,14},{9,15},{10,... | collective-permute-start | bytes 1572872 | tf_op jit(solution)/shard_map/ppermute | solution.py:405
  87.6 1.0 copy-start.9
  88.6 7.0 %copy-start.25 = (bf16[256,1024]{1,0:T(8,128)(2,1)S(1)}, bf16[256,1024]{1,0:T(8,128)(2,1)}, u32[]{:S(2)}) copy-start(bf16[256,1024]{1,0:T(8,128)(2,1)} %get-tuple-element.34) | copy-start | bytes 1572868
  88.6 10.1 %copy-start.24 = (bf16[256,1024]{1,0:T(8,128)(2,1)S(1)}, bf16[256,1024]{1,0:T(8,128)(2,1)}, u32[]{:S(2)}) copy-start(bf16[256,1024]{1,0:T(8,128)(2,1)} %get-tuple-element.35) | copy-start | bytes 1572868
  91.8 14.5 %collective-permute-start.15 = (bf16[64,2176]{1,0:T(8,128)(2,1)}, bf16[64,2176]{1,0:T(8,128)(2,1)S(1)}, u32[]{:S(2)}, u32[]{:S(2)}) collective-permute-start(bf16[64,2176]{1,0:T(8,128)(2,1)} %get-tuple-element.29), channel_id=1, source_target_pairs={{0,192},{64,0},{128,64},{192,128},{1,193},{65,1},{129,65},{193,129... | collective-permute-start | bytes 835592 | tf_op jit(solution)/shard_map/ppermute | solution.py:410
  94.5 11.8 %collective-permute-start.16 = (bf16[64,2176]{1,0:T(8,128)(2,1)}, bf16[64,2176]{1,0:T(8,128)(2,1)S(1)}, u32[]{:S(2)}, u32[]{:S(2)}) collective-permute-start(bf16[64,2176]{1,0:T(8,128)(2,1)} %get-tuple-element.30), channel_id=1, source_target_pairs={{0,128},{64,192},{128,0},{192,64},{1,129},{65,193},{129,1},{193,65... | collective-permute-start | bytes 835592 | tf_op jit(solution)/shard_map/ppermute | solution.py:410
  94.9 15.9 %collective-permute-start.17 = (bf16[64,2176]{1,0:T(8,128)(2,1)}, bf16[64,2176]{1,0:T(8,128)(2,1)S(1)}, u32[]{:S(2)}, u32[]{:S(2)}) collective-permute-start(bf16[64,2176]{1,0:T(8,128)(2,1)} %get-tuple-element.31), channel_id=1, source_target_pairs={{0,64},{64,128},{128,192},{192,0},{1,65},{65,129},{129,193},{193,1... | collective-permute-start | bytes 835592 | tf_op jit(solution)/shard_map/ppermute | solution.py:410
  95.6 24.7 %collective-permute-start.19 = (bf16[256,1024]{1,0:T(8,128)(2,1)S(1)}, bf16[256,1024]{1,0:T(8,128)(2,1)S(1)}, u32[]{:S(2)}, u32[]{:S(2)}) collective-permute-start(bf16[256,1024]{1,0:T(8,128)(2,1)S(1)} %copy-done.25), channel_id=1, source_target_pairs={{0,4},{1,5},{2,6},{3,7},{4,0},{5,1},{6,2},{7,3},{8,12},{9,13},{10,... | collective-permute-start | bytes 1572872 | tf_op jit(solution)/shard_map/ppermute | solution.py:405
  98.7 12.1 %copy-start.8 = (bf16[256,1024]{1,0:T(8,128)(2,1)}, bf16[256,1024]{1,0:T(8,128)(2,1)S(1)}, u32[]{:S(2)}) copy-start(bf16[256,1024]{1,0:T(8,128)(2,1)S(1)} %collective-permute-done.18.rest_0_.r1) | copy-start | bytes 1572868
  98.7 21.6 %collective-permute-start.20 = (bf16[256,1024]{1,0:T(8,128)(2,1)S(1)}, bf16[256,1024]{1,0:T(8,128)(2,1)S(1)}, u32[]{:S(2)}, u32[]{:S(2)}) collective-permute-start(bf16[256,1024]{1,0:T(8,128)(2,1)S(1)} %copy-done.24), channel_id=1, source_target_pairs={{0,2},{1,3},{2,4},{3,5},{4,6},{5,7},{6,0},{7,1},{8,10},{9,11},{10,... | collective-permute-start | bytes 1572872 | tf_op jit(solution)/shard_map/ppermute | solution.py:405
  106.3 4.5 %copy-start.18 = (bf16[64,2176]{1,0:T(8,128)(2,1)}, bf16[64,2176]{1,0:T(8,128)(2,1)S(1)}, u32[]{:S(2)}) copy-start(bf16[64,2176]{1,0:T(8,128)(2,1)S(1)} %collective-permute-done.15.r1) | copy-start | bytes 835588
  106.3 4.5 %copy-start.19 = (bf16[64,2176]{1,0:T(8,128)(2,1)}, bf16[64,2176]{1,0:T(8,128)(2,1)S(1)}, u32[]{:S(2)}) copy-start(bf16[64,2176]{1,0:T(8,128)(2,1)S(1)} %collective-permute-done.16.r2) | copy-start | bytes 835588
  110.8 0.7 copy-start.20
  113.6 17.7 %all-to-all-start.1 = ((bf16[8,8,2176]{2,1,0:T(8,128)(2,1)}), bf16[8,8,2176]{2,1,0:T(8,128)(2,1)S(1)}, u32[]{:S(2)}, u32[]{:S(2)}) async-start(bf16[8,8,2176]{2,1,0:T(8,128)(2,1)} %bitcast.10), calls=%async_computation.1 | async-start | bytes 557056 | tf_op jit(solution)/shard_map/all_to_all | solution.py:414
  120.3 0.8 copy-start.16
  120.3 0.9 copy-start.17
  131.3 0.7 copy-start.10

commit v3 on v2

--- a/solution.py
+++ b/solution.py
@@ -93,11 +93,11 @@
     return jnp.broadcast_to(cols[:, level : level + 1], (cols.shape[0], LANES))
 
 
-def prepare(q0, q1, q2, q3, rq, matched):
+def prepare(q0, q1, q2a, q2b, q3, rq, matched):
     across = level_mask((16, D), 0)
     for side in range(2):
         rows = slice(side * ROWS, (side + 1) * ROWS)
-        for s, block in enumerate((q0[rows, :], q1[rows, :], q2[rows, :], q3[rows, :])):
+        for s, block in enumerate((q0[rows, :], q1[rows, :], (q2a, q2b)[side][...], q3[rows, :])):
             wide = block.astype(F32)
             found = lax.rsqrt(sums_across(wide * wide, across) + EPS)
             rq[side, :, s * ROWS : (s + 1) * ROWS] = found[:8]
@@ -114,7 +114,7 @@
 
 
 def fetch(blocks, xs, ks, sems):
-    q0, q1, q2, q3 = blocks[:4]
+    q0, q1, q2a, q2b, q3 = blocks[:5]
     count = 0
 
     def start(source, target):
@@ -126,11 +126,11 @@
 
     def queries(side):
         rows = slice(side * ROWS, (side + 1) * ROWS)
-        parts = (q0.at[rows, :], q1.at[rows, :], q2.at[rows, :], q3.at[rows, :])
+        parts = (q0.at[rows, :], q1.at[rows, :], (q2a, q2b)[side], q3.at[rows, :])
         return [start(p, xs.at[side, s * ROWS : (s + 1) * ROWS, :]) for s, p in enumerate(parts)]
 
     def keys(part):
-        found = blocks[4 + 4 * part : 8 + 4 * part]
+        found = blocks[5 + 4 * part : 9 + 4 * part]
         return [start(b, ks.at[part * KEYS + s * NEAR : part * KEYS + (s + 1) * NEAR, :]) for s, b in enumerate(found)]
 
     first = queries(0)
@@ -143,9 +143,9 @@
 
 
 def forward(*refs):
-    rq, matched, n0, n1 = refs[12:16]
-    sums, xs, ks, dots, wide, sems = refs[16:]
-    near_queries, near_keys, far_keys, other_queries = fetch(refs[:12], xs, ks, sems)
+    rq, matched, n0, n1 = refs[13:17]
+    sums, xs, ks, dots, wide, sems = refs[17:]
+    near_queries, near_keys, far_keys, other_queries = fetch(refs[:13], xs, ks, sems)
     grown = jnp.exp(matched[...])
     total = jnp.broadcast_to(jnp.sum(matched[...], axis=1, keepdims=True), (8, ROWS))
     spare = [jnp.concatenate([total[r : r + 1] for r in rows], axis=1) for rows in ((0, 1, 2, 3), (4, 5, 5, 5))]
@@ -220,10 +220,10 @@
 
 
 def backward(*refs):
-    rq, matched, n0, n1, s0, s1, s2, s3 = refs[12:20]
-    outs, loss = refs[20:26], refs[26]
-    xs, ks, gq0, gq1, gq2, gq3, gown, gother, dots, wide, ws, ea, acc_q, sems, out_sems = refs[27:]
-    near_queries, near_keys, far_keys, other_queries = fetch(refs[:12], xs, ks, sems)
+    rq, matched, n0, n1, s0, s1, s2, s3 = refs[13:21]
+    outs, loss = refs[21:27], refs[27]
+    xs, ks, gq0, gq1, gq2, gq3, gown, gother, dots, wide, ws, ea, acc_q, sems, out_sems = refs[28:]
+    near_queries, near_keys, far_keys, other_queries = fetch(refs[:13], xs, ks, sems)
     leaving = []
 
     def leave(n, rows, cols):
@@ -431,7 +431,8 @@
 
 def on_device(image, text, image_bank, text_bank):
     query = jnp.concatenate([image, text], axis=0)
-    queries = [query] + [move(query, s) for s in (1, 2, 3)]
+    up, down = move(query, 1), move(query, -1)
+    queries = [query, up, move(up[:ROWS], 1), move(down[ROWS:], -1), down]
     bank = jnp.concatenate([image_bank, text_bank], axis=1)
     near = exchange(jnp.tile(bank, (PAIRS, 1)))
     around = [near] + [along_y(near, s) for s in (1, 2, 3)]
@@ -448,7 +449,7 @@
 
     (sums,) = placed(
         forward,
-        [ANYWHERE] * 12 + [INSIDE] * 4,
+        [ANYWHERE] * 13 + [INSIDE] * 4,
         [INSIDE],
         [shaped((16, CHUNK))],
         held + scores + [pltpu.SemaphoreType.DMA((16,))],
@@ -464,7 +465,7 @@
     ]
     gq0, gq1, gq2, gq3, gown, gother, loss = placed(
         backward,
-        [ANYWHERE] * 12 + [INSIDE] * 8,
+        [ANYWHERE] * 13 + [INSIDE] * 8,
         [ANYWHERE] * 6 + [INSIDE],
         grads + [shaped((8, LANES))],
         held

time: 135 us -> 133 us (0.985)
  blocking collectives: 0 us -> 18.1 us
  starting transfers between devices: 39.6 us -> 29.5 us
  waiting for transfers between devices: 44.3 us -> 34.7 us
    all_to_all x0 -> x1, blocking collectives: none -> 18.1 us  [exchange(): return lax.all_to_all(value, 'z', 0, 0, tiled=True)]
    all_to_all x2 -> x1, waiting for transfers between devices: 16.3 us -> 3.78 us  [exchange(): return lax.all_to_all(value, 'z', 0, 0, tiled=True)]
    all_to_all x2 -> x1, starting transfers between devices: 14.8 us -> 3.42 us  [exchange(): return lax.all_to_all(value, 'z', 0, 0, tiled=True)]
    ppermute x15 -> x16, starting transfers between devices: 17.2 us -> 20.8 us  [move(): return lax.ppermute(value, ('x', 'c'), pairs)]
    ppermute x6, waiting for transfers between devices: 10.9 us -> 13.4 us  [along_y(): return lax.ppermute(value, 'y', [(i, (i + step) % n) for i in range(n)])]
    ppermute x6, starting transfers between devices: 7.55 us -> 5.24 us  [along_y(): return lax.ppermute(value, 'y', [(i, (i + step) % n) for i in range(n)])]
    unnamed x53 -> x55, local copies, waits for them, and re-layouts: 6.75 us -> 7.38 us
    ppermute x15 -> x16, waiting for transfers between devices: 17 us -> 17.6 us  [move(): return lax.ppermute(value, ('x', 'c'), pairs)]
  transfers between devices with their start and end apart: 23 -> 23, of which waited for: 11 -> 12; matrix products, arithmetic and copies ran while one was open for 1% -> 1% of each run, Pallas kernels for 11% -> 11%
where the time goes in v3:
time: 133 us; the launch traced here: 132 us
  Pallas kernels  39.8 us (30%)
  waiting for transfers between devices  34.7 us (26%)
  starting transfers between devices  29.5 us (22%)
  blocking collectives  18.1 us (14%)
  local copies, waits for them, and re-layouts  8.41 us (6%)
    ppermute x16, starting transfers between devices, move(): return lax.ppermute(value, ('x', 'c'), pairs)  20.8 us
    all_to_all x1, blocking collectives, exchange(): return lax.all_to_all(value, 'z', 0, 0, tiled=True)  18.1 us
    ppermute x16, waiting for transfers between devices, move(): return lax.ppermute(value, ('x', 'c'), pairs)  17.6 us
    pallas_call x1, Pallas kernels, on_device(): placed(backward, [ANYWHERE] * 13 + [INSIDE] * 8, [ANYWHERE] * 6 + [INSIDE...  17.4 us
    ppermute x6, waiting for transfers between devices, along_y(): return lax.ppermute(value, 'y', [(i, (i + step) % n) for i in range(n)])  13.4 us
    unnamed x55, local copies, waits for them, and re-layouts  7.38 us
    pallas_call x1, Pallas kernels, on_device(): placed(forward, [ANYWHERE] * 13 + [INSIDE] * 4, [INSIDE], [shaped((16, CH...  6.51 us
    ppermute x6, starting transfers between devices, along_y(): return lax.ppermute(value, 'y', [(i, (i + step) % n) for i in range(n)])  5.24 us
  transfers between devices with their start and end apart: 23, of which 12 were waited for; matrix products, arithmetic and copies ran while one was open for 1% of the time, Pallas kernels for 11%

profile of v3, /device:TPU:1, one launch (start us, length us, event | category | flops | bytes accessed | tf_op | source)
XLA Modules:
  0.0 132.2 jit_solution(7924204331031761029)
XLA Ops:
  0.6 1.0 constant_dynamic-update-slice_fusion.1
  1.6 1.0 constant_dynamic-update-slice_fusion.q0.refs_0_
  2.6 0.0 copy-start.2
  2.6 3.4 %collective-permute-start.2 = (bf16[256,1024]{1,0:T(8,128)(2,1)S(1)}, bf16[256,1024]{1,0:T(8,128)(2,1)S(1)}, u32[]{:S(2)}, u32[]{:S(2)}) collective-permute-start(bf16[256,1024]{1,0:T(8,128)(2,1)S(1)} %constant_dynamic-update-slice_fusion.q0.refs_0_), channel_id=1, source_target_pairs={{0,6},{1,7},{2,0},{3,1},{4,2},{5,3},{6,4},{7,5},{8,14},{9,15},{10,... | collective-permute-start | bytes 1572872 | tf_op jit(solution)/shard_map/ppermute | solution.py:405
  6.0 0.0 collective-permute-start
  6.0 0.7 pad_maximum_fusion
  6.7 18.1 %all_to_all.19 = bf16[8,8,2048]{2,1,0:T(8,128)(2,1)S(1)} all-to-all(bf16[8,8,2048]{2,1,0:T(8,128)(2,1)S(1)} %tile.2), channel_id=1, replica_groups=mesh['y'=4,'z'=8,'x'=4,'c'=2] {'z'}, dimensions={0} | all-to-all | bytes 524288 | tf_op jit(solution)/shard_map/all_to_all | solution.py:414
  24.8 2.7 %collective-permute-start.6 = (bf16[64,2048]{1,0:T(8,128)(2,1)S(1)}, bf16[64,2048]{1,0:T(8,128)(2,1)S(1)}, u32[]{:S(2)}, u32[]{:S(2)}) collective-permute-start(bf16[64,2048]{1,0:T(8,128)(2,1)S(1)} %bitcast.3), channel_id=1, source_target_pairs={{0,192},{64,0},{128,64},{192,128},{1,193},{65,1},{129,65},{193,129... | collective-permute-start | bytes 786440 | tf_op jit(solution)/shard_map/ppermute | solution.py:410
  27.5 0.3 collective-permute-start.5
  27.9 0.7 collective-permute-start.4
  28.6 0.0 collective-permute-done.2.q3.refs_4_
  28.6 2.8 %collective-permute-start.3 = (bf16[128,1024]{1,0:T(8,128)(2,1)S(1)}, bf16[128,1024]{1,0:T(8,128)(2,1)S(1)}, u32[]{:S(2)}, u32[]{:S(2)}) collective-permute-start(bf16[128,1024]{1,0:T(8,128)(2,1)S(1)} %slice.9), channel_id=1, source_target_pairs={{0,6},{1,7},{2,0},{3,1},{4,2},{5,3},{6,4},{7,5},{8,14},{9,15},{10,... | collective-permute-start | bytes 786440 | tf_op jit(solution)/shard_map/ppermute | solution.py:405
  31.4 0.0 collective-permute-done.q1.refs_1_
  31.4 0.1 collective-permute-start.1
  31.5 2.3 %collective-permute-done.6.b3.refs_8_ = bf16[64,2048]{1,0:T(8,128)(2,1)S(1)} collective-permute-done((bf16[64,2048]{1,0:T(8,128)(2,1)S(1)}, bf16[64,2048]{1,0:T(8,128)(2,1)S(1)}, u32[]{:S(2)}, u32[]{:S(2)}) %collective-permute-start.6) | collective-permute-done | bytes 262176 | tf_op jit(solution)/shard_map/ppermute | solution.py:410
  33.9 5.8 %collective-permute-start.7 = (bf16[64,2048]{1,0:T(8,128)(2,1)S(1)}, bf16[64,2048]{1,0:T(8,128)(2,1)S(1)}, u32[]{:S(2)}, u32[]{:S(2)}) collective-permute-start(bf16[64,2048]{1,0:T(8,128)(2,1)S(1)} %bitcast.6), channel_id=1, source_target_pairs={{0,1},{1,0},{2,3},{3,2},{4,5},{5,4},{6,7},{7,6},{8,9},{9,8},{10,11... | collective-permute-start | bytes 786440 | tf_op jit(solution)/shard_map/ppermute | solution.py:405
  39.7 0.0 collective-permute-done.5.b2.refs_7_
  39.7 1.0 collective-permute-start.10
  40.7 1.4 %collective-permute-done.4.b1.refs_6_ = bf16[64,2048]{1,0:T(8,128)(2,1)S(1)} collective-permute-done((bf16[64,2048]{1,0:T(8,128)(2,1)S(1)}, bf16[64,2048]{1,0:T(8,128)(2,1)S(1)}, u32[]{:S(2)}, u32[]{:S(2)}) %collective-permute-start.4) | collective-permute-done | bytes 262176 | tf_op jit(solution)/shard_map/ppermute | solution.py:410
  42.1 1.3 %collective-permute-start.9 = (bf16[64,2048]{1,0:T(8,128)(2,1)S(1)}, bf16[64,2048]{1,0:T(8,128)(2,1)S(1)}, u32[]{:S(2)}, u32[]{:S(2)}) collective-permute-start(bf16[64,2048]{1,0:T(8,128)(2,1)S(1)} %collective-permute-done.5.b2.refs_7_), channel_id=1, source_target_pairs={{0,1},{1,0},{2,3},{3,2},{4,5},{5,4},{6,7},{7,6},{8,9},{9,8},{10,11... | collective-permute-start | bytes 786440 | tf_op jit(solution)/shard_map/ppermute | solution.py:405
  43.4 0.0 collective-permute-done.3.q2b.refs_3_
  43.4 0.1 collective-permute-start.8
  43.5 0.6 copy-done.7
  44.1 0.7 copy-done.8
  44.8 3.5 %shard_map.83 = (f32[2,8,512]{2,1,0:T(8,128)}, f32[8,128]{1,0:T(8,128)}) custom-call(bf16[256,1024]{1,0:T(8,128)(2,1)} %copy-done.2, bf16[256,1024]{1,0:T(8,128)(2,1)} %copy-done.1, bf16[128,1024]{1,0:T(8,128)(2,1)} %copy-done.8, bf16[128,1024]{1,0:T(8,128)(2,1)} %copy-done.7, bf16[256,1024]{1,0:T(8,128)(2,1)} %copy-done), custom_call_target="tpu_custom_call" | custom-call | tf_op jit(solution)/shard_map/pallas_call | solution.py:439
  48.3 2.7 %shard_map.84.refs_15_ = f32[2,256,128]{2,1,0:T(8,128)} custom-call(bf16[64,2048]{1,0:T(8,128)(2,1)} %bitcast.7, bf16[64,2048]{1,0:T(8,128)(2,1)} %copy-done.6, bf16[64,2048]{1,0:T(8,128)(2,1)} %copy-done.5, bf16[64,2048]{1,0:T(8,128)(2,1)} %copy-done.4, f32[8,128]{1,0:T(8,128)} %get-tuple-element.24.after.refs_14_), custom_call_target="tpu_custom_call" | custom-call | tf_op jit(solution)/shard_map/pallas_call | solution.py:440
  51.0 0.1 collective-permute-start.11
  51.1 0.0 collective-permute-done.10.refs_12_
  51.1 0.0 collective-permute-done.9.refs_11_
  51.1 1.6 %collective-permute-done.11.refs_16_ = f32[2,256,128]{2,1,0:T(8,128)S(1)} collective-permute-done((f32[2,256,128]{2,1,0:T(8,128)}, f32[2,256,128]{2,1,0:T(8,128)S(1)}, u32[]{:S(2)}, u32[]{:S(2)}) %collective-permute-start.11) | collective-permute-done | bytes 262176 | tf_op jit(solution)/shard_map/ppermute | solution.py:405
  52.8 0.7 copy-done.16
  53.4 6.5 %shard_map.85.refs_17_ = f32[16,512]{1,0:T(8,128)} custom-call(bf16[256,1024]{1,0:T(8,128)(2,1)} %copy-done.2, bf16[256,1024]{1,0:T(8,128)(2,1)} %copy-done.1, bf16[128,1024]{1,0:T(8,128)(2,1)} %copy-done.8, bf16[128,1024]{1,0:T(8,128)(2,1)} %copy-done.7, bf16[256,1024]{1,0:T(8,128)(2,1)} %copy-done, bf16[64,2048]{1,0:T(8,128)(2,1)} %bitcast.8, ...), custom_call_target="tpu_custom_call" | custom-call | tf_op jit(solution)/shard_map/pallas_call | solution.py:450
  60.0 2.8 %collective-permute-start.14 = (f32[16,512]{1,0:T(8,128)}, f32[16,512]{1,0:T(8,128)S(1)}, u32[]{:S(2)}, u32[]{:S(2)}) collective-permute-start(f32[16,512]{1,0:T(8,128)} %shard_map.85.refs_17_), channel_id=1, source_target_pairs={{0,6},{1,7},{2,0},{3,1},{4,2},{5,3},{6,4},{7,5},{8,14},{9,15},{10,... | collective-permute-start | bytes 98312 | tf_op jit(solution)/shard_map/ppermute | solution.py:405
  62.8 0.0 collective-permute-start.13
  62.8 0.7 collective-permute-start.12
  63.4 0.7 collective-permute-done.14.refs_20_
  64.1 3.2 %collective-permute-done.13.refs_19_ = f32[16,512]{1,0:T(8,128)S(1)} collective-permute-done((f32[16,512]{1,0:T(8,128)}, f32[16,512]{1,0:T(8,128)S(1)}, u32[]{:S(2)}, u32[]{:S(2)}) %collective-permute-start.13) | collective-permute-done | bytes 32800 | tf_op jit(solution)/shard_map/ppermute | solution.py:405
  67.3 0.6 copy-done.23
  67.9 0.6 copy-done.24
  68.5 17.4 %shard_map.86 = (f32[256,1024]{1,0:T(8,128)}, bf16[256,1024]{1,0:T(8,128)(2,1)}, bf16[256,1024]{1,0:T(8,128)(2,1)}, bf16[256,1024]{1,0:T(8,128)(2,1)}, f32[256,2...) custom-call(bf16[256,1024]{1,0:T(8,128)(2,1)} %copy-done.2, bf16[256,1024]{1,0:T(8,128)(2,1)} %copy-done.1, ...), custom_call_target="tpu_custom_call" | custom-call | tf_op jit(solution)/shard_map/pallas_call | solution.py:466
  85.9 1.6 %collective-permute-start.15 = (bf16[272,2048]{1,0:T(8,128)(2,1)}, bf16[272,2048]{1,0:T(8,128)(2,1)S(1)}, u32[]{:S(2)}, u32[]{:S(2)}) collective-permute-start(bf16[272,2048]{1,0:T(8,128)(2,1)} %get-tuple-element.26), channel_id=1, source_target_pairs={{0,1},{1,0},{2,3},{3,2},{4,5},{5,4},{6,7},{7,6},{8,9},{9,8},{10,11... | collective-permute-start | bytes 3342344 | tf_op jit(solution)/shard_map/ppermute | solution.py:405
  87.6 0.0 collective-permute-start.19
  87.6 2.6 %collective-permute-done.15.other = bf16[272,2048]{1,0:T(8,128)(2,1)S(1)} collective-permute-done((bf16[272,2048]{1,0:T(8,128)(2,1)}, bf16[272,2048]{1,0:T(8,128)(2,1)S(1)}, u32[]{:S(2)}, u32[]{:S(2)}) %collective-permute-start.15) | collective-permute-done | bytes 1114144 | tf_op jit(solution)/shard_map/ppermute | solution.py:405
  90.2 1.0 copy-done.10
  91.2 3.2 %shard_map.87 = (f32[64,2176]{1,0:T(8,128)}, bf16[64,2176]{1,0:T(8,128)(2,1)}, bf16[64,2176]{1,0:T(8,128)(2,1)}, bf16[64,2176]{1,0:T(8,128)(2,1)}) custom-call(f32[256,2048]{1,0:T(8,128)} %get-tuple-element.25.own, bf16[272,2048]{1,0:T(8,128)(2,1)} %copy-done.10, f32[8,128]{1,0:T(8,128)} %get-tuple-element.27.loss), custom_call_target="tpu_custom_call" | custom-call | tf_op jit(solution)/shard_map/pallas_call | solution.py:484
  94.4 0.3 collective-permute-start.16
  94.7 0.4 collective-permute-start.17
  95.0 0.8 collective-permute-start.18
  95.8 1.1 collective-permute-start.20
  96.9 4.3 %collective-permute-done.19.rest_0_.r1 = bf16[256,1024]{1,0:T(8,128)(2,1)S(1)} collective-permute-done((bf16[256,1024]{1,0:T(8,128)(2,1)}, bf16[256,1024]{1,0:T(8,128)(2,1)S(1)}, u32[]{:S(2)}, u32[]{:S(2)}) %collective-permute-start.19) | collective-permute-done | bytes 524320 | tf_op jit(solution)/shard_map/ppermute | solution.py:405
  101.3 0.0 collective-permute-start.21
  101.3 1.2 collective-permute-done.16.r1
  102.4 1.5 %collective-permute-done.17.r2 = bf16[64,2176]{1,0:T(8,128)(2,1)S(1)} collective-permute-done((bf16[64,2176]{1,0:T(8,128)(2,1)}, bf16[64,2176]{1,0:T(8,128)(2,1)S(1)}, u32[]{:S(2)}, u32[]{:S(2)}) %collective-permute-start.17) | collective-permute-done | bytes 278560 | tf_op jit(solution)/shard_map/ppermute | solution.py:410
  104.0 7.0 %collective-permute-done.18.r3 = bf16[64,2176]{1,0:T(8,128)(2,1)S(1)} collective-permute-done((bf16[64,2176]{1,0:T(8,128)(2,1)}, bf16[64,2176]{1,0:T(8,128)(2,1)S(1)}, u32[]{:S(2)}, u32[]{:S(2)}) %collective-permute-start.18) | collective-permute-done | bytes 278560 | tf_op jit(solution)/shard_map/ppermute | solution.py:410
  111.0 0.7 copy-done.21
  111.6 2.1 %shard_map.88 = bf16[64,2176]{1,0:T(8,128)(2,1)} custom-call(f32[64,2176]{1,0:T(8,128)} %get-tuple-element.28.own, bf16[64,2176]{1,0:T(8,128)(2,1)} %copy-done.19, bf16[64,2176]{1,0:T(8,128)(2,1)} %copy-done.20, bf16[64,2176]{1,0:T(8,128)(2,1)} %copy-done.21, bf16[256,1024]{1,0:T(8,128)(2,1)} %copy-done.9), custom_call_target="tpu_custom_call" | custom-call | tf_op jit(solution)/shard_map/pallas_call | solution.py:489
  113.8 3.4 %all-to-all-start.1 = ((bf16[8,8,2176]{2,1,0:T(8,128)(2,1)}), bf16[8,8,2176]{2,1,0:T(8,128)(2,1)S(1)}, u32[]{:S(2)}, u32[]{:S(2)}) async-start(bf16[8,8,2176]{2,1,0:T(8,128)(2,1)} %bitcast.10), calls=%async_computation.1 | async-start | bytes 557056 | tf_op jit(solution)/shard_map/all_to_all | solution.py:414
  117.2 0.0 collective-permute-done.20.r2
  117.2 5.2 %collective-permute-done.21.r3 = bf16[256,1024]{1,0:T(8,128)(2,1)S(1)} collective-permute-done((bf16[256,1024]{1,0:T(8,128)(2,1)S(1)}, bf16[256,1024]{1,0:T(8,128)(2,1)S(1)}, u32[]{:S(2)}, u32[]{:S(2)}) %collective-permute-start.21) | collective-permute-done | bytes 524320 | tf_op jit(solution)/shard_map/ppermute | solution.py:405
  122.4 0.8 copy-done.18
  123.2 2.7 %shard_map.89 = (f32[128,1024]{1,0:T(8,128)}, f32[128,1024]{1,0:T(8,128)}) custom-call(f32[256,1024]{1,0:T(8,128)} %get-tuple-element.33.own, bf16[256,1024]{1,0:T(8,128)(2,1)} %copy-done.9, bf16[256,1024]{1,0:T(8,128)(2,1)} %copy-done.17, bf16[256,1024]{1,0:T(8,128)(2,1)} %copy-done.18), custom_call_target="tpu_custom_call" | custom-call | tf_op jit(solution)/shard_map/pallas_call | solution.py:493
  126.0 3.8 %all-to-all-done.1 = bf16[8,8,2176]{2,1,0:T(8,128)(2,1)S(1)} async-done(((bf16[8,8,2176]{2,1,0:T(8,128)(2,1)}), bf16[8,8,2176]{2,1,0:T(8,128)(2,1)S(1)}, u32[]{:S(2)}, u32[]{:S(2)}) %all-to-all-start.1) | async-done | bytes 278560 | tf_op jit(solution)/shard_map/all_to_all | solution.py:414
  129.7 0.7 copy-done.11
  130.4 1.6 %shard_map.90 = (f32[8,1024]{1,0:T(8,128)}, f32[8,1024]{1,0:T(8,128)}, f32[6]{0:T(128)}) custom-call(bf16[64,2176]{1,0:T(8,128)(2,1)} %bitcast.11, f32[128,1024]{1,0:T(8,128)} %get-tuple-element.19.after), custom_call_target="tpu_custom_call" | custom-call | tf_op jit(solution)/shard_map/pallas_call | solution.py:494
  (51 shorter events, 0.1 us)
Async XLA Ops:
  2.6 40.9 %copy-start.2 = (bf16[256,1024]{1,0:T(8,128)(2,1)}, bf16[256,1024]{1,0:T(8,128)(2,1)S(1)}, u32[]{:S(2)}) copy-start(bf16[256,1024]{1,0:T(8,128)(2,1)S(1)} %constant_dynamic-update-slice_fusion.q0.refs_0_) | copy-start | bytes 1572868
  2.6 26.0 %collective-permute-start.2 = (bf16[256,1024]{1,0:T(8,128)(2,1)S(1)}, bf16[256,1024]{1,0:T(8,128)(2,1)S(1)}, u32[]{:S(2)}, u32[]{:S(2)}) collective-permute-start(bf16[256,1024]{1,0:T(8,128)(2,1)S(1)} %constant_dynamic-update-slice_fusion.q0.refs_0_), channel_id=1, source_target_pairs={{0,6},{1,7},{2,0},{3,1},{4,2},{5,3},{6,4},{7,5},{8,14},{9,15},{10,... | collective-permute-start | bytes 1572872 | tf_op jit(solution)/shard_map/ppermute | solution.py:405
  6.0 25.4 %collective-permute-start = (bf16[256,1024]{1,0:T(8,128)(2,1)S(1)}, bf16[256,1024]{1,0:T(8,128)(2,1)S(1)}, u32[]{:S(2)}, u32[]{:S(2)}) collective-permute-start(bf16[256,1024]{1,0:T(8,128)(2,1)S(1)} %constant_dynamic-update-slice_fusion.q0.refs_0_), channel_id=1, source_target_pairs={{0,2},{1,3},{2,4},{3,5},{4,6},{5,7},{6,0},{7,1},{8,10},{9,11},{10,... | collective-permute-start | bytes 1572872 | tf_op jit(solution)/shard_map/ppermute | solution.py:405
  24.8 23.5 %copy-start.3 = (bf16[8,8,2048]{2,1,0:T(8,128)(2,1)}, bf16[8,8,2048]{2,1,0:T(8,128)(2,1)S(1)}, u32[]{:S(2)}) copy-start(bf16[8,8,2048]{2,1,0:T(8,128)(2,1)S(1)} %all_to_all.19) | copy-start | bytes 786436
  24.8 9.0 %collective-permute-start.6 = (bf16[64,2048]{1,0:T(8,128)(2,1)S(1)}, bf16[64,2048]{1,0:T(8,128)(2,1)S(1)}, u32[]{:S(2)}, u32[]{:S(2)}) collective-permute-start(bf16[64,2048]{1,0:T(8,128)(2,1)S(1)} %bitcast.3), channel_id=1, source_target_pairs={{0,192},{64,0},{128,64},{192,128},{1,193},{65,1},{129,65},{193,129... | collective-permute-start | bytes 786440 | tf_op jit(solution)/shard_map/ppermute | solution.py:410
  27.5 12.1 %collective-permute-start.5 = (bf16[64,2048]{1,0:T(8,128)(2,1)S(1)}, bf16[64,2048]{1,0:T(8,128)(2,1)S(1)}, u32[]{:S(2)}, u32[]{:S(2)}) collective-permute-start(bf16[64,2048]{1,0:T(8,128)(2,1)S(1)} %bitcast.4), channel_id=1, source_target_pairs={{0,128},{64,192},{128,0},{192,64},{1,129},{65,193},{129,1},{193,65... | collective-permute-start | bytes 786440 | tf_op jit(solution)/shard_map/ppermute | solution.py:410
  27.9 14.2 %collective-permute-start.4 = (bf16[64,2048]{1,0:T(8,128)(2,1)S(1)}, bf16[64,2048]{1,0:T(8,128)(2,1)S(1)}, u32[]{:S(2)}, u32[]{:S(2)}) collective-permute-start(bf16[64,2048]{1,0:T(8,128)(2,1)S(1)} %bitcast.5), channel_id=1, source_target_pairs={{0,64},{64,128},{128,192},{192,0},{1,65},{65,129},{129,193},{193,1... | collective-permute-start | bytes 786440 | tf_op jit(solution)/shard_map/ppermute | solution.py:410
  28.6 14.9 %copy-start = (bf16[256,1024]{1,0:T(8,128)(2,1)}, bf16[256,1024]{1,0:T(8,128)(2,1)S(1)}, u32[]{:S(2)}) copy-start(bf16[256,1024]{1,0:T(8,128)(2,1)S(1)} %collective-permute-done.2.q3.refs_4_) | copy-start | bytes 1572868
  28.6 14.8 %collective-permute-start.3 = (bf16[128,1024]{1,0:T(8,128)(2,1)S(1)}, bf16[128,1024]{1,0:T(8,128)(2,1)S(1)}, u32[]{:S(2)}, u32[]{:S(2)}) collective-permute-start(bf16[128,1024]{1,0:T(8,128)(2,1)S(1)} %slice.9), channel_id=1, source_target_pairs={{0,6},{1,7},{2,0},{3,1},{4,2},{5,3},{6,4},{7,5},{8,14},{9,15},{10,... | collective-permute-start | bytes 786440 | tf_op jit(solution)/shard_map/ppermute | solution.py:405
  31.4 12.1 %copy-start.1 = (bf16[256,1024]{1,0:T(8,128)(2,1)}, bf16[256,1024]{1,0:T(8,128)(2,1)S(1)}, u32[]{:S(2)}) copy-start(bf16[256,1024]{1,0:T(8,128)(2,1)S(1)} %collective-permute-done.q1.refs_1_) | copy-start | bytes 1572868
  31.4 12.1 %collective-permute-start.1 = (bf16[128,1024]{1,0:T(8,128)(2,1)S(1)}, bf16[128,1024]{1,0:T(8,128)(2,1)S(1)}, u32[]{:S(2)}, u32[]{:S(2)}) collective-permute-start(bf16[128,1024]{1,0:T(8,128)(2,1)S(1)} %slice.8), channel_id=1, source_target_pairs={{0,2},{1,3},{2,4},{3,5},{4,6},{5,7},{6,0},{7,1},{8,10},{9,11},{10,... | collective-permute-start | bytes 786440 | tf_op jit(solution)/shard_map/ppermute | solution.py:405
  33.9 14.4 %copy-start.4 = (bf16[64,2048]{1,0:T(8,128)(2,1)}, bf16[64,2048]{1,0:T(8,128)(2,1)S(1)}, u32[]{:S(2)}) copy-start(bf16[64,2048]{1,0:T(8,128)(2,1)S(1)} %collective-permute-done.6.b3.refs_8_) | copy-start | bytes 786436
  33.9 17.2 %collective-permute-start.7 = (bf16[64,2048]{1,0:T(8,128)(2,1)S(1)}, bf16[64,2048]{1,0:T(8,128)(2,1)S(1)}, u32[]{:S(2)}, u32[]{:S(2)}) collective-permute-start(bf16[64,2048]{1,0:T(8,128)(2,1)S(1)} %bitcast.6), channel_id=1, source_target_pairs={{0,1},{1,0},{2,3},{3,2},{4,5},{5,4},{6,7},{7,6},{8,9},{9,8},{10,11... | collective-permute-start | bytes 786440 | tf_op jit(solution)/shard_map/ppermute | solution.py:405
  39.7 8.6 %copy-start.5 = (bf16[64,2048]{1,0:T(8,128)(2,1)}, bf16[64,2048]{1,0:T(8,128)(2,1)S(1)}, u32[]{:S(2)}) copy-start(bf16[64,2048]{1,0:T(8,128)(2,1)S(1)} %collective-permute-done.5.b2.refs_7_) | copy-start | bytes 786436
  39.7 11.4 %collective-permute-start.10 = (bf16[64,2048]{1,0:T(8,128)(2,1)S(1)}, bf16[64,2048]{1,0:T(8,128)(2,1)S(1)}, u32[]{:S(2)}, u32[]{:S(2)}) collective-permute-start(bf16[64,2048]{1,0:T(8,128)(2,1)S(1)} %collective-permute-done.6.b3.refs_8_), channel_id=1, source_target_pairs={{0,1},{1,0},{2,3},{3,2},{4,5},{5,4},{6,7},{7,6},{8,9},{9,8},{10,11... | collective-permute-start | bytes 786440 | tf_op jit(solution)/shard_map/ppermute | solution.py:405
  42.0 6.3 %copy-start.6 = (bf16[64,2048]{1,0:T(8,128)(2,1)}, bf16[64,2048]{1,0:T(8,128)(2,1)S(1)}, u32[]{:S(2)}) copy-start(bf16[64,2048]{1,0:T(8,128)(2,1)S(1)} %collective-permute-done.4.b1.refs_6_) | copy-start | bytes 786436
  42.1 9.0 %collective-permute-start.9 = (bf16[64,2048]{1,0:T(8,128)(2,1)S(1)}, bf16[64,2048]{1,0:T(8,128)(2,1)S(1)}, u32[]{:S(2)}, u32[]{:S(2)}) collective-permute-start(bf16[64,2048]{1,0:T(8,128)(2,1)S(1)} %collective-permute-done.5.b2.refs_7_), channel_id=1, source_target_pairs={{0,1},{1,0},{2,3},{3,2},{4,5},{5,4},{6,7},{7,6},{8,9},{9,8},{10,11... | collective-permute-start | bytes 786440 | tf_op jit(solution)/shard_map/ppermute | solution.py:405
  43.4 0.7 copy-start.7
  43.4 7.7 %collective-permute-start.8 = (bf16[64,2048]{1,0:T(8,128)(2,1)S(1)}, bf16[64,2048]{1,0:T(8,128)(2,1)S(1)}, u32[]{:S(2)}, u32[]{:S(2)}) collective-permute-start(bf16[64,2048]{1,0:T(8,128)(2,1)S(1)} %collective-permute-done.4.b1.refs_6_), channel_id=1, source_target_pairs={{0,1},{1,0},{2,3},{3,2},{4,5},{5,4},{6,7},{7,6},{8,9},{9,8},{10,11... | collective-permute-start | bytes 786440 | tf_op jit(solution)/shard_map/ppermute | solution.py:405
  44.1 0.7 copy-start.8
  51.0 1.7 %collective-permute-start.11 = (f32[2,256,128]{2,1,0:T(8,128)}, f32[2,256,128]{2,1,0:T(8,128)S(1)}, u32[]{:S(2)}, u32[]{:S(2)}) collective-permute-start(f32[2,256,128]{2,1,0:T(8,128)} %shard_map.84.refs_15_), channel_id=1, source_target_pairs={{0,1},{1,0},{2,3},{3,2},{4,5},{5,4},{6,7},{7,6},{8,9},{9,8},{10,11... | collective-permute-start | bytes 786440 | tf_op jit(solution)/shard_map/ppermute | solution.py:405
  51.1 1.7 %copy-start.12 = (bf16[64,2048]{1,0:T(8,128)(2,1)}, bf16[64,2048]{1,0:T(8,128)(2,1)S(1)}, u32[]{:S(2)}) copy-start(bf16[64,2048]{1,0:T(8,128)(2,1)S(1)} %collective-permute-done.7.refs_9_) | copy-start | bytes 786436
  51.1 1.7 %copy-start.13 = (bf16[64,2048]{1,0:T(8,128)(2,1)}, bf16[64,2048]{1,0:T(8,128)(2,1)S(1)}, u32[]{:S(2)}) copy-start(bf16[64,2048]{1,0:T(8,128)(2,1)S(1)} %collective-permute-done.10.refs_12_) | copy-start | bytes 786436
  51.1 1.7 %copy-start.14 = (bf16[64,2048]{1,0:T(8,128)(2,1)}, bf16[64,2048]{1,0:T(8,128)(2,1)S(1)}, u32[]{:S(2)}) copy-start(bf16[64,2048]{1,0:T(8,128)(2,1)S(1)} %collective-permute-done.9.refs_11_) | copy-start | bytes 786436
  51.1 1.7 %copy-start.15 = (bf16[64,2048]{1,0:T(8,128)(2,1)}, bf16[64,2048]{1,0:T(8,128)(2,1)S(1)}, u32[]{:S(2)}) copy-start(bf16[64,2048]{1,0:T(8,128)(2,1)S(1)} %collective-permute-done.8.refs_10_) | copy-start | bytes 786436
  52.7 0.7 copy-start.16
  60.0 4.1 %collective-permute-start.14 = (f32[16,512]{1,0:T(8,128)}, f32[16,512]{1,0:T(8,128)S(1)}, u32[]{:S(2)}, u32[]{:S(2)}) collective-permute-start(f32[16,512]{1,0:T(8,128)} %shard_map.85.refs_17_), channel_id=1, source_target_pairs={{0,6},{1,7},{2,0},{3,1},{4,2},{5,3},{6,4},{7,5},{8,14},{9,15},{10,... | collective-permute-start | bytes 98312 | tf_op jit(solution)/shard_map/ppermute | solution.py:405
  62.8 4.5 %collective-permute-start.13 = (f32[16,512]{1,0:T(8,128)}, f32[16,512]{1,0:T(8,128)S(1)}, u32[]{:S(2)}, u32[]{:S(2)}) collective-permute-start(f32[16,512]{1,0:T(8,128)} %shard_map.85.refs_17_), channel_id=1, source_target_pairs={{0,4},{1,5},{2,6},{3,7},{4,0},{5,1},{6,2},{7,3},{8,12},{9,13},{10,... | collective-permute-start | bytes 98312 | tf_op jit(solution)/shard_map/ppermute | solution.py:405
  62.8 4.5 %collective-permute-start.12 = (f32[16,512]{1,0:T(8,128)}, f32[16,512]{1,0:T(8,128)S(1)}, u32[]{:S(2)}, u32[]{:S(2)}) collective-permute-start(f32[16,512]{1,0:T(8,128)} %shard_map.85.refs_17_), channel_id=1, source_target_pairs={{0,2},{1,3},{2,4},{3,5},{4,6},{5,7},{6,0},{7,1},{8,10},{9,11},{10,... | collective-permute-start | bytes 98312 | tf_op jit(solution)/shard_map/ppermute | solution.py:405
  64.1 3.2 %copy-start.22 = (f32[16,512]{1,0:T(8,128)}, f32[16,512]{1,0:T(8,128)S(1)}, u32[]{:S(2)}) copy-start(f32[16,512]{1,0:T(8,128)S(1)} %collective-permute-done.14.refs_20_) | copy-start | bytes 98308
  67.3 0.6 copy-start.23
  67.9 0.6 copy-start.24
  85.9 4.2 %collective-permute-start.15 = (bf16[272,2048]{1,0:T(8,128)(2,1)}, bf16[272,2048]{1,0:T(8,128)(2,1)S(1)}, u32[]{:S(2)}, u32[]{:S(2)}) collective-permute-start(bf16[272,2048]{1,0:T(8,128)(2,1)} %get-tuple-element.26), channel_id=1, source_target_pairs={{0,1},{1,0},{2,3},{3,2},{4,5},{5,4},{6,7},{7,6},{8,9},{9,8},{10,11... | collective-permute-start | bytes 3342344 | tf_op jit(solution)/shard_map/ppermute | solution.py:405
  87.6 13.7 %collective-permute-start.19 = (bf16[256,1024]{1,0:T(8,128)(2,1)}, bf16[256,1024]{1,0:T(8,128)(2,1)S(1)}, u32[]{:S(2)}, u32[]{:S(2)}) collective-permute-start(bf16[256,1024]{1,0:T(8,128)(2,1)} %get-tuple-element.32), channel_id=1, source_target_pairs={{0,6},{1,7},{2,0},{3,1},{4,2},{5,3},{6,4},{7,5},{8,14},{9,15},{10,... | collective-permute-start | bytes 1572872 | tf_op jit(solution)/shard_map/ppermute | solution.py:405
  90.2 1.0 copy-start.10
  91.2 4.7 %copy-start.26 = (bf16[256,1024]{1,0:T(8,128)(2,1)S(1)}, bf16[256,1024]{1,0:T(8,128)(2,1)}, u32[]{:S(2)}) copy-start(bf16[256,1024]{1,0:T(8,128)(2,1)} %get-tuple-element.34) | copy-start | bytes 1572868
  91.2 10.1 %copy-start.25 = (bf16[256,1024]{1,0:T(8,128)(2,1)S(1)}, bf16[256,1024]{1,0:T(8,128)(2,1)}, u32[]{:S(2)}) copy-start(bf16[256,1024]{1,0:T(8,128)(2,1)} %get-tuple-element.35) | copy-start | bytes 1572868
  94.4 8.1 %collective-permute-start.16 = (bf16[64,2176]{1,0:T(8,128)(2,1)}, bf16[64,2176]{1,0:T(8,128)(2,1)S(1)}, u32[]{:S(2)}, u32[]{:S(2)}) collective-permute-start(bf16[64,2176]{1,0:T(8,128)(2,1)} %get-tuple-element.29), channel_id=1, source_target_pairs={{0,192},{64,0},{128,64},{192,128},{1,193},{65,1},{129,65},{193,129... | collective-permute-start | bytes 835592 | tf_op jit(solution)/shard_map/ppermute | solution.py:410
  94.7 9.3 %collective-permute-start.17 = (bf16[64,2176]{1,0:T(8,128)(2,1)}, bf16[64,2176]{1,0:T(8,128)(2,1)S(1)}, u32[]{:S(2)}, u32[]{:S(2)}) collective-permute-start(bf16[64,2176]{1,0:T(8,128)(2,1)} %get-tuple-element.30), channel_id=1, source_target_pairs={{0,128},{64,192},{128,0},{192,64},{1,129},{65,193},{129,1},{193,65... | collective-permute-start | bytes 835592 | tf_op jit(solution)/shard_map/ppermute | solution.py:410
  95.0 15.9 %collective-permute-start.18 = (bf16[64,2176]{1,0:T(8,128)(2,1)}, bf16[64,2176]{1,0:T(8,128)(2,1)S(1)}, u32[]{:S(2)}, u32[]{:S(2)}) collective-permute-start(bf16[64,2176]{1,0:T(8,128)(2,1)} %get-tuple-element.31), channel_id=1, source_target_pairs={{0,64},{64,128},{128,192},{192,0},{1,65},{65,129},{129,193},{193,1... | collective-permute-start | bytes 835592 | tf_op jit(solution)/shard_map/ppermute | solution.py:410
  95.8 21.4 %collective-permute-start.20 = (bf16[256,1024]{1,0:T(8,128)(2,1)S(1)}, bf16[256,1024]{1,0:T(8,128)(2,1)S(1)}, u32[]{:S(2)}, u32[]{:S(2)}) collective-permute-start(bf16[256,1024]{1,0:T(8,128)(2,1)S(1)} %copy-done.26), channel_id=1, source_target_pairs={{0,4},{1,5},{2,6},{3,7},{4,0},{5,1},{6,2},{7,3},{8,12},{9,13},{10,... | collective-permute-start | bytes 1572872 | tf_op jit(solution)/shard_map/ppermute | solution.py:405
  101.3 9.7 %copy-start.9 = (bf16[256,1024]{1,0:T(8,128)(2,1)}, bf16[256,1024]{1,0:T(8,128)(2,1)S(1)}, u32[]{:S(2)}) copy-start(bf16[256,1024]{1,0:T(8,128)(2,1)S(1)} %collective-permute-done.19.rest_0_.r1) | copy-start | bytes 1572868
  101.3 21.1 %collective-permute-start.21 = (bf16[256,1024]{1,0:T(8,128)(2,1)S(1)}, bf16[256,1024]{1,0:T(8,128)(2,1)S(1)}, u32[]{:S(2)}, u32[]{:S(2)}) collective-permute-start(bf16[256,1024]{1,0:T(8,128)(2,1)S(1)} %copy-done.25), channel_id=1, source_target_pairs={{0,2},{1,3},{2,4},{3,5},{4,6},{5,7},{6,0},{7,1},{8,10},{9,11},{10,... | collective-permute-start | bytes 1572872 | tf_op jit(solution)/shard_map/ppermute | solution.py:405
  102.4 8.5 %copy-start.19 = (bf16[64,2176]{1,0:T(8,128)(2,1)}, bf16[64,2176]{1,0:T(8,128)(2,1)S(1)}, u32[]{:S(2)}) copy-start(bf16[64,2176]{1,0:T(8,128)(2,1)S(1)} %collective-permute-done.16.r1) | copy-start | bytes 835588
  104.0 7.0 %copy-start.20 = (bf16[64,2176]{1,0:T(8,128)(2,1)}, bf16[64,2176]{1,0:T(8,128)(2,1)S(1)}, u32[]{:S(2)}) copy-start(bf16[64,2176]{1,0:T(8,128)(2,1)S(1)} %collective-permute-done.17.r2) | copy-start | bytes 835588
  110.9 0.7 copy-start.21
  113.8 16.0 %all-to-all-start.1 = ((bf16[8,8,2176]{2,1,0:T(8,128)(2,1)}), bf16[8,8,2176]{2,1,0:T(8,128)(2,1)S(1)}, u32[]{:S(2)}, u32[]{:S(2)}) async-start(bf16[8,8,2176]{2,1,0:T(8,128)(2,1)} %bitcast.10), calls=%async_computation.1 | async-start | bytes 557056 | tf_op jit(solution)/shard_map/all_to_all | solution.py:414
  117.2 5.2 %copy-start.17 = (bf16[256,1024]{1,0:T(8,128)(2,1)}, bf16[256,1024]{1,0:T(8,128)(2,1)S(1)}, u32[]{:S(2)}) copy-start(bf16[256,1024]{1,0:T(8,128)(2,1)S(1)} %collective-permute-done.20.r2) | copy-start | bytes 1572868
  122.4 0.8 copy-start.18
  129.7 0.7 copy-start.11

commit v4 on v3

--- a/solution.py
+++ b/solution.py
@@ -105,7 +105,7 @@
     matched[...] = SCALE * sums_across(product, across)[:8] * rq[0, :, :ROWS] * rq[1, :, :ROWS]
 
 
-def prepare_keys(b0, b1, b2, b3, after, kn):
+def prepare_keys(b0, b1, b2, b3, after, later, kn):
     down = level_mask((D, LANES), 1)
     for s, block in enumerate((b0, b1, b2, b3)):
         for side in range(2):
@@ -437,7 +437,9 @@
     near = exchange(jnp.tile(bank, (PAIRS, 1)))
     around = [near] + [along_y(near, s) for s in (1, 2, 3)]
     rq, matched = call(prepare, [shaped((2, 8, CHUNK)), shaped((8, ROWS))])(*queries)
-    (n0,) = placed(prepare_keys, [INSIDE] * 4 + [ANYWHERE], [INSIDE], [shaped((2, KEYS, LANES))])(*around, matched)
+    (n0,) = placed(prepare_keys, [INSIDE] * 4 + [ANYWHERE] * 2, [INSIDE], [shaped((2, KEYS, LANES))])(
+        *around, queries[2], queries[3]
+    )
     n1 = move(n0, 0, 1)
     far = [move(b, 0, 1) for b in around]
     blocks = queries + around + far

time: 133 us -> 132 us (level)
  waiting for transfers between devices: 34.7 us -> 33.1 us
    ppermute x16, waiting for transfers between devices: 17.6 us -> 16 us  [move(): return lax.ppermute(value, ('x', 'c'), pairs)]
  transfers between devices with their start and end apart: 23 -> 23, of which waited for: 12 -> 11; matrix products, arithmetic and copies ran while one was open for 1% -> 1% of each run, Pallas kernels for 11% -> 11%
where the time goes in v4:
time: 132 us
  Pallas kernels  39.8 us (30%)
  waiting for transfers between devices  33.1 us (25%)
  starting transfers between devices  30.1 us (23%)
  blocking collectives  18.1 us (14%)
  local copies, waits for them, and re-layouts  8.74 us (7%)
    ppermute x16, starting transfers between devices, move(): return lax.ppermute(value, ('x', 'c'), pairs)  21.4 us
    all_to_all x1, blocking collectives, exchange(): return lax.all_to_all(value, 'z', 0, 0, tiled=True)  18.1 us
    pallas_call x1, Pallas kernels, on_device(): placed(backward, [ANYWHERE] * 13 + [INSIDE] * 8, [ANYWHERE] * 6 + [INSIDE...  17.4 us
    ppermute x16, waiting for transfers between devices, move(): return lax.ppermute(value, ('x', 'c'), pairs)  16 us
    ppermute x6, waiting for transfers between devices, along_y(): return lax.ppermute(value, 'y', [(i, (i + step) % n) for i in range(n)])  13.4 us
    unnamed x55, local copies, waits for them, and re-layouts  7.72 us
    pallas_call x1, Pallas kernels, on_device(): placed(forward, [ANYWHERE] * 13 + [INSIDE] * 4, [INSIDE], [shaped((16, CH...  6.51 us
    ppermute x6, starting transfers between devices, along_y(): return lax.ppermute(value, 'y', [(i, (i + step) % n) for i in range(n)])  5.24 us
  transfers between devices with their start and end apart: 23, of which 11 were waited for; matrix products, arithmetic and copies ran while one was open for 1% of the time, Pallas kernels for 11%

profile of v4, /device:TPU:1, one launch (start us, length us, event | category | flops | bytes accessed | tf_op | source)
XLA Modules:
  0.0 131.6 jit_solution(17642145343762408879)
XLA Ops:
  0.6 1.0 constant_dynamic-update-slice_fusion.1
  1.6 1.0 constant_dynamic-update-slice_fusion.q0.refs_0_
  2.6 0.0 copy-start.2
  2.6 3.4 %collective-permute-start.2 = (bf16[256,1024]{1,0:T(8,128)(2,1)S(1)}, bf16[256,1024]{1,0:T(8,128)(2,1)S(1)}, u32[]{:S(2)}, u32[]{:S(2)}) collective-permute-start(bf16[256,1024]{1,0:T(8,128)(2,1)S(1)} %constant_dynamic-update-slice_fusion.q0.refs_0_), channel_id=1, source_target_pairs={{0,6},{1,7},{2,0},{3,1},{4,2},{5,3},{6,4},{7,5},{8,14},{9,15},{10,... | collective-permute-start | bytes 1572872 | tf_op jit(solution)/shard_map/ppermute | solution.py:405
  6.0 0.0 collective-permute-start
  6.0 0.7 pad_maximum_fusion
  6.7 18.1 %all_to_all.19 = bf16[8,8,2048]{2,1,0:T(8,128)(2,1)S(1)} all-to-all(bf16[8,8,2048]{2,1,0:T(8,128)(2,1)S(1)} %tile.2), channel_id=1, replica_groups=mesh['y'=4,'z'=8,'x'=4,'c'=2] {'z'}, dimensions={0} | all-to-all | bytes 524288 | tf_op jit(solution)/shard_map/all_to_all | solution.py:414
  24.8 2.7 %collective-permute-start.6 = (bf16[64,2048]{1,0:T(8,128)(2,1)S(1)}, bf16[64,2048]{1,0:T(8,128)(2,1)S(1)}, u32[]{:S(2)}, u32[]{:S(2)}) collective-permute-start(bf16[64,2048]{1,0:T(8,128)(2,1)S(1)} %bitcast.3), channel_id=1, source_target_pairs={{0,192},{64,0},{128,64},{192,128},{1,193},{65,1},{129,65},{193,129... | collective-permute-start | bytes 786440 | tf_op jit(solution)/shard_map/ppermute | solution.py:410
  27.5 0.3 collective-permute-start.5
  27.9 0.7 collective-permute-start.4
  28.6 0.0 collective-permute-done.2.q3.refs_4_
  28.6 2.8 %collective-permute-start.3 = (bf16[128,1024]{1,0:T(8,128)(2,1)S(1)}, bf16[128,1024]{1,0:T(8,128)(2,1)S(1)}, u32[]{:S(2)}, u32[]{:S(2)}) collective-permute-start(bf16[128,1024]{1,0:T(8,128)(2,1)S(1)} %slice.9), channel_id=1, source_target_pairs={{0,6},{1,7},{2,0},{3,1},{4,2},{5,3},{6,4},{7,5},{8,14},{9,15},{10,... | collective-permute-start | bytes 786440 | tf_op jit(solution)/shard_map/ppermute | solution.py:405
  31.4 0.0 collective-permute-done.q1.refs_1_
  31.4 0.1 collective-permute-start.1
  31.5 2.3 %collective-permute-done.6.b3.refs_8_ = bf16[64,2048]{1,0:T(8,128)(2,1)S(1)} collective-permute-done((bf16[64,2048]{1,0:T(8,128)(2,1)S(1)}, bf16[64,2048]{1,0:T(8,128)(2,1)S(1)}, u32[]{:S(2)}, u32[]{:S(2)}) %collective-permute-start.6) | collective-permute-done | bytes 262176 | tf_op jit(solution)/shard_map/ppermute | solution.py:410
  33.9 5.8 %collective-permute-start.7 = (bf16[64,2048]{1,0:T(8,128)(2,1)S(1)}, bf16[64,2048]{1,0:T(8,128)(2,1)S(1)}, u32[]{:S(2)}, u32[]{:S(2)}) collective-permute-start(bf16[64,2048]{1,0:T(8,128)(2,1)S(1)} %bitcast.6), channel_id=1, source_target_pairs={{0,1},{1,0},{2,3},{3,2},{4,5},{5,4},{6,7},{7,6},{8,9},{9,8},{10,11... | collective-permute-start | bytes 786440 | tf_op jit(solution)/shard_map/ppermute | solution.py:405
  39.7 1.0 collective-permute-start.10
  40.7 1.4 %collective-permute-done.4.b1.refs_6_ = bf16[64,2048]{1,0:T(8,128)(2,1)S(1)} collective-permute-done((bf16[64,2048]{1,0:T(8,128)(2,1)S(1)}, bf16[64,2048]{1,0:T(8,128)(2,1)S(1)}, u32[]{:S(2)}, u32[]{:S(2)}) %collective-permute-start.4) | collective-permute-done | bytes 262176 | tf_op jit(solution)/shard_map/ppermute | solution.py:410
  42.1 1.3 %collective-permute-start.9 = (bf16[64,2048]{1,0:T(8,128)(2,1)S(1)}, bf16[64,2048]{1,0:T(8,128)(2,1)S(1)}, u32[]{:S(2)}, u32[]{:S(2)}) collective-permute-start(bf16[64,2048]{1,0:T(8,128)(2,1)S(1)} %collective-permute-done.5.b2.refs_7_), channel_id=1, source_target_pairs={{0,1},{1,0},{2,3},{3,2},{4,5},{5,4},{6,7},{7,6},{8,9},{9,8},{10,11... | collective-permute-start | bytes 786440 | tf_op jit(solution)/shard_map/ppermute | solution.py:405
  43.4 0.0 collective-permute-done.3.q2b.later.refs_3_
  43.4 0.1 collective-permute-start.8
  43.5 0.6 copy-done.4
  44.1 0.7 copy-done.5
  44.8 2.7 %shard_map.84.refs_15_ = f32[2,256,128]{2,1,0:T(8,128)} custom-call(bf16[64,2048]{1,0:T(8,128)(2,1)} %bitcast.7, bf16[64,2048]{1,0:T(8,128)(2,1)} %copy-done.8, bf16[64,2048]{1,0:T(8,128)(2,1)} %copy-done.7, bf16[64,2048]{1,0:T(8,128)(2,1)} %copy-done.6, bf16[128,1024]{1,0:T(8,128)(2,1)} %copy-done.5, bf16[128,1024]{1,0:T(8,128)(2,1)} %copy-done.4), custom_call_target="tpu_custom_call" | custom-call | tf_op jit(solution)/shard_map/pallas_call | solution.py:440
  47.5 0.4 collective-permute-start.11
  47.8 3.5 %shard_map.83 = (f32[2,8,512]{2,1,0:T(8,128)}, f32[8,128]{1,0:T(8,128)}) custom-call(bf16[256,1024]{1,0:T(8,128)(2,1)} %copy-done.2, bf16[256,1024]{1,0:T(8,128)(2,1)} %copy-done.1, bf16[128,1024]{1,0:T(8,128)(2,1)} %copy-done.5, bf16[128,1024]{1,0:T(8,128)(2,1)} %copy-done.4, bf16[256,1024]{1,0:T(8,128)(2,1)} %copy-done), custom_call_target="tpu_custom_call" | custom-call | tf_op jit(solution)/shard_map/pallas_call | solution.py:439
  51.4 0.0 collective-permute-done.9.refs_11_
  51.4 0.0 collective-permute-done.8.refs_10_
  51.4 0.6 copy-done.12
  52.1 0.1 copy-done.13
  52.1 0.1 copy-done.14
  52.2 0.1 copy-done.15
  52.4 0.1 copy-done.16
  52.5 6.5 %shard_map.85.refs_17_ = f32[16,512]{1,0:T(8,128)} custom-call(bf16[256,1024]{1,0:T(8,128)(2,1)} %copy-done.2, bf16[256,1024]{1,0:T(8,128)(2,1)} %copy-done.1, bf16[128,1024]{1,0:T(8,128)(2,1)} %copy-done.5, bf16[128,1024]{1,0:T(8,128)(2,1)} %copy-done.4, bf16[256,1024]{1,0:T(8,128)(2,1)} %copy-done, bf16[64,2048]{1,0:T(8,128)(2,1)} %bitcast.8, ...), custom_call_target="tpu_custom_call" | custom-call | tf_op jit(solution)/shard_map/pallas_call | solution.py:452
  59.0 2.8 %collective-permute-start.14 = (f32[16,512]{1,0:T(8,128)}, f32[16,512]{1,0:T(8,128)S(1)}, u32[]{:S(2)}, u32[]{:S(2)}) collective-permute-start(f32[16,512]{1,0:T(8,128)} %shard_map.85.refs_17_), channel_id=1, source_target_pairs={{0,6},{1,7},{2,0},{3,1},{4,2},{5,3},{6,4},{7,5},{8,14},{9,15},{10,... | collective-permute-start | bytes 98312 | tf_op jit(solution)/shard_map/ppermute | solution.py:405
  61.8 0.7 collective-permute-start.12
  62.5 0.7 collective-permute-done.14.refs_20_
  63.1 3.2 %collective-permute-done.13.refs_19_ = f32[16,512]{1,0:T(8,128)S(1)} collective-permute-done((f32[16,512]{1,0:T(8,128)}, f32[16,512]{1,0:T(8,128)S(1)}, u32[]{:S(2)}, u32[]{:S(2)}) %collective-permute-start.13) | collective-permute-done | bytes 32800 | tf_op jit(solution)/shard_map/ppermute | solution.py:405
  66.3 0.0 collective-permute-done.12.refs_18_
  66.3 0.6 copy-done.23
  66.9 0.6 copy-done.24
  67.5 17.4 %shard_map.86 = (f32[256,1024]{1,0:T(8,128)}, bf16[256,1024]{1,0:T(8,128)(2,1)}, bf16[256,1024]{1,0:T(8,128)(2,1)}, bf16[256,1024]{1,0:T(8,128)(2,1)}, f32[256,2...) custom-call(bf16[256,1024]{1,0:T(8,128)(2,1)} %copy-done.2, bf16[256,1024]{1,0:T(8,128)(2,1)} %copy-done.1, ...), custom_call_target="tpu_custom_call" | custom-call | tf_op jit(solution)/shard_map/pallas_call | solution.py:468
  85.0 1.9 %collective-permute-start.15 = (bf16[272,2048]{1,0:T(8,128)(2,1)}, bf16[272,2048]{1,0:T(8,128)(2,1)S(1)}, u32[]{:S(2)}, u32[]{:S(2)}) collective-permute-start(bf16[272,2048]{1,0:T(8,128)(2,1)} %get-tuple-element.26), channel_id=1, source_target_pairs={{0,1},{1,0},{2,3},{3,2},{4,5},{5,4},{6,7},{7,6},{8,9},{9,8},{10,11... | collective-permute-start | bytes 3342344 | tf_op jit(solution)/shard_map/ppermute | solution.py:405
  86.9 0.0 collective-permute-start.19
  86.9 2.6 %collective-permute-done.15.other = bf16[272,2048]{1,0:T(8,128)(2,1)S(1)} collective-permute-done((bf16[272,2048]{1,0:T(8,128)(2,1)}, bf16[272,2048]{1,0:T(8,128)(2,1)S(1)}, u32[]{:S(2)}, u32[]{:S(2)}) %collective-permute-start.15) | collective-permute-done | bytes 1114144 | tf_op jit(solution)/shard_map/ppermute | solution.py:405
  89.5 1.0 copy-done.10
  90.5 3.2 %shard_map.87 = (f32[64,2176]{1,0:T(8,128)}, bf16[64,2176]{1,0:T(8,128)(2,1)}, bf16[64,2176]{1,0:T(8,128)(2,1)}, bf16[64,2176]{1,0:T(8,128)(2,1)}) custom-call(f32[256,2048]{1,0:T(8,128)} %get-tuple-element.25.own, bf16[272,2048]{1,0:T(8,128)(2,1)} %copy-done.10, f32[8,128]{1,0:T(8,128)} %get-tuple-element.27.loss), custom_call_target="tpu_custom_call" | custom-call | tf_op jit(solution)/shard_map/pallas_call | solution.py:486
  93.7 0.3 collective-permute-start.16
  94.0 0.4 collective-permute-start.17
  94.4 0.8 collective-permute-start.18
  95.1 1.1 collective-permute-start.20
  96.3 4.3 %collective-permute-done.19.rest_0_.r1 = bf16[256,1024]{1,0:T(8,128)(2,1)S(1)} collective-permute-done((bf16[256,1024]{1,0:T(8,128)(2,1)}, bf16[256,1024]{1,0:T(8,128)(2,1)S(1)}, u32[]{:S(2)}, u32[]{:S(2)}) %collective-permute-start.19) | collective-permute-done | bytes 524320 | tf_op jit(solution)/shard_map/ppermute | solution.py:405
  100.6 1.2 collective-permute-done.16.r1
  101.8 1.5 %collective-permute-done.17.r2 = bf16[64,2176]{1,0:T(8,128)(2,1)S(1)} collective-permute-done((bf16[64,2176]{1,0:T(8,128)(2,1)}, bf16[64,2176]{1,0:T(8,128)(2,1)S(1)}, u32[]{:S(2)}, u32[]{:S(2)}) %collective-permute-start.17) | collective-permute-done | bytes 278560 | tf_op jit(solution)/shard_map/ppermute | solution.py:410
  103.3 7.0 %collective-permute-done.18.r3 = bf16[64,2176]{1,0:T(8,128)(2,1)S(1)} collective-permute-done((bf16[64,2176]{1,0:T(8,128)(2,1)}, bf16[64,2176]{1,0:T(8,128)(2,1)S(1)}, u32[]{:S(2)}, u32[]{:S(2)}) %collective-permute-start.18) | collective-permute-done | bytes 278560 | tf_op jit(solution)/shard_map/ppermute | solution.py:410
  110.3 0.7 copy-done.21
  111.0 2.1 %shard_map.88 = bf16[64,2176]{1,0:T(8,128)(2,1)} custom-call(f32[64,2176]{1,0:T(8,128)} %get-tuple-element.28.own, bf16[64,2176]{1,0:T(8,128)(2,1)} %copy-done.19, bf16[64,2176]{1,0:T(8,128)(2,1)} %copy-done.20, bf16[64,2176]{1,0:T(8,128)(2,1)} %copy-done.21, bf16[256,1024]{1,0:T(8,128)(2,1)} %copy-done.9), custom_call_target="tpu_custom_call" | custom-call | tf_op jit(solution)/shard_map/pallas_call | solution.py:491
  113.1 3.4 %all-to-all-start.1 = ((bf16[8,8,2176]{2,1,0:T(8,128)(2,1)}), bf16[8,8,2176]{2,1,0:T(8,128)(2,1)S(1)}, u32[]{:S(2)}, u32[]{:S(2)}) async-start(bf16[8,8,2176]{2,1,0:T(8,128)(2,1)} %bitcast.10), calls=%async_computation.1 | async-start | bytes 557056 | tf_op jit(solution)/shard_map/all_to_all | solution.py:414
  116.5 5.2 %collective-permute-done.21.r3 = bf16[256,1024]{1,0:T(8,128)(2,1)S(1)} collective-permute-done((bf16[256,1024]{1,0:T(8,128)(2,1)S(1)}, bf16[256,1024]{1,0:T(8,128)(2,1)S(1)}, u32[]{:S(2)}, u32[]{:S(2)}) %collective-permute-start.21) | collective-permute-done | bytes 524320 | tf_op jit(solution)/shard_map/ppermute | solution.py:405
  121.7 0.8 copy-done.18
  122.5 2.7 %shard_map.89 = (f32[128,1024]{1,0:T(8,128)}, f32[128,1024]{1,0:T(8,128)}) custom-call(f32[256,1024]{1,0:T(8,128)} %get-tuple-element.33.own, bf16[256,1024]{1,0:T(8,128)(2,1)} %copy-done.9, bf16[256,1024]{1,0:T(8,128)(2,1)} %copy-done.17, bf16[256,1024]{1,0:T(8,128)(2,1)} %copy-done.18), custom_call_target="tpu_custom_call" | custom-call | tf_op jit(solution)/shard_map/pallas_call | solution.py:495
  125.3 3.8 %all-to-all-done.1 = bf16[8,8,2176]{2,1,0:T(8,128)(2,1)S(1)} async-done(((bf16[8,8,2176]{2,1,0:T(8,128)(2,1)}), bf16[8,8,2176]{2,1,0:T(8,128)(2,1)S(1)}, u32[]{:S(2)}, u32[]{:S(2)}) %all-to-all-start.1) | async-done | bytes 278560 | tf_op jit(solution)/shard_map/all_to_all | solution.py:414
  129.1 0.7 copy-done.11
  129.8 1.6 %shard_map.90 = (f32[8,1024]{1,0:T(8,128)}, f32[8,1024]{1,0:T(8,128)}, f32[6]{0:T(128)}) custom-call(bf16[64,2176]{1,0:T(8,128)(2,1)} %bitcast.11, f32[128,1024]{1,0:T(8,128)} %get-tuple-element.19.after), custom_call_target="tpu_custom_call" | custom-call | tf_op jit(solution)/shard_map/pallas_call | solution.py:496
  (51 shorter events, 0.1 us)
Async XLA Ops:
  2.6 44.9 %copy-start.2 = (bf16[256,1024]{1,0:T(8,128)(2,1)}, bf16[256,1024]{1,0:T(8,128)(2,1)S(1)}, u32[]{:S(2)}) copy-start(bf16[256,1024]{1,0:T(8,128)(2,1)S(1)} %constant_dynamic-update-slice_fusion.q0.refs_0_) | copy-start | bytes 1572868
  2.6 26.0 %collective-permute-start.2 = (bf16[256,1024]{1,0:T(8,128)(2,1)S(1)}, bf16[256,1024]{1,0:T(8,128)(2,1)S(1)}, u32[]{:S(2)}, u32[]{:S(2)}) collective-permute-start(bf16[256,1024]{1,0:T(8,128)(2,1)S(1)} %constant_dynamic-update-slice_fusion.q0.refs_0_), channel_id=1, source_target_pairs={{0,6},{1,7},{2,0},{3,1},{4,2},{5,3},{6,4},{7,5},{8,14},{9,15},{10,... | collective-permute-start | bytes 1572872 | tf_op jit(solution)/shard_map/ppermute | solution.py:405
  6.0 25.4 %collective-permute-start = (bf16[256,1024]{1,0:T(8,128)(2,1)S(1)}, bf16[256,1024]{1,0:T(8,128)(2,1)S(1)}, u32[]{:S(2)}, u32[]{:S(2)}) collective-permute-start(bf16[256,1024]{1,0:T(8,128)(2,1)S(1)} %constant_dynamic-update-slice_fusion.q0.refs_0_), channel_id=1, source_target_pairs={{0,2},{1,3},{2,4},{3,5},{4,6},{5,7},{6,0},{7,1},{8,10},{9,11},{10,... | collective-permute-start | bytes 1572872 | tf_op jit(solution)/shard_map/ppermute | solution.py:405
  24.8 18.7 %copy-start.3 = (bf16[8,8,2048]{2,1,0:T(8,128)(2,1)}, bf16[8,8,2048]{2,1,0:T(8,128)(2,1)S(1)}, u32[]{:S(2)}) copy-start(bf16[8,8,2048]{2,1,0:T(8,128)(2,1)S(1)} %all_to_all.19) | copy-start | bytes 786436
  24.8 9.0 %collective-permute-start.6 = (bf16[64,2048]{1,0:T(8,128)(2,1)S(1)}, bf16[64,2048]{1,0:T(8,128)(2,1)S(1)}, u32[]{:S(2)}, u32[]{:S(2)}) collective-permute-start(bf16[64,2048]{1,0:T(8,128)(2,1)S(1)} %bitcast.3), channel_id=1, source_target_pairs={{0,192},{64,0},{128,64},{192,128},{1,193},{65,1},{129,65},{193,129... | collective-permute-start | bytes 786440 | tf_op jit(solution)/shard_map/ppermute | solution.py:410
  27.5 12.1 %collective-permute-start.5 = (bf16[64,2048]{1,0:T(8,128)(2,1)S(1)}, bf16[64,2048]{1,0:T(8,128)(2,1)S(1)}, u32[]{:S(2)}, u32[]{:S(2)}) collective-permute-start(bf16[64,2048]{1,0:T(8,128)(2,1)S(1)} %bitcast.4), channel_id=1, source_target_pairs={{0,128},{64,192},{128,0},{192,64},{1,129},{65,193},{129,1},{193,65... | collective-permute-start | bytes 786440 | tf_op jit(solution)/shard_map/ppermute | solution.py:410
  27.9 14.2 %collective-permute-start.4 = (bf16[64,2048]{1,0:T(8,128)(2,1)S(1)}, bf16[64,2048]{1,0:T(8,128)(2,1)S(1)}, u32[]{:S(2)}, u32[]{:S(2)}) collective-permute-start(bf16[64,2048]{1,0:T(8,128)(2,1)S(1)} %bitcast.5), channel_id=1, source_target_pairs={{0,64},{64,128},{128,192},{192,0},{1,65},{65,129},{129,193},{193,1... | collective-permute-start | bytes 786440 | tf_op jit(solution)/shard_map/ppermute | solution.py:410
  28.6 18.9 %copy-start = (bf16[256,1024]{1,0:T(8,128)(2,1)}, bf16[256,1024]{1,0:T(8,128)(2,1)S(1)}, u32[]{:S(2)}) copy-start(bf16[256,1024]{1,0:T(8,128)(2,1)S(1)} %collective-permute-done.2.q3.refs_4_) | copy-start | bytes 1572868
  28.6 14.8 %collective-permute-start.3 = (bf16[128,1024]{1,0:T(8,128)(2,1)S(1)}, bf16[128,1024]{1,0:T(8,128)(2,1)S(1)}, u32[]{:S(2)}, u32[]{:S(2)}) collective-permute-start(bf16[128,1024]{1,0:T(8,128)(2,1)S(1)} %slice.9), channel_id=1, source_target_pairs={{0,6},{1,7},{2,0},{3,1},{4,2},{5,3},{6,4},{7,5},{8,14},{9,15},{10,... | collective-permute-start | bytes 786440 | tf_op jit(solution)/shard_map/ppermute | solution.py:405
  31.4 16.0 %copy-start.1 = (bf16[256,1024]{1,0:T(8,128)(2,1)}, bf16[256,1024]{1,0:T(8,128)(2,1)S(1)}, u32[]{:S(2)}) copy-start(bf16[256,1024]{1,0:T(8,128)(2,1)S(1)} %collective-permute-done.q1.refs_1_) | copy-start | bytes 1572868
  31.4 12.1 %collective-permute-start.1 = (bf16[128,1024]{1,0:T(8,128)(2,1)S(1)}, bf16[128,1024]{1,0:T(8,128)(2,1)S(1)}, u32[]{:S(2)}, u32[]{:S(2)}) collective-permute-start(bf16[128,1024]{1,0:T(8,128)(2,1)S(1)} %slice.8), channel_id=1, source_target_pairs={{0,2},{1,3},{2,4},{3,5},{4,6},{5,7},{6,0},{7,1},{8,10},{9,11},{10,... | collective-permute-start | bytes 786440 | tf_op jit(solution)/shard_map/ppermute | solution.py:405
  33.9 9.6 %copy-start.6 = (bf16[64,2048]{1,0:T(8,128)(2,1)}, bf16[64,2048]{1,0:T(8,128)(2,1)S(1)}, u32[]{:S(2)}) copy-start(bf16[64,2048]{1,0:T(8,128)(2,1)S(1)} %collective-permute-done.6.b3.refs_8_) | copy-start | bytes 786436
  33.9 17.5 %collective-permute-start.7 = (bf16[64,2048]{1,0:T(8,128)(2,1)S(1)}, bf16[64,2048]{1,0:T(8,128)(2,1)S(1)}, u32[]{:S(2)}, u32[]{:S(2)}) collective-permute-start(bf16[64,2048]{1,0:T(8,128)(2,1)S(1)} %bitcast.6), channel_id=1, source_target_pairs={{0,1},{1,0},{2,3},{3,2},{4,5},{5,4},{6,7},{7,6},{8,9},{9,8},{10,11... | collective-permute-start | bytes 786440 | tf_op jit(solution)/shard_map/ppermute | solution.py:405
  39.7 3.8 %copy-start.7 = (bf16[64,2048]{1,0:T(8,128)(2,1)}, bf16[64,2048]{1,0:T(8,128)(2,1)S(1)}, u32[]{:S(2)}) copy-start(bf16[64,2048]{1,0:T(8,128)(2,1)S(1)} %collective-permute-done.5.b2.refs_7_) | copy-start | bytes 786436
  39.7 11.7 %collective-permute-start.10 = (bf16[64,2048]{1,0:T(8,128)(2,1)S(1)}, bf16[64,2048]{1,0:T(8,128)(2,1)S(1)}, u32[]{:S(2)}, u32[]{:S(2)}) collective-permute-start(bf16[64,2048]{1,0:T(8,128)(2,1)S(1)} %collective-permute-done.6.b3.refs_8_), channel_id=1, source_target_pairs={{0,1},{1,0},{2,3},{3,2},{4,5},{5,4},{6,7},{7,6},{8,9},{9,8},{10,11... | collective-permute-start | bytes 786440 | tf_op jit(solution)/shard_map/ppermute | solution.py:405
  42.0 1.5 %copy-start.8 = (bf16[64,2048]{1,0:T(8,128)(2,1)}, bf16[64,2048]{1,0:T(8,128)(2,1)S(1)}, u32[]{:S(2)}) copy-start(bf16[64,2048]{1,0:T(8,128)(2,1)S(1)} %collective-permute-done.4.b1.refs_6_) | copy-start | bytes 786436
  42.1 9.3 %collective-permute-start.9 = (bf16[64,2048]{1,0:T(8,128)(2,1)S(1)}, bf16[64,2048]{1,0:T(8,128)(2,1)S(1)}, u32[]{:S(2)}, u32[]{:S(2)}) collective-permute-start(bf16[64,2048]{1,0:T(8,128)(2,1)S(1)} %collective-permute-done.5.b2.refs_7_), channel_id=1, source_target_pairs={{0,1},{1,0},{2,3},{3,2},{4,5},{5,4},{6,7},{7,6},{8,9},{9,8},{10,11... | collective-permute-start | bytes 786440 | tf_op jit(solution)/shard_map/ppermute | solution.py:405
  43.4 0.7 copy-start.4
  43.4 8.0 %collective-permute-start.8 = (bf16[64,2048]{1,0:T(8,128)(2,1)S(1)}, bf16[64,2048]{1,0:T(8,128)(2,1)S(1)}, u32[]{:S(2)}, u32[]{:S(2)}) collective-permute-start(bf16[64,2048]{1,0:T(8,128)(2,1)S(1)} %collective-permute-done.4.b1.refs_6_), channel_id=1, source_target_pairs={{0,1},{1,0},{2,3},{3,2},{4,5},{5,4},{6,7},{7,6},{8,9},{9,8},{10,11... | collective-permute-start | bytes 786440 | tf_op jit(solution)/shard_map/ppermute | solution.py:405
  44.1 0.7 copy-start.5
  47.5 3.9 %collective-permute-start.11 = (f32[2,256,128]{2,1,0:T(8,128)}, f32[2,256,128]{2,1,0:T(8,128)S(1)}, u32[]{:S(2)}, u32[]{:S(2)}) collective-permute-start(f32[2,256,128]{2,1,0:T(8,128)} %shard_map.84.refs_15_), channel_id=1, source_target_pairs={{0,1},{1,0},{2,3},{3,2},{4,5},{5,4},{6,7},{7,6},{8,9},{9,8},{10,11... | collective-permute-start | bytes 786440 | tf_op jit(solution)/shard_map/ppermute | solution.py:405
  51.3 0.7 copy-start.12
  51.4 0.8 copy-start.13
  51.4 0.9 copy-start.14
  51.4 1.0 copy-start.15
  51.4 1.0 copy-start.16
  59.0 4.1 %collective-permute-start.14 = (f32[16,512]{1,0:T(8,128)}, f32[16,512]{1,0:T(8,128)S(1)}, u32[]{:S(2)}, u32[]{:S(2)}) collective-permute-start(f32[16,512]{1,0:T(8,128)} %shard_map.85.refs_17_), channel_id=1, source_target_pairs={{0,6},{1,7},{2,0},{3,1},{4,2},{5,3},{6,4},{7,5},{8,14},{9,15},{10,... | collective-permute-start | bytes 98312 | tf_op jit(solution)/shard_map/ppermute | solution.py:405
  61.8 4.5 %collective-permute-start.13 = (f32[16,512]{1,0:T(8,128)}, f32[16,512]{1,0:T(8,128)S(1)}, u32[]{:S(2)}, u32[]{:S(2)}) collective-permute-start(f32[16,512]{1,0:T(8,128)} %shard_map.85.refs_17_), channel_id=1, source_target_pairs={{0,4},{1,5},{2,6},{3,7},{4,0},{5,1},{6,2},{7,3},{8,12},{9,13},{10,... | collective-permute-start | bytes 98312 | tf_op jit(solution)/shard_map/ppermute | solution.py:405
  61.8 4.5 %collective-permute-start.12 = (f32[16,512]{1,0:T(8,128)}, f32[16,512]{1,0:T(8,128)S(1)}, u32[]{:S(2)}, u32[]{:S(2)}) collective-permute-start(f32[16,512]{1,0:T(8,128)} %shard_map.85.refs_17_), channel_id=1, source_target_pairs={{0,2},{1,3},{2,4},{3,5},{4,6},{5,7},{6,0},{7,1},{8,10},{9,11},{10,... | collective-permute-start | bytes 98312 | tf_op jit(solution)/shard_map/ppermute | solution.py:405
  63.1 3.2 %copy-start.22 = (f32[16,512]{1,0:T(8,128)}, f32[16,512]{1,0:T(8,128)S(1)}, u32[]{:S(2)}) copy-start(f32[16,512]{1,0:T(8,128)S(1)} %collective-permute-done.14.refs_20_) | copy-start | bytes 98308
  66.3 0.6 copy-start.23
  66.9 0.6 copy-start.24
  85.0 4.5 %collective-permute-start.15 = (bf16[272,2048]{1,0:T(8,128)(2,1)}, bf16[272,2048]{1,0:T(8,128)(2,1)S(1)}, u32[]{:S(2)}, u32[]{:S(2)}) collective-permute-start(bf16[272,2048]{1,0:T(8,128)(2,1)} %get-tuple-element.26), channel_id=1, source_target_pairs={{0,1},{1,0},{2,3},{3,2},{4,5},{5,4},{6,7},{7,6},{8,9},{9,8},{10,11... | collective-permute-start | bytes 3342344 | tf_op jit(solution)/shard_map/ppermute | solution.py:405
  86.9 13.7 %collective-permute-start.19 = (bf16[256,1024]{1,0:T(8,128)(2,1)}, bf16[256,1024]{1,0:T(8,128)(2,1)S(1)}, u32[]{:S(2)}, u32[]{:S(2)}) collective-permute-start(bf16[256,1024]{1,0:T(8,128)(2,1)} %get-tuple-element.32), channel_id=1, source_target_pairs={{0,6},{1,7},{2,0},{3,1},{4,2},{5,3},{6,4},{7,5},{8,14},{9,15},{10,... | collective-permute-start | bytes 1572872 | tf_op jit(solution)/shard_map/ppermute | solution.py:405
  89.5 1.0 copy-start.10
  90.5 4.7 %copy-start.26 = (bf16[256,1024]{1,0:T(8,128)(2,1)S(1)}, bf16[256,1024]{1,0:T(8,128)(2,1)}, u32[]{:S(2)}) copy-start(bf16[256,1024]{1,0:T(8,128)(2,1)} %get-tuple-element.34) | copy-start | bytes 1572868
  90.5 10.1 %copy-start.25 = (bf16[256,1024]{1,0:T(8,128)(2,1)S(1)}, bf16[256,1024]{1,0:T(8,128)(2,1)}, u32[]{:S(2)}) copy-start(bf16[256,1024]{1,0:T(8,128)(2,1)} %get-tuple-element.35) | copy-start | bytes 1572868
  93.7 8.1 %collective-permute-start.16 = (bf16[64,2176]{1,0:T(8,128)(2,1)}, bf16[64,2176]{1,0:T(8,128)(2,1)S(1)}, u32[]{:S(2)}, u32[]{:S(2)}) collective-permute-start(bf16[64,2176]{1,0:T(8,128)(2,1)} %get-tuple-element.29), channel_id=1, source_target_pairs={{0,192},{64,0},{128,64},{192,128},{1,193},{65,1},{129,65},{193,129... | collective-permute-start | bytes 835592 | tf_op jit(solution)/shard_map/ppermute | solution.py:410
  94.0 9.3 %collective-permute-start.17 = (bf16[64,2176]{1,0:T(8,128)(2,1)}, bf16[64,2176]{1,0:T(8,128)(2,1)S(1)}, u32[]{:S(2)}, u32[]{:S(2)}) collective-permute-start(bf16[64,2176]{1,0:T(8,128)(2,1)} %get-tuple-element.30), channel_id=1, source_target_pairs={{0,128},{64,192},{128,0},{192,64},{1,129},{65,193},{129,1},{193,65... | collective-permute-start | bytes 835592 | tf_op jit(solution)/shard_map/ppermute | solution.py:410
  94.4 15.9 %collective-permute-start.18 = (bf16[64,2176]{1,0:T(8,128)(2,1)}, bf16[64,2176]{1,0:T(8,128)(2,1)S(1)}, u32[]{:S(2)}, u32[]{:S(2)}) collective-permute-start(bf16[64,2176]{1,0:T(8,128)(2,1)} %get-tuple-element.31), channel_id=1, source_target_pairs={{0,64},{64,128},{128,192},{192,0},{1,65},{65,129},{129,193},{193,1... | collective-permute-start | bytes 835592 | tf_op jit(solution)/shard_map/ppermute | solution.py:410
  95.1 21.4 %collective-permute-start.20 = (bf16[256,1024]{1,0:T(8,128)(2,1)S(1)}, bf16[256,1024]{1,0:T(8,128)(2,1)S(1)}, u32[]{:S(2)}, u32[]{:S(2)}) collective-permute-start(bf16[256,1024]{1,0:T(8,128)(2,1)S(1)} %copy-done.26), channel_id=1, source_target_pairs={{0,4},{1,5},{2,6},{3,7},{4,0},{5,1},{6,2},{7,3},{8,12},{9,13},{10,... | collective-permute-start | bytes 1572872 | tf_op jit(solution)/shard_map/ppermute | solution.py:405
  100.6 9.7 %copy-start.9 = (bf16[256,1024]{1,0:T(8,128)(2,1)}, bf16[256,1024]{1,0:T(8,128)(2,1)S(1)}, u32[]{:S(2)}) copy-start(bf16[256,1024]{1,0:T(8,128)(2,1)S(1)} %collective-permute-done.19.rest_0_.r1) | copy-start | bytes 1572868
  100.6 21.1 %collective-permute-start.21 = (bf16[256,1024]{1,0:T(8,128)(2,1)S(1)}, bf16[256,1024]{1,0:T(8,128)(2,1)S(1)}, u32[]{:S(2)}, u32[]{:S(2)}) collective-permute-start(bf16[256,1024]{1,0:T(8,128)(2,1)S(1)} %copy-done.25), channel_id=1, source_target_pairs={{0,2},{1,3},{2,4},{3,5},{4,6},{5,7},{6,0},{7,1},{8,10},{9,11},{10,... | collective-permute-start | bytes 1572872 | tf_op jit(solution)/shard_map/ppermute | solution.py:405
  101.7 8.5 %copy-start.19 = (bf16[64,2176]{1,0:T(8,128)(2,1)}, bf16[64,2176]{1,0:T(8,128)(2,1)S(1)}, u32[]{:S(2)}) copy-start(bf16[64,2176]{1,0:T(8,128)(2,1)S(1)} %collective-permute-done.16.r1) | copy-start | bytes 835588
  103.3 7.0 %copy-start.20 = (bf16[64,2176]{1,0:T(8,128)(2,1)}, bf16[64,2176]{1,0:T(8,128)(2,1)S(1)}, u32[]{:S(2)}) copy-start(bf16[64,2176]{1,0:T(8,128)(2,1)S(1)} %collective-permute-done.17.r2) | copy-start | bytes 835588
  110.3 0.7 copy-start.21
  113.1 16.0 %all-to-all-start.1 = ((bf16[8,8,2176]{2,1,0:T(8,128)(2,1)}), bf16[8,8,2176]{2,1,0:T(8,128)(2,1)S(1)}, u32[]{:S(2)}, u32[]{:S(2)}) async-start(bf16[8,8,2176]{2,1,0:T(8,128)(2,1)} %bitcast.10), calls=%async_computation.1 | async-start | bytes 557056 | tf_op jit(solution)/shard_map/all_to_all | solution.py:414
  116.5 5.2 %copy-start.17 = (bf16[256,1024]{1,0:T(8,128)(2,1)}, bf16[256,1024]{1,0:T(8,128)(2,1)S(1)}, u32[]{:S(2)}) copy-start(bf16[256,1024]{1,0:T(8,128)(2,1)S(1)} %collective-permute-done.20.r2) | copy-start | bytes 1572868
  121.7 0.8 copy-start.18
  129.1 0.7 copy-start.11
